TPU v7x, 128 devices: a whole 4x4x4 slice. The times are simulated.
128 devices in a mesh: src: 8 (over y, core), help: 16 (over z, x).
Axes of the slice: x: 4, y: 4, z: 4, core: 2. Of those that a mesh axis runs over, the one named last changes fastest.
Arguments:
- tiles: int32 [2, 1024], P(None, 'src'), may hold values from 0 to 127, as said below
- cell_slot: int32 [2, 128], replicated, may hold values from 0 to 127, as said below
- counts: int32 [128, 2], P(('src', 'help')), may hold values from 128 to 512, as said below
- src_points: bfloat16 [65536, 512], P(('src', 'help')), may hold values from -9 to 9
- tgt_points: bfloat16 [65536, 512], P(('src', 'help')), may hold values from -9 to 9
Outputs:
- source_potential: float32 [65536], P(('src', 'help'))
- target_potential: float32 [65536], P(('src', 'help'))
- transport: float32 [65536, 512], P(('src', 'help'))
Inputs may be any that keep to these rules, and one draw needn't show every extreme that they name: `tiles`: columns come in blocks of 128, block g for group g of 16 cells: a block's source cells have ids g * 16 to g * 16 + 15, its target cells lie in group g or in group g + 1 (group 8 - 1 is followed by group 0); no pair is listed twice, and every source cell and every target cell is named in some column. Each row is a permutation that keeps every cell in its group: cell c is stored at slot cell_slot[side, c], with cell_slot[side, c] // 16 equal to c // 16; slot k is rows k * 512 to k * 512 + 511 of the point arrays. `counts`: rows of a slot at and beyond its count are padding. Both ends of the range occur in each column.
All inputs are finite; a program needn't handle non-finite values.
Results may differ from a plain program's by a relative error of at most 0.004.
Values may be sent and summed in bfloat16 or wider, within the bound.
No kernel may reach another device: no remote copies, remote signals or barrier semaphores. Data moves between devices by JAX's collectives and lax.ppermute only.
A program may use at most 192 MiB of HBM per device.

v0:
```python
import math

import jax
import jax.numpy as jnp
from jax import lax
from jax.sharding import PartitionSpec as P

ITERS = 2


EPSILON = 0.2
NEGATIVE = -1e30


def passed_along(array, axis, by):
    count = lax.axis_size(axis)
    return lax.ppermute(array, axis, [(i, (i + by) % count) for i in range(count)])


def join_parts(first, second):
    highest = jnp.maximum(first[0], second[0])
    return (
        highest,
        first[1] * jnp.exp(first[0] - highest) + second[1] * jnp.exp(second[0] - highest),
    )


def lookup(cell_ids, slot_table):
    matches = cell_ids[:, None] == jnp.arange(slot_table.shape[0], dtype=jnp.int32)[None, :]
    return jnp.sum(jnp.where(matches, slot_table[None, :], 0), axis=1)


def half_norms(points, group_size, cell_rows):
    return 0.5 * jnp.sum(jnp.square(points.astype(jnp.float32)), axis=1).reshape(
        group_size, cell_rows
    )


def shards(tiles, cell_slot, counts, src_points, tgt_points):
    group_size = lax.axis_size("help")
    help_index = lax.axis_index("help")
    src_index = lax.axis_index("src")
    cell_rows = src_points.shape[0]
    width = src_points.shape[1]
    cost_scale = math.sqrt(width)
    source_all, source_counts = (src_points, counts)
    source_cells_held = 1
    own_points, own_counts = (
        lax.all_gather(tgt_points, "help", axis=0, tiled=True),
        lax.all_gather(counts, "help", axis=0, tiled=True),
    )
    next_points, next_counts = passed_along((own_points, own_counts), "src", -1)
    candidates = 2 * group_size
    positions = jnp.arange(cell_rows, dtype=jnp.int32)
    source_live = positions[None, :] < source_counts[:, 0:1]
    target_live = jnp.stack(
        [positions[None, :] < own_counts[:, 1:2], positions[None, :] < next_counts[:, 1:2]], axis=0
    )
    flat_live = target_live.reshape(candidates, cell_rows)
    source_half = half_norms(source_all, source_cells_held, cell_rows)
    target_half = jnp.stack(
        [
            half_norms(own_points, group_size, cell_rows),
            half_norms(next_points, group_size, cell_rows),
        ],
        axis=0,
    )
    flat_half = target_half.reshape(candidates, cell_rows)
    target_points = jnp.concatenate([own_points, next_points], axis=0)
    src_slot = lookup(tiles[0], cell_slot[0])
    tgt_slot = lookup(tiles[1], cell_slot[1])
    src_cells = src_slot % group_size
    tgt_cells = tgt_slot % group_size
    tgt_sides = jnp.where(tgt_slot // group_size == src_index, 0, 1)
    tgt_keys = tgt_sides * group_size + tgt_cells
    key_ids = jnp.arange(candidates, dtype=jnp.int32)
    is_mine = src_cells == help_index
    listed_keys = jnp.any(is_mine[:, None] & (tgt_keys[:, None] == key_ids[None, :]), axis=0)
    inner = lax.dot_general(
        src_points, target_points, (((1,), (1,)), ((), ())), preferred_element_type=jnp.float32
    )
    cost = (source_half[0][:, None] + flat_half.reshape(-1)[None, :] - inner) / cost_scale
    column_live = (flat_live & listed_keys[:, None]).reshape(-1)
    mask = source_live[0][:, None] & column_live[None, :]
    own_live = source_live[0]
    target_table = jnp.zeros((2, group_size, cell_rows), jnp.float32)
    source_table = jnp.zeros((source_cells_held, cell_rows), jnp.float32)
    source_own = jnp.zeros((cell_rows,), jnp.float32)
    target_own = jnp.zeros((cell_rows,), jnp.float32)
    for sweep in range(ITERS):
        row_flat_target = target_table.reshape(candidates, cell_rows)
        row_scores = jnp.where(
            mask, (row_flat_target.reshape(-1)[None, :] - cost) / EPSILON, NEGATIVE
        )
        part_max = jnp.max(row_scores, axis=1)
        part_sum = jnp.sum(jnp.exp(row_scores - part_max[:, None]), axis=1)
        row_source_own = jnp.where(own_live, -EPSILON * (part_max + jnp.log(part_sum)), 0.0)
        row_source_table = row_source_own[None, :]
        source_table = row_source_table
        source_own = row_source_own
        scores = jnp.where(mask, (source_table[0][:, None] - cost) / EPSILON, NEGATIVE)
        peaks = jnp.max(scores, axis=0)
        sums = jnp.sum(jnp.exp(scores - peaks[None, :]), axis=0)
        peaks = peaks.reshape(2, group_size, cell_rows)
        sums = sums.reshape(2, group_size, cell_rows)
        highest = lax.pmax(peaks.astype(jnp.bfloat16), "help").astype(peaks.dtype)
        rescaled = sums * jnp.exp(peaks - highest)
        summed = lax.psum_scatter(rescaled, "help", scatter_dimension=1, tiled=True)
        own_peak = lax.dynamic_slice_in_dim(highest, help_index, 1, 1)[:, 0]
        carried_max, carried_sum = passed_along((own_peak[1], summed[1, 0]), "src", 1)
        joined = join_parts((own_peak[0], summed[0, 0]), (carried_max, carried_sum))
        col_target_own = jnp.where(
            target_live[0, help_index], -EPSILON * (joined[0] + jnp.log(joined[1])), 0.0
        )
        target_after = passed_along(col_target_own, "src", -1)
        group_own = lax.all_gather(col_target_own[None, :], "help", axis=0, tiled=True)
        group_after = lax.all_gather(target_after[None, :], "help", axis=0, tiled=True)
        col_target_table = jnp.stack([group_own, group_after], axis=0)
        target_table = col_target_table
        target_own = col_target_own
    flat_target = target_table.reshape(candidates, cell_rows)
    exponent = (source_table[0][:, None] + flat_target.reshape(-1)[None, :] - cost) / EPSILON
    weight = jnp.where(mask, jnp.exp(exponent), 0.0).astype(jnp.bfloat16)
    own_numerator = jnp.dot(weight, target_points, preferred_element_type=jnp.float32)
    own_denominator = jnp.sum(weight.astype(jnp.float32), axis=1)
    safe_total = jnp.where(own_live, own_denominator, 1.0)
    transport = jnp.where(own_live[:, None], own_numerator / safe_total[:, None], 0.0)
    return (source_own, target_own, transport)


def solution(mesh):
    in_specs = (
        P(None, "src"),
        P(),
        P(("src", "help"), None),
        P(("src", "help"), None),
        P(("src", "help"), None),
    )
    out_specs = (P(("src", "help")), P(("src", "help")), P(("src", "help"), None))
    return jax.shard_map(shards, mesh=mesh, in_specs=in_specs, out_specs=out_specs, check_vma=False)
```

profile of v0, /device:TPU:17, one launch (start us, length us, event | category | flops | bytes accessed | tf_op | source)
XLA Modules:
  0.0 743.8 jit_solution(12003397124178640335)
XLA Ops:
  8.0 75.3 %all-gather.11.cloned.1.call-done = bf16[8192,512]{1,0:T(8,128)(2,1)} async-done(((bf16[512,512]{1,0:T(8,128)(2,1)}), bf16[8192,512]{1,0:T(8,128)(2,1)}) %all-gather.11.cloned.1.call-update) | async-done | bytes 8388624 | tf_op jit(solution)/shard_map/all_gather | solution.py:49
  83.9 15.9 %all-gather.4 = s32[16,1,2]{2,1,0:T(1,128)S(1)} all-gather(s32[1,1,2]{2,1,0:T(1,128)} %bitcast.72), channel_id=1, replica_groups=mesh['src'=8,'help'=16] {'help'}, dimensions={0}, use_global_device_ids=true | all-gather | bytes 136 | tf_op jit(solution)/shard_map/all_gather | solution.py:50
  109.1 67.3 %collective-permute-done = s32[16,2]{0,1:T(2,128)S(1)} collective-permute-done((s32[16,2]{0,1:T(2,128)S(1)}, s32[16,2]{0,1:T(2,128)S(1)}, u32[]{:S(2)}, u32[]{:S(2)}) %collective-permute-start) | collective-permute-done | bytes 160 | tf_op jit(solution)/shard_map/ppermute | solution.py:17
  181.7 7.1 constant_dynamic-update-slice_fusion.1
  201.1 18.8 %fusion.2 = (f32[512]{0:T(512)S(1)}, f32[512,16384]{0,1:T(8,128)S(1)}) fusion(pred[512]{0:T(512)(128)(4,1)S(1)} %iota_compare_fusion.5, pred[16384]{0:T(1024)(128)(4,1)S(1)} %and.81, bf16[16384,512]{1,0:T(8,128)(2,1)} %constant_dynamic-update-slice_fusion, bf16[512,512]{1,0:T(8,128)(2,1)S(1)} %copy-done.1, f32[16384]{0:T(1024)S(1)} %bitcast.64, ...), kind=kOutput, calls=%fused_computation.13 | convolution fusion | flops 8657043456 | bytes 50942464 | tf_op jit(solution)/shard_map/dot_general | solution.py:79
  219.9 13.6 %exponential_reduce_fusion.3 = f32[512]{0:T(512)S(1)} fusion(f32[512,16384]{0,1:T(8,128)S(1)} %get-tuple-element.18, f32[512]{0:T(512)S(1)} %get-tuple-element.17, pred[512]{0:T(512)(128)(4,1)S(1)} %iota_compare_fusion.5, pred[16384]{0:T(1024)(128)(4,1)S(1)} %and.81), kind=kLoop, calls=%fused_computation.12 | loop fusion | flops 50331136 | bytes 33575424 | tf_op jit(solution)/shard_map/reduce_sum | solution.py:96
  233.6 9.6 %fusion.3 = f32[16384]{0:T(1024)S(1)} fusion(f32[512,16384]{0,1:T(8,128)S(1)} %get-tuple-element.18, f32[512]{0:T(512)S(1)} %multiply_select_fusion.3, pred[512]{0:T(512)(128)(4,1)S(1)} %iota_compare_fusion.5, pred[16384]{0:T(1024)(128)(4,1)S(1)} %and.81), kind=kLoop, calls=%fused_computation.14 | loop fusion | flops 41926656 | bytes 33638912 | tf_op jit(solution)/shard_map/reduce_max | solution.py:102
  243.2 14.9 %exponential_reduce_fusion.2 = f32[16384]{0:T(1024)S(1)} fusion(f32[512,16384]{0,1:T(8,128)} %copy-done, f32[16384]{0:T(1024)S(1)} %fusion.3, f32[512]{0:T(512)S(1)} %multiply_select_fusion.3, pred[512]{0:T(512)(128)(4,1)S(1)} %iota_compare_fusion.5, pred[16384]{0:T(1024)(128)(4,1)S(1)} %and.81), kind=kLoop, calls=%fused_computation.11 | loop fusion | flops 50315264 | bytes 33704448 | tf_op jit(solution)/shard_map/reduce_sum | solution.py:103
  258.2 58.4 %pmax.14 = bf16[2,16,512]{2,1,0:T(8,128)(2,1)S(1)} all-reduce(bf16[2,16,512]{2,1,0:T(8,128)(2,1)S(1)} %convert_element_type.30), channel_id=1, replica_groups=mesh['src'=8,'help'=16] {'help'}, use_global_device_ids=true, to_apply=%region_9.10 | all-reduce | flops 16384 | bytes 65536 | tf_op jit(solution)/shard_map/pmax | solution.py:106
  317.4 13.9 %collective-permute-start.2 = (f32[512]{0:T(512)S(1)}, f32[512]{0:T(512)S(1)}, u32[]{:S(2)}, u32[]{:S(2)}) collective-permute-start(f32[512]{0:T(512)S(1)} %bitcast.80), channel_id=1, source_target_pairs={{0,16},{16,32},{32,48},{48,64},{64,80},{80,96},{96,112},{112,0},{1... | collective-permute-start | bytes 6152 | tf_op jit(solution)/shard_map/ppermute | solution.py:17
  331.3 73.9 %all-reduce.5.cloned.1.call-done = f32[2,16,512]{2,0,1:T(2,128)} async-done(((f32[2,16,512]{2,0,1:T(2,128)}), f32[2,16,512]{2,0,1:T(2,128)}) %all-reduce.5.cloned.1.call-update) | async-done | bytes 65552
  411.9 17.1 %all-gather.5 = f32[16,1,512]{2,1,0:T(1,128)S(1)} all-gather(f32[1,1,512]{2,1,0:T(1,128)S(1)} %bitcast.67), channel_id=2, replica_groups=mesh['src'=8,'help'=16] {'help'}, dimensions={0}, use_global_device_ids=true | all-gather | bytes 34816 | tf_op jit(solution)/shard_map/all_gather | solution.py:116
  429.0 16.0 %all-gather.6 = f32[16,1,512]{2,1,0:T(1,128)S(1)} all-gather(f32[1,1,512]{2,1,0:T(1,128)S(1)} %bitcast.77), channel_id=3, replica_groups=mesh['src'=8,'help'=16] {'help'}, dimensions={0}, use_global_device_ids=true | all-gather | bytes 34816 | tf_op jit(solution)/shard_map/all_gather | solution.py:117
  445.1 13.1 %fusion.4 = f32[512]{0:T(512)S(1)} fusion(f32[512,16384]{0,1:T(8,128)} %copy-done, f32[16384]{0:T(1024)S(1)} %bitcast.52, pred[512]{0:T(512)(128)(4,1)S(1)} %iota_compare_fusion.5, pred[16384]{0:T(1024)(128)(4,1)S(1)} %and.81), kind=kLoop, calls=%fused_computation.15 | loop fusion | flops 41942528 | bytes 33638912 | tf_op jit(solution)/shard_map/reduce_max | solution.py:95
  458.2 14.2 %exponential_reduce_fusion.1 = f32[512]{0:T(512)S(1)} fusion(f32[512,16384]{0,1:T(8,128)} %copy-done, f32[512]{0:T(512)S(1)} %fusion.4, f32[16384]{0:T(1024)S(1)} %bitcast.53, pred[512]{0:T(512)(128)(4,1)S(1)} %iota_compare_fusion.5, pred[16384]{0:T(1024)(128)(4,1)S(1)} %and.81), kind=kLoop, calls=%fused_computation.10 | loop fusion | flops 50331136 | bytes 33640960 | tf_op jit(solution)/shard_map/reduce_sum | solution.py:96
  472.4 15.2 %fusion.5 = f32[16384]{0:T(1024)S(1)} fusion(f32[512,16384]{0,1:T(8,128)} %copy-done, f32[512]{0:T(512)S(1)} %multiply_select_fusion.1, pred[512]{0:T(512)(128)(4,1)S(1)} %iota_compare_fusion.5, pred[16384]{0:T(1024)(128)(4,1)S(1)} %and.81), kind=kLoop, calls=%fused_computation.16 | loop fusion | flops 41926656 | bytes 33638912 | tf_op jit(solution)/shard_map/reduce_max | solution.py:102
  487.6 14.9 %exponential_reduce_fusion = f32[16384]{0:T(1024)S(1)} fusion(f32[512,16384]{0,1:T(8,128)} %copy-done, f32[16384]{0:T(1024)S(1)} %fusion.5, f32[512]{0:T(512)S(1)} %multiply_select_fusion.1, pred[512]{0:T(512)(128)(4,1)S(1)} %iota_compare_fusion.5, pred[16384]{0:T(1024)(128)(4,1)S(1)} %and.81), kind=kLoop, calls=%fused_computation.9 | loop fusion | flops 50315264 | bytes 33704448 | tf_op jit(solution)/shard_map/reduce_sum | solution.py:103
  502.6 57.9 %pmax.15 = bf16[2,16,512]{2,1,0:T(8,128)(2,1)S(1)} all-reduce(bf16[2,16,512]{2,1,0:T(8,128)(2,1)S(1)} %convert_element_type.32), channel_id=1, replica_groups=mesh['src'=8,'help'=16] {'help'}, use_global_device_ids=true, to_apply=%region_15.16 | all-reduce | flops 16384 | bytes 65536 | tf_op jit(solution)/shard_map/pmax | solution.py:106
  561.3 25.8 %collective-permute-start.5 = (f32[512]{0:T(512)S(1)}, f32[512]{0:T(512)S(1)}, u32[]{:S(2)}, u32[]{:S(2)}) collective-permute-start(f32[512]{0:T(512)S(1)} %bitcast.79), channel_id=1, source_target_pairs={{0,16},{16,32},{32,48},{48,64},{64,80},{80,96},{96,112},{112,0},{1... | collective-permute-start | bytes 6152 | tf_op jit(solution)/shard_map/ppermute | solution.py:17
  587.1 74.2 %all-reduce.7.cloned.1.call-done = f32[2,16,512]{2,0,1:T(2,128)} async-done(((f32[2,16,512]{2,0,1:T(2,128)}), f32[2,16,512]{2,0,1:T(2,128)}) %all-reduce.7.cloned.1.call-update) | async-done | bytes 65552
  668.1 17.1 %all-gather.7 = f32[16,1,512]{2,1,0:T(1,128)S(1)} all-gather(f32[1,1,512]{2,1,0:T(1,128)S(1)} %bitcast.66), channel_id=4, replica_groups=mesh['src'=8,'help'=16] {'help'}, dimensions={0}, use_global_device_ids=true | all-gather | bytes 34816 | tf_op jit(solution)/shard_map/all_gather | solution.py:116
  685.2 15.8 %all-gather.8 = f32[16,1,512]{2,1,0:T(1,128)S(1)} all-gather(f32[1,1,512]{2,1,0:T(1,128)S(1)} %bitcast.78), channel_id=5, replica_groups=mesh['src'=8,'help'=16] {'help'}, dimensions={0}, use_global_device_ids=true | all-gather | bytes 34816 | tf_op jit(solution)/shard_map/all_gather | solution.py:117
  701.1 18.0 %convert_reduce_fusion = (f32[512]{0:T(512)S(1)}, bf16[512,16384]{0,1:T(8,128)(2,1)}) fusion(f32[512,16384]{0,1:T(8,128)} %copy-done, f32[16384]{0:T(1024)S(1)} %bitcast.54, f32[512]{0:T(512)S(1)} %multiply_select_fusion.1, pred[16384]{0:T(1024)(128)(4,1)S(1)} %and.81, pred[512]{0:T(512)(128)(4,1)S(1)} %iota_compare_fusion.5), kind=kLoop, calls=%fused_computation.8 | loop fusion | flops 67108352 | bytes 50418176 | tf_op jit(solution)/shard_map/reduce_sum | solution.py:125
  719.2 18.1 %fusion.6 = f32[512,512]{1,0:T(8,128)} fusion(bf16[512,16384]{0,1:T(8,128)(2,1)} %get-tuple-element.4, bf16[16384,512]{1,0:T(8,128)(2,1)} %constant_dynamic-update-slice_fusion, f32[512]{0:T(512)S(1)} %broadcast_select_fusion, pred[512]{0:T(512)(128)(4,1)S(1)} %iota_compare_fusion.5), kind=kOutput, calls=%fused_computation.20 | convolution fusion | flops 8590458880 | bytes 34605568 | tf_op jit(solution)/shard_map/dot_general | solution.py:124
  (86 shorter events, 43.4 us)
Async XLA Ops:
  7.2 194.0 %copy-start.1 = (bf16[512,512]{1,0:T(8,128)(2,1)S(1)}, bf16[512,512]{1,0:T(8,128)(2,1)}, u32[]{:S(2)}) copy-start(bf16[512,512]{1,0:T(8,128)(2,1)} %param.8) | copy-start | bytes 1572868
  7.2 76.1 %all-gather.11.cloned.1.call-start = ((), (), s32[]{:S(2)}) async-start(), calls=%async_computation | async-start | bytes 8912896 | tf_op jit(solution)/shard_map/all_gather | solution.py:49
  7.9 397.3 %all-reduce.5.cloned.1.call-start = ((), (), s32[]{:S(2)}) async-start(), calls=%async_computation.1 | async-start | bytes 131072
  83.2 105.6 %collective-permute-start.1 = (bf16[8192,512]{1,0:T(8,128)(2,1)}, bf16[8192,512]{1,0:T(8,128)(2,1)}, u32[]{:S(2)}, u32[]{:S(2)}) collective-permute-start(bf16[8192,512]{1,0:T(8,128)(2,1)} %all-gather.11.cloned.1.call-done), channel_id=1, source_target_pairs={{0,112},{16,0},{32,16},{48,32},{64,48},{80,64},{96,80},{112,96},{1... | collective-permute-start | bytes 25165832 | tf_op jit(solution)/shard_map/ppermute | solution.py:17
  99.9 76.5 %collective-permute-start = (s32[16,2]{0,1:T(2,128)S(1)}, s32[16,2]{0,1:T(2,128)S(1)}, u32[]{:S(2)}, u32[]{:S(2)}) collective-permute-start(s32[16,2]{0,1:T(2,128)S(1)} %bitcast.83), channel_id=1, source_target_pairs={{0,112},{16,0},{32,16},{48,32},{64,48},{80,64},{96,80},{112,96},{1... | collective-permute-start | bytes 392 | tf_op jit(solution)/shard_map/ppermute | solution.py:17
  219.9 13.7 %copy-start = (f32[512,16384]{0,1:T(8,128)}, f32[512,16384]{0,1:T(8,128)S(1)}, u32[]{:S(2)}) copy-start(f32[512,16384]{0,1:T(8,128)S(1)} %get-tuple-element.18) | copy-start | bytes 100663296
  219.9 13.6 %copy-start.4 = (s32[1,2]{1,0:T(1,128)S(1)}, s32[1,2]{1,0:T(1,128)}, u32[]{:S(2)}) copy-start(s32[1,2]{1,0:T(1,128)} %param.7) | copy-start | bytes 28
  317.3 344.0 %all-reduce.7.cloned.1.call-start = ((), (), s32[]{:S(2)}) async-start(), calls=%async_computation.2 | async-start | bytes 131072
  317.4 92.3 %collective-permute-start.2 = (f32[512]{0:T(512)S(1)}, f32[512]{0:T(512)S(1)}, u32[]{:S(2)}, u32[]{:S(2)}) collective-permute-start(f32[512]{0:T(512)S(1)} %bitcast.80), channel_id=1, source_target_pairs={{0,16},{16,32},{32,48},{48,64},{64,80},{80,96},{96,112},{112,0},{1... | collective-permute-start | bytes 6152 | tf_op jit(solution)/shard_map/ppermute | solution.py:17
  406.6 3.8 collective-permute-start.3
  410.4 18.6 %collective-permute-start.4 = (f32[512]{0:T(512)S(1)}, f32[512]{0:T(512)S(1)}, u32[]{:S(2)}, u32[]{:S(2)}) collective-permute-start(f32[512]{0:T(512)S(1)} %multiply_select_fusion.2), channel_id=1, source_target_pairs={{0,112},{16,0},{32,16},{48,32},{64,48},{80,64},{96,80},{112,96},{1... | collective-permute-start | bytes 6152 | tf_op jit(solution)/shard_map/ppermute | solution.py:17
  472.4 228.7 %copy-start.2 = (f32[512]{0:T(512)}, f32[512]{0:T(512)S(1)}, u32[]{:S(2)}) copy-start(f32[512]{0:T(512)S(1)} %multiply_select_fusion.1) | copy-start | bytes 6148
  561.3 104.5 %collective-permute-start.5 = (f32[512]{0:T(512)S(1)}, f32[512]{0:T(512)S(1)}, u32[]{:S(2)}, u32[]{:S(2)}) collective-permute-start(f32[512]{0:T(512)S(1)} %bitcast.79), channel_id=1, source_target_pairs={{0,16},{16,32},{32,48},{48,64},{64,80},{80,96},{96,112},{112,0},{1... | collective-permute-start | bytes 6152 | tf_op jit(solution)/shard_map/ppermute | solution.py:17
  662.8 3.8 collective-permute-start.6
  666.6 70.7 %copy-start.3 = (f32[512]{0:T(512)}, f32[512]{0:T(512)S(1)}, u32[]{:S(2)}) copy-start(f32[512]{0:T(512)S(1)} %multiply_select_fusion) | copy-start | bytes 6148
  666.6 18.6 %collective-permute-start.7 = (f32[512]{0:T(512)S(1)}, f32[512]{0:T(512)S(1)}, u32[]{:S(2)}, u32[]{:S(2)}) collective-permute-start(f32[512]{0:T(512)S(1)} %multiply_select_fusion), channel_id=1, source_target_pairs={{0,112},{16,0},{32,16},{48,32},{64,48},{80,64},{96,80},{112,96},{1... | collective-permute-start | bytes 6152 | tf_op jit(solution)/shard_map/ppermute | solution.py:17
Sparse Core Ops, SparseCore 0:
  10.2 73.0 all-gather.10
  317.5 87.7 all-reduce.4
  561.4 99.9 all-reduce.6
where the time goes:
time: 756 us; the launch traced here: 744 us
  waiting for transfers between devices  293 us (39%)
  blocking collectives  198 us (26%)
  other arithmetic  127 us (17%)
  starting transfers between devices  53.6 us (7%)
  matrix products  36.9 us (5%)
  local copies, waits for them, and re-layouts  21.6 us (3%)
  between operations  14.1 us (2%)
    unnamed x5, waiting for transfers between devices  149 us
    pmax x2, blocking collectives, shards(): highest = lax.pmax(peaks.astype(jnp.bfloat16), 'help').astype(peaks.dtype)  116 us
    all_gather x1, waiting for transfers between devices, shards(): lax.all_gather(tgt_points, 'help', axis=0, tiled=True)  75.3 us
    ppermute x8, waiting for transfers between devices, passed_along(): lax.ppermute(array, axis, [(i, (i + by) % count) for i in range(count)])  68.8 us
    ppermute x8, starting transfers between devices, passed_along(): lax.ppermute(array, axis, [(i, (i + by) % count) for i in range(count)])  53.4 us
    all_gather x2, blocking collectives, shards(): lax.all_gather(col_target_own[None, :], 'help', axis=0, tiled=True)  34.2 us
    all_gather x2, blocking collectives, shards(): lax.all_gather(target_after[None, :], 'help', axis=0, tiled=True)  31.8 us
    reduce_sum x2, other arithmetic, shards(): sums = jnp.sum(jnp.exp(scores - peaks[None, :]), axis=0)  29.9 us
  transfers between devices with their start and end apart: 11, of which 6 were waited for; matrix products, arithmetic and copies ran while one was open for 3% of the time, Pallas kernels for 0%

commit v1 on v0

v1 whole, which is shorter than its diff:
```python
import functools
import math

import jax
import jax.numpy as jnp
from jax import lax
from jax.experimental import pallas as pl
from jax.experimental.pallas import tpu as pltpu
from jax.sharding import PartitionSpec as P

ITERS = 2
EPSILON = 0.2
LOG2E = 1.0 / math.log(2.0)
DEAD = -1e30
EMPTY = -2e30
MARK = 1024.0
SIDE = 4
PART = 128
WIDTH = 512
SRC_CELLS = 16
TGT_CELLS = 32
TAIL = 16
PAIRS = 128
F32 = jnp.float32
BF16 = jnp.bfloat16
VMEM_LIMIT = 48 * 1024 * 1024


def x_perm(by):
    return [(z * SIDE + x, z * SIDE + (x + by) % SIDE) for z in range(SIDE) for x in range(SIDE)]


def z_perm(by):
    return [(z * SIDE + x, (z + by) % SIDE * SIDE + x) for z in range(SIDE) for x in range(SIDE)]


def to_group(array, by):
    count = lax.axis_size("src")
    return lax.ppermute(array, "src", [(i, (i + by) % count) for i in range(count)])


def to_help(array, perm):
    return lax.ppermute(array, "help", perm)


def lookup(cell_ids, slot_table):
    matches = cell_ids[:, None] == jnp.arange(slot_table.shape[0], dtype=jnp.int32)[None, :]
    return jnp.sum(jnp.where(matches, slot_table[None, :], 0), axis=1)


def spread(points, perm, me):
    parts = [lax.dynamic_slice_in_dim(points, me * PART, PART, 0)]
    for by in range(1, SIDE):
        other = (me + by) % SIDE
        parts.append(to_help(lax.dynamic_slice_in_dim(points, other * PART, PART, 0), perm(by)))
    return jnp.concatenate(parts, axis=0)


def collect(block, perm):
    rows = block.shape[0]
    half = rows // 2
    behind = to_help(block, perm(1))
    ahead = to_help(block, perm(SIDE - 1))
    far_low = to_help(behind[:half], perm(1))
    far_high = to_help(ahead[half:], perm(SIDE - 1))
    return [
        (0, rows, block),
        (rows, rows, behind),
        (3 * rows, rows, ahead),
        (2 * rows, half, far_low),
        (2 * rows + half, half, far_high),
    ]


def ring_parts(array, perm):
    return [array] + [to_help(array, perm(by)) for by in range(1, SIDE)]


def join(parts):
    top = functools.reduce(jnp.maximum, parts)
    total = functools.reduce(jnp.add, [jnp.exp2(part - top) for part in parts])
    return top + jnp.log2(total)


def eye():
    return lax.broadcasted_iota(jnp.int32, (PART, PART), 0) == lax.broadcasted_iota(
        jnp.int32, (PART, PART), 1
    )


def to_lanes(column):
    return jnp.sum(jnp.where(eye(), jnp.broadcast_to(column, (PART, PART)), 0.0), axis=0, keepdims=True)


def to_rows(lane_vector):
    return jnp.transpose(jnp.broadcast_to(lane_vector, (PART, PART)))


def part_of(index):
    return pl.ds(pl.multiple_of(index * PART, PART), PART)


def load_blocks(refs, places, order, target, sem):
    copies = []
    for (start, rows), ref in zip(places, refs):
        for cell in range(rows // PART):
            place = start // PART + cell
            side, place = place // SRC_CELLS, place % SRC_CELLS
            goal = part_of(side * SRC_CELLS + order[place])
            copies.append(
                pltpu.make_async_copy(
                    ref.at[pl.ds(cell * PART, PART)], target.at[goal], sem.at[len(copies)]
                )
            )
    for copy in copies:
        copy.start()
    return copies


def row_sums(starts, targets, table_ref, level_ref, sums_ref, fill):
    def cell(s, carry):
        first, last = starts[s], starts[s + 1]

        def highest(n, top):
            scores = (fill(s, n) if fill is not None else table_ref[n]) + level_ref[pl.ds(targets[n], 1), :]
            return jnp.maximum(top, scores)

        top = lax.fori_loop(first, last, highest, jnp.full((PART, PART), EMPTY, F32))
        top = jnp.max(top, axis=1, keepdims=True)

        def add(n, total):
            return total + jnp.exp2(table_ref[n] + level_ref[pl.ds(targets[n], 1), :] - top)

        total = lax.fori_loop(first, last, add, jnp.zeros((PART, PART), F32))
        total = jnp.sum(total, axis=1, keepdims=True)
        sums_ref[pl.ds(s, 1), :] = to_lanes(top + jnp.log2(total))
        return carry

    lax.fori_loop(0, SRC_CELLS, cell, 0)


def first_kernel(places_s, places_t, scale, starts, targets, s_order, t_order, *refs):
    ns, nt = len(places_s), len(places_t)
    s_refs, t_refs = refs[:ns], refs[ns : ns + nt]
    table_ref, sums_ref, level_ref, live_ref = refs[ns + nt : ns + nt + 4]
    xs, ys, s_sem, t_sem = refs[ns + nt + 4 :]
    copies = load_blocks(s_refs, places_s, s_order, xs, s_sem)
    copies += load_blocks(t_refs, places_t, t_order, ys, t_sem)
    for copy in copies:
        copy.wait()

    def target_cell(t, carry):
        points = ys[part_of(t), :].astype(F32)
        half = to_lanes(jnp.sum(points * points, axis=1, keepdims=True)) * (0.5 * scale)
        level_ref[pl.ds(t, 1), :] = jnp.where(half > 1e7, DEAD, -half)
        return carry

    lax.fori_loop(0, TGT_CELLS, target_cell, 0)

    def source_cell(s, carry):
        mark = xs[part_of(s), :PART].astype(F32)
        dead = jnp.where(eye() & (mark > 0.5 * MARK), DEAD, 0.0)
        live_ref[pl.ds(s, 1), :] = jnp.sum(dead, axis=0, keepdims=True)
        return carry

    lax.fori_loop(0, SRC_CELLS, source_cell, 0)

    def fill(s, n):
        inner = lax.dot_general(
            xs[part_of(s), :],
            ys[part_of(targets[n]), :],
            (((1,), (1,)), ((), ())),
            preferred_element_type=F32,
        )
        inner = inner * scale
        table_ref[n] = inner
        return inner

    row_sums(starts, targets, table_ref, level_ref, sums_ref, fill)


def source_levels(parts, live):
    return jnp.where(live < 0.5 * DEAD, DEAD, -join([part[...] for part in parts]))


def column_kernel(starts, targets, r0, r1, r2, r3, live_ref, table_ref, sums_ref, level_ref, tops, totals):
    level_ref[...] = source_levels((r0, r1, r2, r3), live_ref[...])
    tops[...] = jnp.full(tops.shape, EMPTY, F32)
    totals[...] = jnp.ones(totals.shape, F32)

    def cell(s, carry):
        level = to_rows(level_ref[pl.ds(s, 1), :])

        def tile(n, inner_carry):
            t = targets[n]
            scores = (table_ref[n] + level).reshape(PART // 8, 8, PART)
            old = tops[t]
            top = jnp.maximum(old, jnp.max(scores, axis=0))
            tops[t] = top
            totals[t] = totals[t] * jnp.exp2(old - top) + jnp.sum(jnp.exp2(scores - top[None]), axis=0)
            return inner_carry

        return lax.fori_loop(starts[s], starts[s + 1], tile, carry)

    lax.fori_loop(0, SRC_CELLS, cell, 0)
    tops_all = tops[...]
    top = jnp.max(tops_all, axis=1)
    total = jnp.sum(totals[...] * jnp.exp2(tops_all - top[:, None, :]), axis=1)
    sums_ref[...] = top + jnp.log2(total)


def target_levels(joined, before, after, first_level):
    own = -join([joined[:SRC_CELLS], before])
    following = -join([joined[SRC_CELLS:], after])
    levels = jnp.concatenate([own, following], axis=0)
    return jnp.where(first_level < 0.5 * DEAD, DEAD, levels)


def row_kernel(starts, targets, joined, before, after, first_level, table_ref, sums_ref, level_ref):
    level_ref[...] = target_levels(joined[...], before[...], after[...], first_level[...])
    row_sums(starts, targets, table_ref, level_ref, sums_ref, None)


def pieces(value, count):
    found = []
    for _ in range(count):
        piece = value.astype(BF16).astype(F32)
        found.append(piece)
        value = value - piece
    return found


def transport_kernel(places_t, starts, targets, t_order, joined, before, after, first_level, src_level, table_ref, *refs):
    nt = len(places_t)
    t_refs = refs[:nt]
    out_ref, ys, level_ref, total_ref, t_sem = refs[nt:]
    copies = load_blocks(t_refs, places_t, t_order, ys, t_sem)
    level_ref[...] = target_levels(joined[...], before[...], after[...], first_level[...])
    for copy in copies:
        copy.wait()

    def cell(s, carry):
        row_level = src_level[pl.ds(s, 1), :]
        level = to_rows(row_level)
        total_ref[...] = jnp.zeros(total_ref.shape, F32)

        def tile(n, weight_sum):
            t = targets[n]
            weight = jnp.exp2(table_ref[n] + level_ref[pl.ds(t, 1), :] + level).astype(BF16)
            total_ref[...] += jnp.dot(weight, ys[part_of(t), :], preferred_element_type=F32)
            return weight_sum + weight.astype(F32)

        weight_sum = lax.fori_loop(starts[s], starts[s + 1], tile, jnp.zeros((PART, PART), F32))
        weight_sum = to_lanes(jnp.sum(weight_sum, axis=1, keepdims=True))
        out_ref[s, :PART, :] = total_ref[...].astype(BF16)
        col_level = level_ref[pl.ds(s, 1), :]
        parts = pieces(weight_sum, 2) + pieces(row_level, 3) + pieces(col_level, 3)
        rows = lax.broadcasted_iota(jnp.int32, (TAIL, WIDTH), 0)
        tail = jnp.where(
            rows == 0,
            jnp.concatenate(parts[:4], axis=1),
            jnp.where(rows == 1, jnp.concatenate(parts[4:], axis=1), 0.0),
        )
        out_ref[s, PART:, :] = tail.astype(BF16)
        return carry

    lax.fori_loop(0, SRC_CELLS, cell, 0)


def finish_kernel(counts, got, half_src, half_tgt, src_ref, tgt_ref, map_ref):
    def tail(sender):
        return got[sender, PART:, :].astype(F32)

    def segment(rows, index):
        return rows[index // SIDE : index // SIDE + 1, index % SIDE * PART : (index % SIDE + 1) * PART]

    lanes = lax.broadcasted_iota(jnp.int32, (1, PART), 1)
    rows = lax.broadcasted_iota(jnp.int32, (PART, 1), 0)
    src_live, tgt_live = counts[0, 0], counts[0, 1]
    for q in range(SIDE):
        tails = [tail(q * SIDE + x) for x in range(SIDE)]
        weight_sum = sum(segment(one, 0) + segment(one, 1) for one in tails)
        live = rows + q * PART < src_live
        inverse = jnp.where(live, 1.0 / to_rows(weight_sum), 0.0)
        for chunk in range(WIDTH // PART):
            columns = slice(chunk * PART, (chunk + 1) * PART)
            numerator = sum(got[q * SIDE + x, :PART, columns].astype(F32) for x in range(SIDE))
            map_ref[q * PART : (q + 1) * PART, columns] = jnp.where(live, numerator * inverse, 0.0)
        level = segment(tails[0], 2) + segment(tails[0], 3) + segment(tails[0], 4)
        value = (level + half_src[q : q + 1, :]) * (EPSILON / LOG2E)
        src_ref[q : q + 1, :] = jnp.where(lanes + q * PART < src_live, value, 0.0)
        first = tail(q)
        level = segment(first, 5) + segment(first, 6) + segment(first, 7)
        value = (level + half_tgt[q : q + 1, :]) * (EPSILON / LOG2E)
        tgt_ref[q : q + 1, :] = jnp.where(lanes + q * PART < tgt_live, value, 0.0)


VM = pl.BlockSpec(memory_space=pltpu.VMEM)
SM = pl.BlockSpec(memory_space=pltpu.SMEM)
ANY = pl.BlockSpec(memory_space=pl.ANY)


def call(kernel, out_shape, in_specs, scratch, *args):
    outs = jax.tree.map(lambda _: VM, out_shape)
    return pl.pallas_call(
        kernel,
        out_shape=out_shape,
        in_specs=in_specs,
        out_specs=outs,
        scratch_shapes=scratch,
        compiler_params=pltpu.CompilerParams(vmem_limit_bytes=VMEM_LIMIT),
    )(*args)


def shape(*dims, dtype=F32):
    return jax.ShapeDtypeStruct(dims, dtype)


def shards(tiles, cell_slot, counts, src_points, tgt_points):
    help_index = lax.axis_index("help")
    src_index = lax.axis_index("src")
    z, x = help_index // SIDE, help_index % SIDE
    scale = LOG2E / (math.sqrt(WIDTH) * EPSILON)

    positions = jnp.arange(SIDE * PART, dtype=jnp.int32)[:, None]
    marked_src = jnp.where(positions < counts[0, 0], src_points, jnp.asarray(MARK, BF16))
    marked_tgt = jnp.where(positions < counts[0, 1], tgt_points, jnp.asarray(-MARK, BF16))
    tgt_block = spread(marked_tgt, x_perm, x)
    src_block = spread(marked_src, z_perm, z)
    own = collect(tgt_block, z_perm)
    following = [
        (SIDE * SIDE * PART + start, rows, to_group(array, -1)) for start, rows, array in own
    ]
    sources = collect(src_block, x_perm)
    targets_all = own + following
    places_s = tuple((start, rows) for start, rows, _ in sources)
    places_t = tuple((start, rows) for start, rows, _ in targets_all)
    s_arrays = [array for _, _, array in sources]
    t_arrays = [array for _, _, array in targets_all]

    half_src = (0.5 * scale) * jnp.sum(jnp.square(src_points.astype(F32)), axis=1).reshape(SIDE, PART)
    half_tgt = (0.5 * scale) * jnp.sum(jnp.square(tgt_points.astype(F32)), axis=1).reshape(SIDE, PART)

    src_slot = lookup(tiles[0], cell_slot[0])
    tgt_slot = lookup(tiles[1], cell_slot[1])
    src_local = src_slot % SRC_CELLS
    tgt_local = tgt_slot % SRC_CELLS + jnp.where(tgt_slot // SRC_CELLS == src_index, 0, SRC_CELLS)
    keys = src_local * TGT_CELLS + tgt_local
    ranks = jnp.sum((keys[None, :] < keys[:, None]).astype(jnp.int32), axis=1)
    hits = ranks[None, :] == jnp.arange(PAIRS, dtype=jnp.int32)[:, None]
    targets = jnp.sum(jnp.where(hits, tgt_local[None, :], 0), axis=1)
    starts = jnp.sum(
        (src_local[None, :] < jnp.arange(SRC_CELLS + 1, dtype=jnp.int32)[:, None]).astype(jnp.int32), axis=1
    )
    local = jnp.arange(SRC_CELLS, dtype=jnp.int32)
    s_order = (z - local % SIDE) % SIDE * SIDE + (x - local // SIDE) % SIDE
    t_order = (z - local // SIDE) % SIDE * SIDE + (x - local % SIDE) % SIDE

    sums, small = shape(SRC_CELLS, PART), shape(TGT_CELLS, PART)
    table, row_part, first_level, live = call(
        functools.partial(first_kernel, places_s, places_t, scale),
        (shape(PAIRS, PART, PART), sums, small, sums),
        [SM] * 4 + [ANY] * (len(s_arrays) + len(t_arrays)),
        [
            pltpu.VMEM((SRC_CELLS * PART, WIDTH), BF16),
            pltpu.VMEM((TGT_CELLS * PART, WIDTH), BF16),
            pltpu.SemaphoreType.DMA((SRC_CELLS,)),
            pltpu.SemaphoreType.DMA((TGT_CELLS,)),
        ],
        starts,
        targets,
        s_order,
        t_order,
        *s_arrays,
        *t_arrays,
    )
    for sweep in range(ITERS):
        if sweep:
            row_part, _ = call(
                row_kernel,
                (sums, small),
                [SM, SM] + [VM] * 5,
                [],
                starts,
                targets,
                joined,
                before,
                after,
                first_level,
                table,
            )
        col_part, src_level = call(
            column_kernel,
            (small, sums),
            [SM, SM] + [VM] * 6,
            [pltpu.VMEM((TGT_CELLS, 8, PART), F32), pltpu.VMEM((TGT_CELLS, 8, PART), F32)],
            starts,
            targets,
            *ring_parts(row_part, x_perm),
            live,
            table,
        )
        joined = join(ring_parts(col_part, z_perm))
        before = to_group(joined[SRC_CELLS:], 1)
        after = to_group(joined[:SRC_CELLS], -1)
    blocks = call(
        functools.partial(transport_kernel, places_t),
        shape(SRC_CELLS, PART + TAIL, WIDTH, dtype=BF16),
        [SM, SM, SM] + [VM] * 6 + [ANY] * len(t_arrays),
        [
            pltpu.VMEM((TGT_CELLS * PART, WIDTH), BF16),
            pltpu.VMEM((TGT_CELLS, PART), F32),
            pltpu.VMEM((PART, WIDTH), F32),
            pltpu.SemaphoreType.DMA((TGT_CELLS,)),
        ],
        starts,
        targets,
        t_order,
        joined,
        before,
        after,
        first_level,
        src_level,
        table,
        *t_arrays,
    )
    got = lax.all_to_all(blocks, "help", 0, 0)
    source_out, target_out, transport = call(
        finish_kernel,
        (shape(SIDE, PART), shape(SIDE, PART), shape(SIDE * PART, WIDTH)),
        [SM] + [VM] * 3,
        [],
        counts,
        got,
        half_src,
        half_tgt,
    )
    return (source_out.reshape(-1), target_out.reshape(-1), transport)


def solution(mesh):
    in_specs = (
        P(None, "src"),
        P(),
        P(("src", "help"), None),
        P(("src", "help"), None),
        P(("src", "help"), None),
    )
    out_specs = (P(("src", "help")), P(("src", "help")), P(("src", "help"), None))
    return jax.shard_map(shards, mesh=mesh, in_specs=in_specs, out_specs=out_specs, check_vma=False)
```

time: 756 us -> 253 us (0.33); the launches traced: 744 us -> 252 us
  waiting for transfers between devices: 293 us -> 70.4 us
  blocking collectives: 198 us -> 0 us
  other arithmetic: 127 us -> 3.71 us
  Pallas kernels: 0 us -> 118 us
  matrix products: 36.9 us -> 0 us
  local copies, waits for them, and re-layouts: 21.6 us -> 1.54 us
  between operations: 14.1 us -> 1.08 us
    unnamed x5 -> x0, waiting for transfers between devices: 149 us -> none
    pallas_call x0 -> x6, Pallas kernels: none -> 118 us  [call(): pl.pallas_call(kernel, out_shape=out_shape, in_specs=in_specs, out_specs=...]
    pmax x2 -> x0, blocking collectives: 116 us -> none  [shards(): highest = lax.pmax(peaks.astype(jnp.bfloat16), 'help').astype(peaks.dtype)]
    reduce_sum x8 -> x5, other arithmetic: 87.1 us -> 0.75 us  [the longest x1 0.18 us: shards(): jnp.sum(jnp.square(tgt_points.astype(F32)), axis=1).reshape(SIDE, PART)]
    all_gather x5 -> x0, blocking collectives: 81.9 us -> none  [the longest x2 34.2 us: shards(): lax.all_gather(col_target_own[None, :], 'help', axis=0, tiled=True)]
    all_gather x1 -> x0, waiting for transfers between devices: 75.3 us -> none  [shards(): lax.all_gather(tgt_points, 'help', axis=0, tiled=True)]
    reduce_max x3 -> x0, other arithmetic: 37.8 us -> none  [the longest x2 24.8 us: shards(): peaks = jnp.max(scores, axis=0)]
    all_to_all x0 -> x1, waiting for transfers between devices: none -> 37.6 us  [shards(): got = lax.all_to_all(blocks, 'help', 0, 0)]
  transfers between devices with their start and end apart: 11 -> 36, of which waited for: 6 -> 20; matrix products, arithmetic and copies ran while one was open for 3% -> 1% of each run, Pallas kernels for 0% -> 0%
where the time goes in v1:
time: 253 us; the launch traced here: 252 us
  Pallas kernels  118 us (47%)
  waiting for transfers between devices  70.4 us (28%)
  starting transfers between devices  57.3 us (23%)
  other arithmetic  3.71 us (1%)
    pallas_call x6, Pallas kernels, call(): pl.pallas_call(kernel, out_shape=out_shape, in_specs=in_specs, out_specs=...  118 us
    all_to_all x1, waiting for transfers between devices, shards(): got = lax.all_to_all(blocks, 'help', 0, 0)  37.6 us
    ppermute x26, starting transfers between devices, to_help(): return lax.ppermute(array, 'help', perm)  35.9 us
    ppermute x9, waiting for transfers between devices, to_group(): lax.ppermute(array, 'src', [(i, (i + by) % count) for i in range(count)])  17.3 us
    ppermute x9, starting transfers between devices, to_group(): lax.ppermute(array, 'src', [(i, (i + by) % count) for i in range(count)])  16.1 us
    ppermute x26, waiting for transfers between devices, to_help(): return lax.ppermute(array, 'help', perm)  15.5 us
    all_to_all x1, starting transfers between devices, shards(): got = lax.all_to_all(blocks, 'help', 0, 0)  5.29 us
  transfers between devices with their start and end apart: 36, of which 20 were waited for; matrix products, arithmetic and copies ran while one was open for 1% of the time, Pallas kernels for 0%

profile of v1, /device:TPU:17, one launch (start us, length us, event | category | flops | bytes accessed | tf_op | source)
XLA Modules:
  0.0 252.5 jit_solution(3607980280253536063)
XLA Ops:
  5.3 2.5 collective-permute-start.8
  11.5 3.3 %collective-permute-start.1 = (bf16[128,512]{1,0:T(8,128)(2,1)S(1)}, bf16[128,512]{1,0:T(8,128)(2,1)S(1)}, u32[]{:S(2)}, u32[]{:S(2)}) collective-permute-start(bf16[128,512]{1,0:T(8,128)(2,1)S(1)} %get-tuple-element.34), channel_id=1, source_target_pairs={{0,8},{1,9},{2,10},{3,11},{4,12},{5,13},{6,14},{7,15},{8,0},{9,1},... | collective-permute-start | bytes 393224 | tf_op jit(solution)/shard_map/ppermute | solution.py:43
  18.3 2.9 %collective-permute-start.14 = (bf16[512,512]{1,0:T(8,128)(2,1)S(1)}, bf16[512,512]{1,0:T(8,128)(2,1)S(1)}, u32[]{:S(2)}, u32[]{:S(2)}) collective-permute-start(bf16[512,512]{1,0:T(8,128)(2,1)S(1)} %pad_maximum_fusion.1.refs_5_.refs_0_), channel_id=1, source_target_pairs={{0,112},{16,0},{32,16},{48,32},{64,48},{80,64},{96,80},{112,96},{1... | collective-permute-start | bytes 1572872 | tf_op jit(solution)/shard_map/ppermute | solution.py:39
  21.7 2.4 collective-permute-start.4
  24.2 5.9 %collective-permute-done.10.refs_6_.refs_1_ = bf16[512,512]{1,0:T(8,128)(2,1)S(1)} collective-permute-done((bf16[512,512]{1,0:T(8,128)(2,1)S(1)}, bf16[512,512]{1,0:T(8,128)(2,1)S(1)}, u32[]{:S(2)}, u32[]{:S(2)}) %collective-permute-start.10) | collective-permute-done | bytes 524320 | tf_op jit(solution)/shard_map/ppermute | solution.py:43
  33.9 3.1 %collective-permute-start.15 = (bf16[512,512]{1,0:T(8,128)(2,1)S(1)}, bf16[512,512]{1,0:T(8,128)(2,1)S(1)}, u32[]{:S(2)}, u32[]{:S(2)}) collective-permute-start(bf16[512,512]{1,0:T(8,128)(2,1)S(1)} %collective-permute-done.10.refs_6_.refs_1_), channel_id=1, source_target_pairs={{0,112},{16,0},{32,16},{48,32},{64,48},{80,64},{96,80},{112,96},{1... | collective-permute-start | bytes 1572872 | tf_op jit(solution)/shard_map/ppermute | solution.py:39
  37.2 3.1 %collective-permute-start.6 = (bf16[256,512]{1,0:T(8,128)(2,1)S(1)}, bf16[256,512]{1,0:T(8,128)(2,1)S(1)}, u32[]{:S(2)}, u32[]{:S(2)}) collective-permute-start(bf16[256,512]{1,0:T(8,128)(2,1)S(1)} %slice.57), channel_id=1, source_target_pairs={{0,3},{1,0},{2,1},{3,2},{4,7},{5,4},{6,5},{7,6},{8,11},{9,8},{10,9... | collective-permute-start | bytes 786440 | tf_op jit(solution)/shard_map/ppermute | solution.py:43
  40.3 2.2 collective-permute-start.17
  45.1 5.3 %collective-permute-done.16.refs_12_.refs_7_ = bf16[512,512]{1,0:T(8,128)(2,1)S(1)} collective-permute-done((bf16[512,512]{1,0:T(8,128)(2,1)S(1)}, bf16[512,512]{1,0:T(8,128)(2,1)S(1)}, u32[]{:S(2)}, u32[]{:S(2)}) %collective-permute-start.16) | collective-permute-done | bytes 524320 | tf_op jit(solution)/shard_map/ppermute | solution.py:39
  50.4 2.8 %collective-permute-done.17.refs_13_.refs_8_ = bf16[256,512]{1,0:T(8,128)(2,1)S(1)} collective-permute-done((bf16[256,512]{1,0:T(8,128)(2,1)S(1)}, bf16[256,512]{1,0:T(8,128)(2,1)S(1)}, u32[]{:S(2)}, u32[]{:S(2)}) %collective-permute-start.17) | collective-permute-done | bytes 262176 | tf_op jit(solution)/shard_map/ppermute | solution.py:39
  53.2 2.8 %collective-permute-done.18.refs_14_.refs_9_ = bf16[256,512]{1,0:T(8,128)(2,1)S(1)} collective-permute-done((bf16[256,512]{1,0:T(8,128)(2,1)S(1)}, bf16[256,512]{1,0:T(8,128)(2,1)S(1)}, u32[]{:S(2)}, u32[]{:S(2)}) %collective-permute-start.18) | collective-permute-done | bytes 262176 | tf_op jit(solution)/shard_map/ppermute | solution.py:39
  56.0 48.2 %shard_map.76 = (f32[128,128,128]{2,1,0:T(8,128)}, f32[16,128]{1,0:T(8,128)S(1)}, f32[32,128]{1,0:T(8,128)S(1)}, f32[16,128]{1,0:T(8,128)S(1)}) custom-call(s32[17]{0:T(128)S(1)} %convert_reduce_fusion.1.starts, s32[128]{0:T(128)S(1)} %select_reduce_fusion.targets, s32[16]{0:T(128)S(1)} %get-tuple-element.49.s_order, s32[16]{0:T(128)S(1)} %get-tuple-element.48.t_order, ...), custom_call_target="tpu_custom_call" | custom-call | tf_op jit(solution)/shard_map/pallas_call | solution.py:305
  104.4 4.1 %collective-permute-start.20 = (f32[16,128]{1,0:T(8,128)S(1)}, f32[16,128]{1,0:T(8,128)S(1)}, u32[]{:S(2)}, u32[]{:S(2)}) collective-permute-start(f32[16,128]{1,0:T(8,128)S(1)} %get-tuple-element.14.r0), channel_id=1, source_target_pairs={{0,2},{1,3},{2,0},{3,1},{4,6},{5,7},{6,4},{7,5},{8,10},{9,11},{10,... | collective-permute-start | bytes 24584 | tf_op jit(solution)/shard_map/ppermute | solution.py:43
  111.3 10.0 %shard_map.77 = (f32[32,128]{1,0:T(8,128)S(1)}, f32[16,128]{1,0:T(8,128)}) custom-call(s32[17]{0:T(128)S(1)} %convert_reduce_fusion.1.starts, s32[128]{0:T(128)S(1)} %select_reduce_fusion.targets, f32[16,128]{1,0:T(8,128)S(1)} %get-tuple-element.14.r0, f32[16,128]{1,0:T(8,128)S(1)} %collective-permute-done.19.r1, f32[16,128]{1,0:T(8,128)S(1)} %collective-permute-done.20.r2, ...), custom_call_target="tpu_custom_call" | custom-call | tf_op jit(solution)/shard_map/pallas_call | solution.py:305
  126.2 2.4 collective-permute-start.25
  129.4 2.3 collective-permute-done.26.after
  131.7 11.2 %shard_map.78 = (f32[16,128]{1,0:T(8,128)S(1)}, f32[32,128]{1,0:T(8,128)}) custom-call(s32[17]{0:T(128)S(1)} %convert_reduce_fusion.1.starts, s32[128]{0:T(128)S(1)} %select_reduce_fusion.targets, f32[32,128]{1,0:T(8,128)S(1)} %multiply_add_fusion.1.joined, f32[16,128]{1,0:T(8,128)S(1)} %collective-permute-done.25.before, ...), custom_call_target="tpu_custom_call" | custom-call | tf_op jit(solution)/shard_map/pallas_call | solution.py:305
  142.9 2.1 collective-permute-start.28
  147.5 9.5 %shard_map.79 = (f32[32,128]{1,0:T(8,128)S(1)}, f32[16,128]{1,0:T(8,128)S(1)}) custom-call(s32[17]{0:T(128)S(1)} %convert_reduce_fusion.1.starts, s32[128]{0:T(128)S(1)} %select_reduce_fusion.targets, f32[16,128]{1,0:T(8,128)S(1)} %get-tuple-element.19.r0, f32[16,128]{1,0:T(8,128)S(1)} %collective-permute-done.27.r1, ...), custom_call_target="tpu_custom_call" | custom-call | tf_op jit(solution)/shard_map/pallas_call | solution.py:305
  163.1 3.3 %collective-permute-start.33 = (f32[16,128]{1,0:T(8,128)S(1)}, f32[16,128]{1,0:T(8,128)S(1)}, u32[]{:S(2)}, u32[]{:S(2)}) collective-permute-start(f32[16,128]{1,0:T(8,128)S(1)} %get-tuple-element.37), channel_id=1, source_target_pairs={{0,16},{16,32},{32,48},{48,64},{64,80},{80,96},{96,112},{112,0},{1... | collective-permute-start | bytes 24584 | tf_op jit(solution)/shard_map/ppermute | solution.py:39
  167.3 2.3 collective-permute-done.34.after
  169.5 37.7 %shard_map.80 = bf16[16,144,512]{2,1,0:T(8,128)(2,1)} custom-call(s32[17]{0:T(128)S(1)} %convert_reduce_fusion.1.starts, s32[128]{0:T(128)S(1)} %select_reduce_fusion.targets, s32[16]{0:T(128)S(1)} %get-tuple-element.48.t_order, f32[32,128]{1,0:T(8,128)S(1)} %multiply_add_fusion.joined, f32[16,128]{1,0:T(8,128)S(1)} %collective-permute-done.33.before, ...), custom_call_target="tpu_custom_call" | custom-call | tf_op jit(solution)/shard_map/pallas_call | solution.py:305
  207.3 5.3 %all-to-all-start = ((bf16[16,144,512]{2,1,0:T(8,128)(2,1)}), bf16[16,144,512]{2,1,0:T(8,128)(2,1)S(1)}, u32[]{:S(2)}, u32[]{:S(2)}) async-start(bf16[16,144,512]{2,1,0:T(8,128)(2,1)} %shard_map.80), calls=%async_computation | async-start | bytes 4718592 | tf_op jit(solution)/shard_map/all_to_all | solution.py:427
  213.0 37.6 %all-to-all-done.got = bf16[16,144,512]{2,1,0:T(8,128)(2,1)S(1)} async-done(((bf16[16,144,512]{2,1,0:T(8,128)(2,1)}), bf16[16,144,512]{2,1,0:T(8,128)(2,1)S(1)}, u32[]{:S(2)}, u32[]{:S(2)}) %all-to-all-start) | async-done | bytes 2359328 | tf_op jit(solution)/shard_map/all_to_all | solution.py:427
  (97 shorter events, 39.0 us)
Async XLA Ops:
  4.0 10.8 %collective-permute-start.7 = (bf16[128,512]{1,0:T(8,128)(2,1)S(1)}, bf16[128,512]{1,0:T(8,128)(2,1)S(1)}, u32[]{:S(2)}, u32[]{:S(2)}) collective-permute-start(bf16[128,512]{1,0:T(8,128)(2,1)S(1)} %get-tuple-element.31), channel_id=1, source_target_pairs={{0,1},{1,2},{2,3},{3,0},{4,5},{5,6},{6,7},{7,4},{8,9},{9,10},{10,1... | collective-permute-start | bytes 393224 | tf_op jit(solution)/shard_map/ppermute | solution.py:43
  5.3 10.3 %collective-permute-start.8 = (bf16[128,512]{1,0:T(8,128)(2,1)S(1)}, bf16[128,512]{1,0:T(8,128)(2,1)S(1)}, u32[]{:S(2)}, u32[]{:S(2)}) collective-permute-start(bf16[128,512]{1,0:T(8,128)(2,1)S(1)} %get-tuple-element.30), channel_id=1, source_target_pairs={{0,2},{1,3},{2,0},{3,1},{4,6},{5,7},{6,4},{7,5},{8,10},{9,11},{10,... | collective-permute-start | bytes 393224 | tf_op jit(solution)/shard_map/ppermute | solution.py:43
  7.7 7.8 %collective-permute-start.9 = (bf16[128,512]{1,0:T(8,128)(2,1)S(1)}, bf16[128,512]{1,0:T(8,128)(2,1)S(1)}, u32[]{:S(2)}, u32[]{:S(2)}) collective-permute-start(bf16[128,512]{1,0:T(8,128)(2,1)S(1)} %get-tuple-element.29), channel_id=1, source_target_pairs={{0,3},{1,0},{2,1},{3,2},{4,7},{5,4},{6,5},{7,6},{8,11},{9,8},{10,9... | collective-permute-start | bytes 393224 | tf_op jit(solution)/shard_map/ppermute | solution.py:43
  9.8 8.5 %collective-permute-start = (bf16[128,512]{1,0:T(8,128)(2,1)S(1)}, bf16[128,512]{1,0:T(8,128)(2,1)S(1)}, u32[]{:S(2)}, u32[]{:S(2)}) collective-permute-start(bf16[128,512]{1,0:T(8,128)(2,1)S(1)} %get-tuple-element.35), channel_id=1, source_target_pairs={{0,4},{1,5},{2,6},{3,7},{4,8},{5,9},{6,10},{7,11},{8,12},{9,13},{1... | collective-permute-start | bytes 393224 | tf_op jit(solution)/shard_map/ppermute | solution.py:43
  11.5 9.8 %collective-permute-start.1 = (bf16[128,512]{1,0:T(8,128)(2,1)S(1)}, bf16[128,512]{1,0:T(8,128)(2,1)S(1)}, u32[]{:S(2)}, u32[]{:S(2)}) collective-permute-start(bf16[128,512]{1,0:T(8,128)(2,1)S(1)} %get-tuple-element.34), channel_id=1, source_target_pairs={{0,8},{1,9},{2,10},{3,11},{4,12},{5,13},{6,14},{7,15},{8,0},{9,1},... | collective-permute-start | bytes 393224 | tf_op jit(solution)/shard_map/ppermute | solution.py:43
  14.8 6.4 %collective-permute-start.2 = (bf16[128,512]{1,0:T(8,128)(2,1)S(1)}, bf16[128,512]{1,0:T(8,128)(2,1)S(1)}, u32[]{:S(2)}, u32[]{:S(2)}) collective-permute-start(bf16[128,512]{1,0:T(8,128)(2,1)S(1)} %get-tuple-element.33), channel_id=1, source_target_pairs={{0,12},{1,13},{2,14},{3,15},{4,0},{5,1},{6,2},{7,3},{8,4},{9,5},{1... | collective-permute-start | bytes 393224 | tf_op jit(solution)/shard_map/ppermute | solution.py:43
  15.6 14.6 %collective-permute-start.10 = (bf16[512,512]{1,0:T(8,128)(2,1)S(1)}, bf16[512,512]{1,0:T(8,128)(2,1)S(1)}, u32[]{:S(2)}, u32[]{:S(2)}) collective-permute-start(bf16[512,512]{1,0:T(8,128)(2,1)S(1)} %pad_maximum_fusion.1.refs_5_.refs_0_), channel_id=1, source_target_pairs={{0,4},{1,5},{2,6},{3,7},{4,8},{5,9},{6,10},{7,11},{8,12},{9,13},{1... | collective-permute-start | bytes 1572872 | tf_op jit(solution)/shard_map/ppermute | solution.py:43
  16.4 15.2 %collective-permute-start.11 = (bf16[512,512]{1,0:T(8,128)(2,1)S(1)}, bf16[512,512]{1,0:T(8,128)(2,1)S(1)}, u32[]{:S(2)}, u32[]{:S(2)}) collective-permute-start(bf16[512,512]{1,0:T(8,128)(2,1)S(1)} %pad_maximum_fusion.1.refs_5_.refs_0_), channel_id=1, source_target_pairs={{0,12},{1,13},{2,14},{3,15},{4,0},{5,1},{6,2},{7,3},{8,4},{9,5},{1... | collective-permute-start | bytes 1572872 | tf_op jit(solution)/shard_map/ppermute | solution.py:43
  18.3 15.6 %collective-permute-start.14 = (bf16[512,512]{1,0:T(8,128)(2,1)S(1)}, bf16[512,512]{1,0:T(8,128)(2,1)S(1)}, u32[]{:S(2)}, u32[]{:S(2)}) collective-permute-start(bf16[512,512]{1,0:T(8,128)(2,1)S(1)} %pad_maximum_fusion.1.refs_5_.refs_0_), channel_id=1, source_target_pairs={{0,112},{16,0},{32,16},{48,32},{64,48},{80,64},{96,80},{112,96},{1... | collective-permute-start | bytes 1572872 | tf_op jit(solution)/shard_map/ppermute | solution.py:39
  21.3 12.1 %collective-permute-start.3 = (bf16[512,512]{1,0:T(8,128)(2,1)S(1)}, bf16[512,512]{1,0:T(8,128)(2,1)S(1)}, u32[]{:S(2)}, u32[]{:S(2)}) collective-permute-start(bf16[512,512]{1,0:T(8,128)(2,1)S(1)} %pad_maximum_fusion.refs_0_), channel_id=1, source_target_pairs={{0,1},{1,2},{2,3},{3,0},{4,5},{5,6},{6,7},{7,4},{8,9},{9,10},{10,1... | collective-permute-start | bytes 1572872 | tf_op jit(solution)/shard_map/ppermute | solution.py:43
  21.7 15.4 %collective-permute-start.4 = (bf16[512,512]{1,0:T(8,128)(2,1)S(1)}, bf16[512,512]{1,0:T(8,128)(2,1)S(1)}, u32[]{:S(2)}, u32[]{:S(2)}) collective-permute-start(bf16[512,512]{1,0:T(8,128)(2,1)S(1)} %pad_maximum_fusion.refs_0_), channel_id=1, source_target_pairs={{0,3},{1,0},{2,1},{3,2},{4,7},{5,4},{6,5},{7,6},{8,11},{9,8},{10,9... | collective-permute-start | bytes 1572872 | tf_op jit(solution)/shard_map/ppermute | solution.py:43
  30.2 7.0 %collective-permute-start.12 = (bf16[256,512]{1,0:T(8,128)(2,1)S(1)}, bf16[256,512]{1,0:T(8,128)(2,1)S(1)}, u32[]{:S(2)}, u32[]{:S(2)}) collective-permute-start(bf16[256,512]{1,0:T(8,128)(2,1)S(1)} %slice.58), channel_id=1, source_target_pairs={{0,4},{1,5},{2,6},{3,7},{4,8},{5,9},{6,10},{7,11},{8,12},{9,13},{1... | collective-permute-start | bytes 786440 | tf_op jit(solution)/shard_map/ppermute | solution.py:43
  31.6 8.7 %collective-permute-start.13 = (bf16[256,512]{1,0:T(8,128)(2,1)S(1)}, bf16[256,512]{1,0:T(8,128)(2,1)S(1)}, u32[]{:S(2)}, u32[]{:S(2)}) collective-permute-start(bf16[256,512]{1,0:T(8,128)(2,1)S(1)} %slice.59), channel_id=1, source_target_pairs={{0,12},{1,13},{2,14},{3,15},{4,0},{5,1},{6,2},{7,3},{8,4},{9,5},{1... | collective-permute-start | bytes 786440 | tf_op jit(solution)/shard_map/ppermute | solution.py:43
  33.4 9.1 %collective-permute-start.5 = (bf16[256,512]{1,0:T(8,128)(2,1)S(1)}, bf16[256,512]{1,0:T(8,128)(2,1)S(1)}, u32[]{:S(2)}, u32[]{:S(2)}) collective-permute-start(bf16[256,512]{1,0:T(8,128)(2,1)S(1)} %slice.56), channel_id=1, source_target_pairs={{0,1},{1,2},{2,3},{3,0},{4,5},{5,6},{6,7},{7,4},{8,9},{9,10},{10,1... | collective-permute-start | bytes 786440 | tf_op jit(solution)/shard_map/ppermute | solution.py:43
  33.9 11.2 %collective-permute-start.15 = (bf16[512,512]{1,0:T(8,128)(2,1)S(1)}, bf16[512,512]{1,0:T(8,128)(2,1)S(1)}, u32[]{:S(2)}, u32[]{:S(2)}) collective-permute-start(bf16[512,512]{1,0:T(8,128)(2,1)S(1)} %collective-permute-done.10.refs_6_.refs_1_), channel_id=1, source_target_pairs={{0,112},{16,0},{32,16},{48,32},{64,48},{80,64},{96,80},{112,96},{1... | collective-permute-start | bytes 1572872 | tf_op jit(solution)/shard_map/ppermute | solution.py:39
  37.0 13.4 %collective-permute-start.16 = (bf16[512,512]{1,0:T(8,128)(2,1)S(1)}, bf16[512,512]{1,0:T(8,128)(2,1)S(1)}, u32[]{:S(2)}, u32[]{:S(2)}) collective-permute-start(bf16[512,512]{1,0:T(8,128)(2,1)S(1)} %collective-permute-done.11.refs_7_.refs_2_), channel_id=1, source_target_pairs={{0,112},{16,0},{32,16},{48,32},{64,48},{80,64},{96,80},{112,96},{1... | collective-permute-start | bytes 1572872 | tf_op jit(solution)/shard_map/ppermute | solution.py:39
  37.2 7.7 %collective-permute-start.6 = (bf16[256,512]{1,0:T(8,128)(2,1)S(1)}, bf16[256,512]{1,0:T(8,128)(2,1)S(1)}, u32[]{:S(2)}, u32[]{:S(2)}) collective-permute-start(bf16[256,512]{1,0:T(8,128)(2,1)S(1)} %slice.57), channel_id=1, source_target_pairs={{0,3},{1,0},{2,1},{3,2},{4,7},{5,4},{6,5},{7,6},{8,11},{9,8},{10,9... | collective-permute-start | bytes 786440 | tf_op jit(solution)/shard_map/ppermute | solution.py:43
  40.3 12.9 %collective-permute-start.17 = (bf16[256,512]{1,0:T(8,128)(2,1)S(1)}, bf16[256,512]{1,0:T(8,128)(2,1)S(1)}, u32[]{:S(2)}, u32[]{:S(2)}) collective-permute-start(bf16[256,512]{1,0:T(8,128)(2,1)S(1)} %collective-permute-done.12.refs_8_.refs_3_), channel_id=1, source_target_pairs={{0,112},{16,0},{32,16},{48,32},{64,48},{80,64},{96,80},{112,96},{1... | collective-permute-start | bytes 786440 | tf_op jit(solution)/shard_map/ppermute | solution.py:39
  42.6 13.5 %collective-permute-start.18 = (bf16[256,512]{1,0:T(8,128)(2,1)S(1)}, bf16[256,512]{1,0:T(8,128)(2,1)S(1)}, u32[]{:S(2)}, u32[]{:S(2)}) collective-permute-start(bf16[256,512]{1,0:T(8,128)(2,1)S(1)} %collective-permute-done.13.refs_9_.refs_4_), channel_id=1, source_target_pairs={{0,112},{16,0},{32,16},{48,32},{64,48},{80,64},{96,80},{112,96},{1... | collective-permute-start | bytes 786440 | tf_op jit(solution)/shard_map/ppermute | solution.py:39
  104.3 4.2 %collective-permute-start.19 = (f32[16,128]{1,0:T(8,128)S(1)}, f32[16,128]{1,0:T(8,128)S(1)}, u32[]{:S(2)}, u32[]{:S(2)}) collective-permute-start(f32[16,128]{1,0:T(8,128)S(1)} %get-tuple-element.14.r0), channel_id=1, source_target_pairs={{0,1},{1,2},{2,3},{3,0},{4,5},{5,6},{6,7},{7,4},{8,9},{9,10},{10,1... | collective-permute-start | bytes 24584 | tf_op jit(solution)/shard_map/ppermute | solution.py:43
  104.4 5.2 %collective-permute-start.20 = (f32[16,128]{1,0:T(8,128)S(1)}, f32[16,128]{1,0:T(8,128)S(1)}, u32[]{:S(2)}, u32[]{:S(2)}) collective-permute-start(f32[16,128]{1,0:T(8,128)S(1)} %get-tuple-element.14.r0), channel_id=1, source_target_pairs={{0,2},{1,3},{2,0},{3,1},{4,6},{5,7},{6,4},{7,5},{8,10},{9,11},{10,... | collective-permute-start | bytes 24584 | tf_op jit(solution)/shard_map/ppermute | solution.py:43
  121.3 4.1 %collective-permute-start.23 = (f32[32,128]{1,0:T(8,128)S(1)}, f32[32,128]{1,0:T(8,128)S(1)}, u32[]{:S(2)}, u32[]{:S(2)}) collective-permute-start(f32[32,128]{1,0:T(8,128)S(1)} %get-tuple-element.17), channel_id=1, source_target_pairs={{0,8},{1,9},{2,10},{3,11},{4,12},{5,13},{6,14},{7,15},{8,0},{9,1},... | collective-permute-start | bytes 49160 | tf_op jit(solution)/shard_map/ppermute | solution.py:43
  163.1 4.1 %collective-permute-start.33 = (f32[16,128]{1,0:T(8,128)S(1)}, f32[16,128]{1,0:T(8,128)S(1)}, u32[]{:S(2)}, u32[]{:S(2)}) collective-permute-start(f32[16,128]{1,0:T(8,128)S(1)} %get-tuple-element.37), channel_id=1, source_target_pairs={{0,16},{16,32},{32,48},{48,64},{64,80},{80,96},{96,112},{112,0},{1... | collective-permute-start | bytes 24584 | tf_op jit(solution)/shard_map/ppermute | solution.py:39
  207.3 43.3 %all-to-all-start = ((bf16[16,144,512]{2,1,0:T(8,128)(2,1)}), bf16[16,144,512]{2,1,0:T(8,128)(2,1)S(1)}, u32[]{:S(2)}, u32[]{:S(2)}) async-start(bf16[16,144,512]{2,1,0:T(8,128)(2,1)} %shard_map.80), calls=%async_computation | async-start | bytes 4718592 | tf_op jit(solution)/shard_map/all_to_all | solution.py:427
  (19 other events, 170.5 us)

commit v2 on v1

--- a/solution.py
+++ b/solution.py
@@ -21,6 +21,11 @@
 TGT_CELLS = 32
 TAIL = 16
 PAIRS = 128
+BATCH = 4
+BATCHES = (PAIRS + (BATCH - 1) * SRC_CELLS) // BATCH
+STEPS = (BATCHES + 1) // 2
+NOBODY = TGT_CELLS
+LEVELS = 40
 F32 = jnp.float32
 BF16 = jnp.bfloat16
 VMEM_LIMIT = 48 * 1024 * 1024
@@ -114,39 +119,70 @@
             )
     for copy in copies:
         copy.start()
-    return copies
-
-
-def row_sums(starts, targets, table_ref, level_ref, sums_ref, fill):
+    return list(enumerate(copies))
+
+
+def batch_targets(entries, b):
+    return [entries[b * BATCH + k] for k in range(BATCH)]
+
+
+def tile(k):
+    return slice(k * PART, (k + 1) * PART)
+
+
+def row_stats(scores, s, tops, totals):
+    old = tops[s]
+    top = functools.reduce(jnp.maximum, scores, old)
+    total = functools.reduce(jnp.add, [jnp.exp2(one - top) for one in scores])
+    totals[s] = totals[s] * jnp.exp2(old - top) + total
+    tops[s] = top
+
+
+def clear_stats(tops, totals):
+    for one in tops:
+        one[...] = jnp.full(one.shape, EMPTY, F32)
+    for one in totals:
+        one[...] = jnp.ones(one.shape, F32)
+
+
+def store_row_sums(tops, totals, sums_ref):
     def cell(s, carry):
-        first, last = starts[s], starts[s + 1]
-
-        def highest(n, top):
-            scores = (fill(s, n) if fill is not None else table_ref[n]) + level_ref[pl.ds(targets[n], 1), :]
-            return jnp.maximum(top, scores)
-
-        top = lax.fori_loop(first, last, highest, jnp.full((PART, PART), EMPTY, F32))
-        top = jnp.max(top, axis=1, keepdims=True)
-
-        def add(n, total):
-            return total + jnp.exp2(table_ref[n] + level_ref[pl.ds(targets[n], 1), :] - top)
-
-        total = lax.fori_loop(first, last, add, jnp.zeros((PART, PART), F32))
+        top = jnp.max(jnp.maximum(tops[0][s], tops[1][s]), axis=1, keepdims=True)
+        total = totals[0][s] * jnp.exp2(tops[0][s] - top) + totals[1][s] * jnp.exp2(tops[1][s] - top)
         total = jnp.sum(total, axis=1, keepdims=True)
         sums_ref[pl.ds(s, 1), :] = to_lanes(top + jnp.log2(total))
         return carry
 
-    lax.fori_loop(0, SRC_CELLS, cell, 0)
-
-
-def first_kernel(places_s, places_t, scale, starts, targets, s_order, t_order, *refs):
+    lax.fori_loop(0, SRC_CELLS, cell, 0, unroll=4)
+
+
+def table_copy(kept, table, sem, step, out=False):
+    ends = (table.at[step], kept.at[step])
+    return pltpu.make_async_copy(*(ends if out else ends[::-1]), sem.at[step])
+
+
+def start_table(kept, table, sem, steps):
+    def one(step, carry):
+        table_copy(kept, table, sem, step).start()
+        return carry
+
+    lax.fori_loop(0, steps, one, 0)
+
+
+def first_kernel(places_s, places_t, scale, entries, batches, s_order, t_order, *refs):
     ns, nt = len(places_s), len(places_t)
     s_refs, t_refs = refs[:ns], refs[ns : ns + nt]
-    table_ref, sums_ref, level_ref, live_ref = refs[ns + nt : ns + nt + 4]
-    xs, ys, s_sem, t_sem = refs[ns + nt + 4 :]
-    copies = load_blocks(s_refs, places_s, s_order, xs, s_sem)
-    copies += load_blocks(t_refs, places_t, t_order, ys, t_sem)
-    for copy in copies:
+    kept, sums_ref, first_ref, live_ref = refs[ns + nt : ns + nt + 4]
+    xs, ys, level_ref, top0, top1, total0, total1, table, s_sem, t_sem, sem = refs[ns + nt + 4 :]
+    tops, totals = (top0, top1), (total0, total1)
+    s_copies = load_blocks(s_refs, places_s, s_order, xs, s_sem)
+    t_copies = load_blocks(t_refs, places_t, t_order, ys, t_sem)
+    steps = batches[0]
+    clear_stats(tops, totals)
+    level_ref[...] = jnp.full(level_ref.shape, DEAD, F32)
+    for place, copy in s_copies:
+        copy.wait()
+    for place, copy in t_copies:
         copy.wait()
 
     def target_cell(t, carry):
@@ -155,7 +191,8 @@
         level_ref[pl.ds(t, 1), :] = jnp.where(half > 1e7, DEAD, -half)
         return carry
 
-    lax.fori_loop(0, TGT_CELLS, target_cell, 0)
+    lax.fori_loop(0, TGT_CELLS, target_cell, 0, unroll=4)
+    first_ref[...] = level_ref[:TGT_CELLS, :]
 
     def source_cell(s, carry):
         mark = xs[part_of(s), :PART].astype(F32)
@@ -163,50 +200,79 @@
         live_ref[pl.ds(s, 1), :] = jnp.sum(dead, axis=0, keepdims=True)
         return carry
 
-    lax.fori_loop(0, SRC_CELLS, source_cell, 0)
-
-    def fill(s, n):
-        inner = lax.dot_general(
-            xs[part_of(s), :],
-            ys[part_of(targets[n]), :],
-            (((1,), (1,)), ((), ())),
-            preferred_element_type=F32,
-        )
-        inner = inner * scale
-        table_ref[n] = inner
-        return inner
-
-    row_sums(starts, targets, table_ref, level_ref, sums_ref, fill)
+    lax.fori_loop(0, SRC_CELLS, source_cell, 0, unroll=4)
+
+    def step(i, carry):
+        for half in range(2):
+            b = 2 * i + half
+            near = batch_targets(entries, b)
+            points = jnp.concatenate([ys[part_of(lax.rem(t, NOBODY)), :] for t in near], axis=0)
+            s = batches[1 + b]
+            inner = lax.dot_general(
+                xs[part_of(s), :], points, (((1,), (1,)), ((), ())), preferred_element_type=F32
+            )
+            inner = inner * scale
+            table[i, half] = inner
+            scores = [inner[:, tile(k)] + level_ref[pl.ds(t, 1), :] for k, t in enumerate(near)]
+            row_stats(scores, s, tops[half], totals[half])
+        table_copy(kept, table, sem, i, out=True).start()
+        return carry
+
+    lax.fori_loop(0, steps, step, 0)
+    store_row_sums(tops, totals, sums_ref)
+
+    def settle(i, carry):
+        table_copy(kept, table, sem, i, out=True).wait()
+        return carry
+
+    lax.fori_loop(0, steps, settle, 0)
 
 
 def source_levels(parts, live):
     return jnp.where(live < 0.5 * DEAD, DEAD, -join([part[...] for part in parts]))
 
 
-def column_kernel(starts, targets, r0, r1, r2, r3, live_ref, table_ref, sums_ref, level_ref, tops, totals):
+def spread_rows(level_ref, wide_ref):
+    def cell(s, carry):
+        wide_ref[s] = to_rows(level_ref[pl.ds(s, 1), :])
+        return carry
+
+    lax.fori_loop(0, SRC_CELLS, cell, 0, unroll=4)
+
+
+def column_kernel(
+    entries, batches, r0, r1, r2, r3, live_ref, kept, sums_ref, level_ref, top0, top1, total0, total1, wide_ref, table, sem
+):
+    tops, totals = (top0, top1), (total0, total1)
+    steps = batches[0]
+    start_table(kept, table, sem, steps)
     level_ref[...] = source_levels((r0, r1, r2, r3), live_ref[...])
-    tops[...] = jnp.full(tops.shape, EMPTY, F32)
-    totals[...] = jnp.ones(totals.shape, F32)
-
-    def cell(s, carry):
-        level = to_rows(level_ref[pl.ds(s, 1), :])
-
-        def tile(n, inner_carry):
-            t = targets[n]
-            scores = (table_ref[n] + level).reshape(PART // 8, 8, PART)
-            old = tops[t]
-            top = jnp.maximum(old, jnp.max(scores, axis=0))
-            tops[t] = top
-            totals[t] = totals[t] * jnp.exp2(old - top) + jnp.sum(jnp.exp2(scores - top[None]), axis=0)
-            return inner_carry
-
-        return lax.fori_loop(starts[s], starts[s + 1], tile, carry)
-
-    lax.fori_loop(0, SRC_CELLS, cell, 0)
-    tops_all = tops[...]
-    top = jnp.max(tops_all, axis=1)
-    total = jnp.sum(totals[...] * jnp.exp2(tops_all - top[:, None, :]), axis=1)
-    sums_ref[...] = top + jnp.log2(total)
+    spread_rows(level_ref, wide_ref)
+    clear_stats(tops, totals)
+
+    def step(i, carry):
+        table_copy(kept, table, sem, i).wait()
+        for half in range(2):
+            b = 2 * i + half
+            near = batch_targets(entries, b)
+            level = wide_ref[batches[1 + b]]
+            old = [(tops[half][t], totals[half][t]) for t in near]
+            new = []
+            for k, (old_top, old_total) in enumerate(old):
+                scores = (table[i, half, :, tile(k)] + level).reshape(PART // 8, 8, PART)
+                top = jnp.maximum(old_top, jnp.max(scores, axis=0))
+                total = jnp.sum(jnp.exp2(scores - top[None]), axis=0)
+                new.append((top, old_total * jnp.exp2(old_top - top) + total))
+            for t, (top, total) in zip(near, new):
+                tops[half][t] = top
+                totals[half][t] = total
+        return carry
+
+    lax.fori_loop(0, steps, step, 0)
+    tops = [one[:TGT_CELLS] for one in tops]
+    top = jnp.max(jnp.maximum(*tops), axis=1)
+    total = sum(kept_total[:TGT_CELLS] * jnp.exp2(one - top[:, None, :]) for one, kept_total in zip(tops, totals))
+    sums_ref[...] = top + jnp.log2(jnp.sum(total, axis=1))
 
 
 def target_levels(joined, before, after, first_level):
@@ -216,9 +282,27 @@
     return jnp.where(first_level < 0.5 * DEAD, DEAD, levels)
 
 
-def row_kernel(starts, targets, joined, before, after, first_level, table_ref, sums_ref, level_ref):
-    level_ref[...] = target_levels(joined[...], before[...], after[...], first_level[...])
-    row_sums(starts, targets, table_ref, level_ref, sums_ref, None)
+def row_kernel(
+    entries, batches, joined, before, after, first_level, kept, sums_ref, level_ref, top0, top1, total0, total1, table, sem
+):
+    tops, totals = (top0, top1), (total0, total1)
+    steps = batches[0]
+    start_table(kept, table, sem, steps)
+    level_ref[:TGT_CELLS, :] = target_levels(joined[...], before[...], after[...], first_level[...])
+    level_ref[TGT_CELLS:, :] = jnp.full((LEVELS - TGT_CELLS, PART), DEAD, F32)
+    clear_stats(tops, totals)
+
+    def step(i, carry):
+        table_copy(kept, table, sem, i).wait()
+        for half in range(2):
+            b = 2 * i + half
+            near = batch_targets(entries, b)
+            scores = [table[i, half, :, tile(k)] + level_ref[pl.ds(t, 1), :] for k, t in enumerate(near)]
+            row_stats(scores, batches[1 + b], tops[half], totals[half])
+        return carry
+
+    lax.fori_loop(0, steps, step, 0)
+    store_row_sums(tops, totals, sums_ref)
 
 
 def pieces(value, count):
@@ -230,32 +314,47 @@
     return found
 
 
-def transport_kernel(places_t, starts, targets, t_order, joined, before, after, first_level, src_level, table_ref, *refs):
+def transport_kernel(
+    places_t, entries, batches, t_order, joined, before, after, first_level, src_level, kept, *refs
+):
     nt = len(places_t)
     t_refs = refs[:nt]
-    out_ref, ys, level_ref, total_ref, t_sem = refs[nt:]
+    out_ref, ys, level_ref, wide_ref, map0, map1, mass0, mass1, table, t_sem, sem = refs[nt:]
+    maps, masses = (map0, map1), (mass0, mass1)
+    steps = batches[0]
     copies = load_blocks(t_refs, places_t, t_order, ys, t_sem)
-    level_ref[...] = target_levels(joined[...], before[...], after[...], first_level[...])
-    for copy in copies:
+    start_table(kept, table, sem, steps)
+    level_ref[:TGT_CELLS, :] = target_levels(joined[...], before[...], after[...], first_level[...])
+    level_ref[TGT_CELLS:, :] = jnp.full((LEVELS - TGT_CELLS, PART), DEAD, F32)
+    spread_rows(src_level, wide_ref)
+    for one in maps + masses:
+        one[...] = jnp.zeros(one.shape, F32)
+    for place, copy in copies:
         copy.wait()
 
+    def step(i, carry):
+        table_copy(kept, table, sem, i).wait()
+        for half in range(2):
+            b = 2 * i + half
+            near = batch_targets(entries, b)
+            s = batches[1 + b]
+            level = wide_ref[s]
+            weights = [
+                jnp.exp2(table[i, half, :, tile(k)] + level_ref[pl.ds(t, 1), :] + level).astype(BF16)
+                for k, t in enumerate(near)
+            ]
+            points = jnp.concatenate([ys[part_of(lax.rem(t, NOBODY)), :] for t in near], axis=0)
+            maps[half][s] += jnp.dot(jnp.concatenate(weights, axis=1), points, preferred_element_type=F32)
+            masses[half][s] += functools.reduce(jnp.add, [one.astype(F32) for one in weights])
+        return carry
+
+    lax.fori_loop(0, steps, step, 0)
+    rows = lax.broadcasted_iota(jnp.int32, (TAIL, WIDTH), 0)
+
     def cell(s, carry):
-        row_level = src_level[pl.ds(s, 1), :]
-        level = to_rows(row_level)
-        total_ref[...] = jnp.zeros(total_ref.shape, F32)
-
-        def tile(n, weight_sum):
-            t = targets[n]
-            weight = jnp.exp2(table_ref[n] + level_ref[pl.ds(t, 1), :] + level).astype(BF16)
-            total_ref[...] += jnp.dot(weight, ys[part_of(t), :], preferred_element_type=F32)
-            return weight_sum + weight.astype(F32)
-
-        weight_sum = lax.fori_loop(starts[s], starts[s + 1], tile, jnp.zeros((PART, PART), F32))
-        weight_sum = to_lanes(jnp.sum(weight_sum, axis=1, keepdims=True))
-        out_ref[s, :PART, :] = total_ref[...].astype(BF16)
-        col_level = level_ref[pl.ds(s, 1), :]
-        parts = pieces(weight_sum, 2) + pieces(row_level, 3) + pieces(col_level, 3)
-        rows = lax.broadcasted_iota(jnp.int32, (TAIL, WIDTH), 0)
+        mass = to_lanes(jnp.sum(mass0[s] + mass1[s], axis=1, keepdims=True))
+        out_ref[s, :PART, :] = (map0[s] + map1[s]).astype(BF16)
+        parts = pieces(mass, 2) + pieces(src_level[pl.ds(s, 1), :], 3) + pieces(level_ref[pl.ds(s, 1), :], 3)
         tail = jnp.where(
             rows == 0,
             jnp.concatenate(parts[:4], axis=1),
@@ -264,7 +363,7 @@
         out_ref[s, PART:, :] = tail.astype(BF16)
         return carry
 
-    lax.fori_loop(0, SRC_CELLS, cell, 0)
+    lax.fori_loop(0, SRC_CELLS, cell, 0, unroll=2)
 
 
 def finish_kernel(counts, got, half_src, half_tgt, src_ref, tgt_ref, map_ref):
@@ -300,8 +399,8 @@
 ANY = pl.BlockSpec(memory_space=pl.ANY)
 
 
-def call(kernel, out_shape, in_specs, scratch, *args):
-    outs = jax.tree.map(lambda _: VM, out_shape)
+def call(kernel, out_shape, in_specs, scratch, *args, out_specs=None):
+    outs = jax.tree.map(lambda _: VM, out_shape) if out_specs is None else out_specs
     return pl.pallas_call(
         kernel,
         out_shape=out_shape,
@@ -345,60 +444,81 @@
     tgt_slot = lookup(tiles[1], cell_slot[1])
     src_local = src_slot % SRC_CELLS
     tgt_local = tgt_slot % SRC_CELLS + jnp.where(tgt_slot // SRC_CELLS == src_index, 0, SRC_CELLS)
-    keys = src_local * TGT_CELLS + tgt_local
-    ranks = jnp.sum((keys[None, :] < keys[:, None]).astype(jnp.int32), axis=1)
-    hits = ranks[None, :] == jnp.arange(PAIRS, dtype=jnp.int32)[:, None]
-    targets = jnp.sum(jnp.where(hits, tgt_local[None, :], 0), axis=1)
-    starts = jnp.sum(
-        (src_local[None, :] < jnp.arange(SRC_CELLS + 1, dtype=jnp.int32)[:, None]).astype(jnp.int32), axis=1
-    )
+    same = src_local[None, :] == src_local[:, None]
+    earlier = jnp.arange(PAIRS)[None, :] < jnp.arange(PAIRS)[:, None]
+    rank = jnp.sum((same & earlier).astype(jnp.int32), axis=1)
+    cells = jnp.arange(SRC_CELLS, dtype=jnp.int32)
+    listed = jnp.sum((src_local[None, :] == cells[:, None]).astype(jnp.int32), axis=1)
+    used = (listed + (BATCH - 1)) // BATCH
+    ends = jnp.sum(jnp.where(cells[None, :] <= cells[:, None], used[None, :], 0), axis=1)
+    begins = ends - used
+    begin_of = jnp.sum(jnp.where(src_local[:, None] == cells[None, :], begins[None, :], 0), axis=1)
+    place = begin_of * BATCH + rank
+    hits = place[None, :] == jnp.arange(2 * STEPS * BATCH, dtype=jnp.int32)[:, None]
+    entries = jnp.sum(jnp.where(hits, tgt_local[None, :] - NOBODY, 0), axis=1) + NOBODY
+    numbers = jnp.arange(2 * STEPS, dtype=jnp.int32)
+    batch_src = jnp.sum((ends[None, :] <= numbers[:, None]).astype(jnp.int32), axis=1)
+    batch_src = jnp.minimum(batch_src, SRC_CELLS - 1)
+    batches = jnp.concatenate([(ends[-1:] + 1) // 2, batch_src])
     local = jnp.arange(SRC_CELLS, dtype=jnp.int32)
     s_order = (z - local % SIDE) % SIDE * SIDE + (x - local // SIDE) % SIDE
     t_order = (z - local // SIDE) % SIDE * SIDE + (x - local % SIDE) % SIDE
 
     sums, small = shape(SRC_CELLS, PART), shape(TGT_CELLS, PART)
-    table, row_part, first_level, live = call(
+    levels = pltpu.VMEM((LEVELS, PART), F32)
+    wide = pltpu.VMEM((SRC_CELLS, PART, PART), F32)
+    narrow = pltpu.VMEM((TGT_CELLS + 1, 8, PART), F32)
+    table_dims = (STEPS, 2, PART, BATCH * PART)
+    table = [pltpu.VMEM(table_dims, F32)]
+    table_sem = [pltpu.SemaphoreType.DMA((STEPS,))]
+    t_sem = [pltpu.SemaphoreType.DMA((TGT_CELLS,))]
+    kept, row_part, first_level, live = call(
         functools.partial(first_kernel, places_s, places_t, scale),
-        (shape(PAIRS, PART, PART), sums, small, sums),
+        (shape(*table_dims), sums, small, sums),
         [SM] * 4 + [ANY] * (len(s_arrays) + len(t_arrays)),
         [
             pltpu.VMEM((SRC_CELLS * PART, WIDTH), BF16),
             pltpu.VMEM((TGT_CELLS * PART, WIDTH), BF16),
-            pltpu.SemaphoreType.DMA((SRC_CELLS,)),
-            pltpu.SemaphoreType.DMA((TGT_CELLS,)),
-        ],
-        starts,
-        targets,
+            levels,
+        ]
+        + [wide] * 4
+        + table
+        + [pltpu.SemaphoreType.DMA((SRC_CELLS,))]
+        + t_sem
+        + table_sem,
+        entries,
+        batches,
         s_order,
         t_order,
         *s_arrays,
         *t_arrays,
+        out_specs=(ANY, VM, VM, VM),
     )
     for sweep in range(ITERS):
         if sweep:
             row_part, _ = call(
                 row_kernel,
-                (sums, small),
-                [SM, SM] + [VM] * 5,
-                [],
-                starts,
-                targets,
+                (sums, shape(LEVELS, PART)),
+                [SM, SM] + [VM] * 4 + [ANY],
+                [wide] * 4 + table + table_sem,
+                entries,
+                batches,
                 joined,
                 before,
                 after,
                 first_level,
-                table,
+                kept,
             )
         col_part, src_level = call(
             column_kernel,
             (small, sums),
-            [SM, SM] + [VM] * 6,
-            [pltpu.VMEM((TGT_CELLS, 8, PART), F32), pltpu.VMEM((TGT_CELLS, 8, PART), F32)],
-            starts,
-            targets,
+            [SM, SM] + [VM] * 5 + [ANY],
+            [narrow] * 4 + [wide] + table + table_sem,
+            entries,
+            batches,
             *ring_parts(row_part, x_perm),
             live,
-            table,
+            kept,
         )
         joined = join(ring_parts(col_part, z_perm))
         before = to_group(joined[SRC_CELLS:], 1)
@@ -406,22 +526,22 @@
     blocks = call(
         functools.partial(transport_kernel, places_t),
         shape(SRC_CELLS, PART + TAIL, WIDTH, dtype=BF16),
-        [SM, SM, SM] + [VM] * 6 + [ANY] * len(t_arrays),
-        [
-            pltpu.VMEM((TGT_CELLS * PART, WIDTH), BF16),
-            pltpu.VMEM((TGT_CELLS, PART), F32),
-            pltpu.VMEM((PART, WIDTH), F32),
-            pltpu.SemaphoreType.DMA((TGT_CELLS,)),
-        ],
-        starts,
-        targets,
+        [SM] * 3 + [VM] * 5 + [ANY] * (1 + len(t_arrays)),
+        [pltpu.VMEM((TGT_CELLS * PART, WIDTH), BF16), levels, wide]
+        + [pltpu.VMEM((SRC_CELLS, PART, WIDTH), F32)] * 2
+        + [wide] * 2
+        + table
+        + t_sem
+        + table_sem,
+        entries,
+        batches,
         t_order,
         joined,
         before,
         after,
         first_level,
         src_level,
-        table,
+        kept,
         *t_arrays,
     )
     got = lax.all_to_all(blocks, "help", 0, 0)

time: 253 us -> 197 us (0.78)
  Pallas kernels: 118 us -> 61 us
    pallas_call x6, Pallas kernels: 118 us -> 61 us  [call(): pl.pallas_call(kernel, out_shape=out_shape, in_specs=in_specs, out_specs=...]
  transfers between devices with their start and end apart: 36 -> 36, of which waited for: 20 -> 24; matrix products, arithmetic and copies ran while one was open for 1% -> 1% of each run, Pallas kernels for 0% -> 0%
where the time goes in v2:
time: 197 us
  waiting for transfers between devices  70.9 us (36%)
  Pallas kernels  61 us (31%)
  starting transfers between devices  57.1 us (29%)
  other arithmetic  4.12 us (2%)
  local copies, waits for them, and re-layouts  2.12 us (1%)
    pallas_call x6, Pallas kernels, call(): pl.pallas_call(kernel, out_shape=out_shape, in_specs=in_specs, out_specs=...  61 us
    all_to_all x1, waiting for transfers between devices, shards(): got = lax.all_to_all(blocks, 'help', 0, 0)  37.6 us
    ppermute x26, starting transfers between devices, to_help(): return lax.ppermute(array, 'help', perm)  36.6 us
    ppermute x26, waiting for transfers between devices, to_help(): return lax.ppermute(array, 'help', perm)  17.8 us
    ppermute x9, waiting for transfers between devices, to_group(): lax.ppermute(array, 'src', [(i, (i + by) % count) for i in range(count)])  15.4 us
    ppermute x9, starting transfers between devices, to_group(): lax.ppermute(array, 'src', [(i, (i + by) % count) for i in range(count)])  14.7 us
    all_to_all x1, starting transfers between devices, shards(): got = lax.all_to_all(blocks, 'help', 0, 0)  5.76 us
  transfers between devices with their start and end apart: 36, of which 24 were waited for; matrix products, arithmetic and copies ran while one was open for 1% of the time, Pallas kernels for 0%

profile of v2, /device:TPU:17, one launch (start us, length us, event | category | flops | bytes accessed | tf_op | source)
XLA Modules:
  0.0 196.9 jit_solution(10768018645441227235)
XLA Ops:
  5.2 2.5 %collective-permute-start.8 = (bf16[128,512]{1,0:T(8,128)(2,1)S(1)}, bf16[128,512]{1,0:T(8,128)(2,1)S(1)}, u32[]{:S(2)}, u32[]{:S(2)}) collective-permute-start(bf16[128,512]{1,0:T(8,128)(2,1)S(1)} %get-tuple-element.27), channel_id=1, source_target_pairs={{0,2},{1,3},{2,0},{3,1},{4,6},{5,7},{6,4},{7,5},{8,10},{9,11},{10,... | collective-permute-start | bytes 393224 | tf_op jit(solution)/shard_map/ppermute | solution.py:48
  11.4 3.3 %collective-permute-start.1 = (bf16[128,512]{1,0:T(8,128)(2,1)S(1)}, bf16[128,512]{1,0:T(8,128)(2,1)S(1)}, u32[]{:S(2)}, u32[]{:S(2)}) collective-permute-start(bf16[128,512]{1,0:T(8,128)(2,1)S(1)} %get-tuple-element.31), channel_id=1, source_target_pairs={{0,8},{1,9},{2,10},{3,11},{4,12},{5,13},{6,14},{7,15},{8,0},{9,1},... | collective-permute-start | bytes 393224 | tf_op jit(solution)/shard_map/ppermute | solution.py:48
  20.8 3.9 %collective-permute-start.14 = (bf16[512,512]{1,0:T(8,128)(2,1)S(1)}, bf16[512,512]{1,0:T(8,128)(2,1)S(1)}, u32[]{:S(2)}, u32[]{:S(2)}) collective-permute-start(bf16[512,512]{1,0:T(8,128)(2,1)S(1)} %pad_maximum_fusion.1.refs_5_.refs_0_), channel_id=1, source_target_pairs={{0,112},{16,0},{32,16},{48,32},{64,48},{80,64},{96,80},{112,96},{1... | collective-permute-start | bytes 1572872 | tf_op jit(solution)/shard_map/ppermute | solution.py:44
  24.6 2.4 %collective-permute-start.4 = (bf16[512,512]{1,0:T(8,128)(2,1)S(1)}, bf16[512,512]{1,0:T(8,128)(2,1)S(1)}, u32[]{:S(2)}, u32[]{:S(2)}) collective-permute-start(bf16[512,512]{1,0:T(8,128)(2,1)S(1)} %pad_maximum_fusion.refs_0_), channel_id=1, source_target_pairs={{0,3},{1,0},{2,1},{3,2},{4,7},{5,4},{6,5},{7,6},{8,11},{9,8},{10,9... | collective-permute-start | bytes 1572872 | tf_op jit(solution)/shard_map/ppermute | solution.py:48
  27.2 4.1 %collective-permute-done.10.refs_6_.refs_1_ = bf16[512,512]{1,0:T(8,128)(2,1)S(1)} collective-permute-done((bf16[512,512]{1,0:T(8,128)(2,1)S(1)}, bf16[512,512]{1,0:T(8,128)(2,1)S(1)}, u32[]{:S(2)}, u32[]{:S(2)}) %collective-permute-start.10) | collective-permute-done | bytes 524320 | tf_op jit(solution)/shard_map/ppermute | solution.py:48
  31.4 2.7 %collective-permute-start.13 = (bf16[256,512]{1,0:T(8,128)(2,1)S(1)}, bf16[256,512]{1,0:T(8,128)(2,1)S(1)}, u32[]{:S(2)}, u32[]{:S(2)}) collective-permute-start(bf16[256,512]{1,0:T(8,128)(2,1)S(1)} %slice.63), channel_id=1, source_target_pairs={{0,12},{1,13},{2,14},{3,15},{4,0},{5,1},{6,2},{7,3},{8,4},{9,5},{1... | collective-permute-start | bytes 786440 | tf_op jit(solution)/shard_map/ppermute | solution.py:48
  35.8 2.8 %collective-permute-start.15 = (bf16[512,512]{1,0:T(8,128)(2,1)S(1)}, bf16[512,512]{1,0:T(8,128)(2,1)S(1)}, u32[]{:S(2)}, u32[]{:S(2)}) collective-permute-start(bf16[512,512]{1,0:T(8,128)(2,1)S(1)} %collective-permute-done.10.refs_6_.refs_1_), channel_id=1, source_target_pairs={{0,112},{16,0},{32,16},{48,32},{64,48},{80,64},{96,80},{112,96},{1... | collective-permute-start | bytes 1572872 | tf_op jit(solution)/shard_map/ppermute | solution.py:44
  39.2 3.5 %collective-permute-start.6 = (bf16[256,512]{1,0:T(8,128)(2,1)S(1)}, bf16[256,512]{1,0:T(8,128)(2,1)S(1)}, u32[]{:S(2)}, u32[]{:S(2)}) collective-permute-start(bf16[256,512]{1,0:T(8,128)(2,1)S(1)} %slice.61), channel_id=1, source_target_pairs={{0,3},{1,0},{2,1},{3,2},{4,7},{5,4},{6,5},{7,6},{8,11},{9,8},{10,9... | collective-permute-start | bytes 786440 | tf_op jit(solution)/shard_map/ppermute | solution.py:48
  44.5 3.9 %collective-permute-done.6.refs_4_ = bf16[256,512]{1,0:T(8,128)(2,1)S(1)} collective-permute-done((bf16[256,512]{1,0:T(8,128)(2,1)S(1)}, bf16[256,512]{1,0:T(8,128)(2,1)S(1)}, u32[]{:S(2)}, u32[]{:S(2)}) %collective-permute-start.6) | collective-permute-done | bytes 262176 | tf_op jit(solution)/shard_map/ppermute | solution.py:48
  48.4 3.6 %collective-permute-done.16.refs_12_.refs_7_ = bf16[512,512]{1,0:T(8,128)(2,1)S(1)} collective-permute-done((bf16[512,512]{1,0:T(8,128)(2,1)S(1)}, bf16[512,512]{1,0:T(8,128)(2,1)S(1)}, u32[]{:S(2)}, u32[]{:S(2)}) %collective-permute-start.16) | collective-permute-done | bytes 524320 | tf_op jit(solution)/shard_map/ppermute | solution.py:44
  52.0 2.8 %collective-permute-done.17.refs_13_.refs_8_ = bf16[256,512]{1,0:T(8,128)(2,1)S(1)} collective-permute-done((bf16[256,512]{1,0:T(8,128)(2,1)S(1)}, bf16[256,512]{1,0:T(8,128)(2,1)S(1)}, u32[]{:S(2)}, u32[]{:S(2)}) %collective-permute-start.17) | collective-permute-done | bytes 262176 | tf_op jit(solution)/shard_map/ppermute | solution.py:44
  54.8 2.8 %collective-permute-done.18.refs_14_.refs_9_ = bf16[256,512]{1,0:T(8,128)(2,1)S(1)} collective-permute-done((bf16[256,512]{1,0:T(8,128)(2,1)S(1)}, bf16[256,512]{1,0:T(8,128)(2,1)S(1)}, u32[]{:S(2)}, u32[]{:S(2)}) %collective-permute-start.18) | collective-permute-done | bytes 262176 | tf_op jit(solution)/shard_map/ppermute | solution.py:44
  57.6 23.8 %shard_map.76 = (f32[22,2,128,512]{3,2,1,0:T(8,128)}, f32[16,128]{1,0:T(8,128)S(1)}, f32[32,128]{1,0:T(8,128)S(1)}, f32[16,128]{1,0:T(8,128)S(1)}) custom-call(s32[176]{0:T(256)S(1)} %broadcast_add_fusion.entries, s32[45]{0:T(128)S(1)} %pad_add_fusion.batches, s32[16]{0:T(128)S(1)} %get-tuple-element.46.s_order, s32[16]{0:T(128)S(1)} %get-tuple-element.45.t_order, ...), custom_call_target="tpu_custom_call" | custom-call | tf_op jit(solution)/shard_map/pallas_call | solution.py:404
  81.5 3.6 %collective-permute-start.20 = (f32[16,128]{1,0:T(8,128)S(1)}, f32[16,128]{1,0:T(8,128)S(1)}, u32[]{:S(2)}, u32[]{:S(2)}) collective-permute-start(f32[16,128]{1,0:T(8,128)S(1)} %get-tuple-element.14.r0), channel_id=1, source_target_pairs={{0,2},{1,3},{2,0},{3,1},{4,6},{5,7},{6,4},{7,5},{8,10},{9,11},{10,... | collective-permute-start | bytes 24584 | tf_op jit(solution)/shard_map/ppermute | solution.py:48
  88.0 5.5 %shard_map.77 = (f32[32,128]{1,0:T(8,128)S(1)}, f32[16,128]{1,0:T(8,128)}) custom-call(s32[176]{0:T(256)S(1)} %broadcast_add_fusion.entries, s32[45]{0:T(128)S(1)} %pad_add_fusion.batches, f32[16,128]{1,0:T(8,128)S(1)} %get-tuple-element.14.r0, f32[16,128]{1,0:T(8,128)S(1)} %collective-permute-done.19.r1, f32[16,128]{1,0:T(8,128)S(1)} %collective-permute-done.20.r2, ...), custom_call_target="tpu_custom_call" | custom-call | tf_op jit(solution)/shard_map/pallas_call | solution.py:404
  94.0 2.3 %collective-permute-start.23 = (f32[32,128]{1,0:T(8,128)S(1)}, f32[32,128]{1,0:T(8,128)S(1)}, u32[]{:S(2)}, u32[]{:S(2)}) collective-permute-start(f32[32,128]{1,0:T(8,128)S(1)} %get-tuple-element.17), channel_id=1, source_target_pairs={{0,8},{1,9},{2,10},{3,11},{4,12},{5,13},{6,14},{7,15},{8,0},{9,1},... | collective-permute-start | bytes 49160 | tf_op jit(solution)/shard_map/ppermute | solution.py:48
  99.3 2.6 %collective-permute-start.25 = (f32[16,128]{1,0:T(8,128)S(1)}, f32[16,128]{1,0:T(8,128)S(1)}, u32[]{:S(2)}, u32[]{:S(2)}) collective-permute-start(f32[16,128]{1,0:T(8,128)S(1)} %get-tuple-element.36), channel_id=1, source_target_pairs={{0,16},{16,32},{32,48},{48,64},{64,80},{80,96},{96,112},{112,0},{1... | collective-permute-start | bytes 24584 | tf_op jit(solution)/shard_map/ppermute | solution.py:44
  102.7 2.3 %collective-permute-done.26.after = f32[16,128]{1,0:T(8,128)S(1)} collective-permute-done((f32[16,128]{1,0:T(8,128)S(1)}, f32[16,128]{1,0:T(8,128)S(1)}, u32[]{:S(2)}, u32[]{:S(2)}) %collective-permute-start.26) | collective-permute-done | bytes 8224 | tf_op jit(solution)/shard_map/ppermute | solution.py:44
  105.0 6.2 %shard_map.78 = (f32[16,128]{1,0:T(8,128)S(1)}, f32[40,128]{1,0:T(8,128)}) custom-call(s32[176]{0:T(256)S(1)} %broadcast_add_fusion.entries, s32[45]{0:T(128)S(1)} %pad_add_fusion.batches, f32[32,128]{1,0:T(8,128)S(1)} %multiply_add_fusion.1.joined, f32[16,128]{1,0:T(8,128)S(1)} %collective-permute-done.25.before, ...), custom_call_target="tpu_custom_call" | custom-call | tf_op jit(solution)/shard_map/pallas_call | solution.py:404
  115.9 5.0 %shard_map.79 = (f32[32,128]{1,0:T(8,128)S(1)}, f32[16,128]{1,0:T(8,128)S(1)}) custom-call(s32[176]{0:T(256)S(1)} %broadcast_add_fusion.entries, s32[45]{0:T(128)S(1)} %pad_add_fusion.batches, f32[16,128]{1,0:T(8,128)S(1)} %get-tuple-element.19.r0, f32[16,128]{1,0:T(8,128)S(1)} %collective-permute-done.27.r1, f32[16,128]{1,0:T(8,128)S(1)} %collective-permute-done.28.r2, ...), custom_call_target="tpu_custom_call" | custom-call | tf_op jit(solution)/shard_map/pallas_call | solution.py:404
  126.4 3.2 %collective-permute-start.33 = (f32[16,128]{1,0:T(8,128)S(1)}, f32[16,128]{1,0:T(8,128)S(1)}, u32[]{:S(2)}, u32[]{:S(2)}) collective-permute-start(f32[16,128]{1,0:T(8,128)S(1)} %get-tuple-element.34), channel_id=1, source_target_pairs={{0,16},{16,32},{32,48},{48,64},{64,80},{80,96},{96,112},{112,0},{1... | collective-permute-start | bytes 24584 | tf_op jit(solution)/shard_map/ppermute | solution.py:44
  132.6 18.6 %shard_map.80 = bf16[16,144,512]{2,1,0:T(8,128)(2,1)} custom-call(s32[176]{0:T(256)S(1)} %broadcast_add_fusion.entries, s32[45]{0:T(128)S(1)} %pad_add_fusion.batches, s32[16]{0:T(128)S(1)} %get-tuple-element.45.t_order, f32[32,128]{1,0:T(8,128)S(1)} %multiply_add_fusion.joined, f32[16,128]{1,0:T(8,128)S(1)} %collective-permute-done.33.before, ...), custom_call_target="tpu_custom_call" | custom-call | tf_op jit(solution)/shard_map/pallas_call | solution.py:404
  151.2 5.8 %all-to-all-start = ((bf16[16,144,512]{2,1,0:T(8,128)(2,1)}), bf16[16,144,512]{2,1,0:T(8,128)(2,1)S(1)}, u32[]{:S(2)}, u32[]{:S(2)}) async-start(bf16[16,144,512]{2,1,0:T(8,128)(2,1)} %shard_map.80), calls=%async_computation | async-start | bytes 4718592 | tf_op jit(solution)/shard_map/all_to_all | solution.py:547
  157.4 37.6 %all-to-all-done.got = bf16[16,144,512]{2,1,0:T(8,128)(2,1)S(1)} async-done(((bf16[16,144,512]{2,1,0:T(8,128)(2,1)}), bf16[16,144,512]{2,1,0:T(8,128)(2,1)S(1)}, u32[]{:S(2)}, u32[]{:S(2)}) %all-to-all-start) | async-done | bytes 2359328 | tf_op jit(solution)/shard_map/all_to_all | solution.py:547
  (108 shorter events, 40.5 us)
Async XLA Ops:
  4.0 11.3 %collective-permute-start.7 = (bf16[128,512]{1,0:T(8,128)(2,1)S(1)}, bf16[128,512]{1,0:T(8,128)(2,1)S(1)}, u32[]{:S(2)}, u32[]{:S(2)}) collective-permute-start(bf16[128,512]{1,0:T(8,128)(2,1)S(1)} %get-tuple-element.28), channel_id=1, source_target_pairs={{0,1},{1,2},{2,3},{3,0},{4,5},{5,6},{6,7},{7,4},{8,9},{9,10},{10,1... | collective-permute-start | bytes 393224 | tf_op jit(solution)/shard_map/ppermute | solution.py:48
  5.2 11.0 %collective-permute-start.8 = (bf16[128,512]{1,0:T(8,128)(2,1)S(1)}, bf16[128,512]{1,0:T(8,128)(2,1)S(1)}, u32[]{:S(2)}, u32[]{:S(2)}) collective-permute-start(bf16[128,512]{1,0:T(8,128)(2,1)S(1)} %get-tuple-element.27), channel_id=1, source_target_pairs={{0,2},{1,3},{2,0},{3,1},{4,6},{5,7},{6,4},{7,5},{8,10},{9,11},{10,... | collective-permute-start | bytes 393224 | tf_op jit(solution)/shard_map/ppermute | solution.py:48
  7.7 8.6 %collective-permute-start.9 = (bf16[128,512]{1,0:T(8,128)(2,1)S(1)}, bf16[128,512]{1,0:T(8,128)(2,1)S(1)}, u32[]{:S(2)}, u32[]{:S(2)}) collective-permute-start(bf16[128,512]{1,0:T(8,128)(2,1)S(1)} %get-tuple-element.26), channel_id=1, source_target_pairs={{0,3},{1,0},{2,1},{3,2},{4,7},{5,4},{6,5},{7,6},{8,11},{9,8},{10,9... | collective-permute-start | bytes 393224 | tf_op jit(solution)/shard_map/ppermute | solution.py:48
  9.7 9.3 %collective-permute-start = (bf16[128,512]{1,0:T(8,128)(2,1)S(1)}, bf16[128,512]{1,0:T(8,128)(2,1)S(1)}, u32[]{:S(2)}, u32[]{:S(2)}) collective-permute-start(bf16[128,512]{1,0:T(8,128)(2,1)S(1)} %get-tuple-element.32), channel_id=1, source_target_pairs={{0,4},{1,5},{2,6},{3,7},{4,8},{5,9},{6,10},{7,11},{8,12},{9,13},{1... | collective-permute-start | bytes 393224 | tf_op jit(solution)/shard_map/ppermute | solution.py:48
  11.4 7.8 %collective-permute-start.1 = (bf16[128,512]{1,0:T(8,128)(2,1)S(1)}, bf16[128,512]{1,0:T(8,128)(2,1)S(1)}, u32[]{:S(2)}, u32[]{:S(2)}) collective-permute-start(bf16[128,512]{1,0:T(8,128)(2,1)S(1)} %get-tuple-element.31), channel_id=1, source_target_pairs={{0,8},{1,9},{2,10},{3,11},{4,12},{5,13},{6,14},{7,15},{8,0},{9,1},... | collective-permute-start | bytes 393224 | tf_op jit(solution)/shard_map/ppermute | solution.py:48
  15.3 4.7 %collective-permute-start.2 = (bf16[128,512]{1,0:T(8,128)(2,1)S(1)}, bf16[128,512]{1,0:T(8,128)(2,1)S(1)}, u32[]{:S(2)}, u32[]{:S(2)}) collective-permute-start(bf16[128,512]{1,0:T(8,128)(2,1)S(1)} %get-tuple-element.30), channel_id=1, source_target_pairs={{0,12},{1,13},{2,14},{3,15},{4,0},{5,1},{6,2},{7,3},{8,4},{9,5},{1... | collective-permute-start | bytes 393224 | tf_op jit(solution)/shard_map/ppermute | solution.py:48
  16.3 15.0 %collective-permute-start.10 = (bf16[512,512]{1,0:T(8,128)(2,1)S(1)}, bf16[512,512]{1,0:T(8,128)(2,1)S(1)}, u32[]{:S(2)}, u32[]{:S(2)}) collective-permute-start(bf16[512,512]{1,0:T(8,128)(2,1)S(1)} %pad_maximum_fusion.1.refs_5_.refs_0_), channel_id=1, source_target_pairs={{0,4},{1,5},{2,6},{3,7},{4,8},{5,9},{6,10},{7,11},{8,12},{9,13},{1... | collective-permute-start | bytes 1572872 | tf_op jit(solution)/shard_map/ppermute | solution.py:48
  17.1 14.3 %collective-permute-start.11 = (bf16[512,512]{1,0:T(8,128)(2,1)S(1)}, bf16[512,512]{1,0:T(8,128)(2,1)S(1)}, u32[]{:S(2)}, u32[]{:S(2)}) collective-permute-start(bf16[512,512]{1,0:T(8,128)(2,1)S(1)} %pad_maximum_fusion.1.refs_5_.refs_0_), channel_id=1, source_target_pairs={{0,12},{1,13},{2,14},{3,15},{4,0},{5,1},{6,2},{7,3},{8,4},{9,5},{1... | collective-permute-start | bytes 1572872 | tf_op jit(solution)/shard_map/ppermute | solution.py:48
  20.0 14.1 %collective-permute-start.3 = (bf16[512,512]{1,0:T(8,128)(2,1)S(1)}, bf16[512,512]{1,0:T(8,128)(2,1)S(1)}, u32[]{:S(2)}, u32[]{:S(2)}) collective-permute-start(bf16[512,512]{1,0:T(8,128)(2,1)S(1)} %pad_maximum_fusion.refs_0_), channel_id=1, source_target_pairs={{0,1},{1,2},{2,3},{3,0},{4,5},{5,6},{6,7},{7,4},{8,9},{9,10},{10,1... | collective-permute-start | bytes 1572872 | tf_op jit(solution)/shard_map/ppermute | solution.py:48
  20.8 15.0 %collective-permute-start.14 = (bf16[512,512]{1,0:T(8,128)(2,1)S(1)}, bf16[512,512]{1,0:T(8,128)(2,1)S(1)}, u32[]{:S(2)}, u32[]{:S(2)}) collective-permute-start(bf16[512,512]{1,0:T(8,128)(2,1)S(1)} %pad_maximum_fusion.1.refs_5_.refs_0_), channel_id=1, source_target_pairs={{0,112},{16,0},{32,16},{48,32},{64,48},{80,64},{96,80},{112,96},{1... | collective-permute-start | bytes 1572872 | tf_op jit(solution)/shard_map/ppermute | solution.py:44
  24.6 14.0 %collective-permute-start.4 = (bf16[512,512]{1,0:T(8,128)(2,1)S(1)}, bf16[512,512]{1,0:T(8,128)(2,1)S(1)}, u32[]{:S(2)}, u32[]{:S(2)}) collective-permute-start(bf16[512,512]{1,0:T(8,128)(2,1)S(1)} %pad_maximum_fusion.refs_0_), channel_id=1, source_target_pairs={{0,3},{1,0},{2,1},{3,2},{4,7},{5,4},{6,5},{7,6},{8,11},{9,8},{10,9... | collective-permute-start | bytes 1572872 | tf_op jit(solution)/shard_map/ppermute | solution.py:48
  31.3 7.9 %collective-permute-start.12 = (bf16[256,512]{1,0:T(8,128)(2,1)S(1)}, bf16[256,512]{1,0:T(8,128)(2,1)S(1)}, u32[]{:S(2)}, u32[]{:S(2)}) collective-permute-start(bf16[256,512]{1,0:T(8,128)(2,1)S(1)} %slice.62), channel_id=1, source_target_pairs={{0,4},{1,5},{2,6},{3,7},{4,8},{5,9},{6,10},{7,11},{8,12},{9,13},{1... | collective-permute-start | bytes 786440 | tf_op jit(solution)/shard_map/ppermute | solution.py:48
  31.4 11.2 %collective-permute-start.13 = (bf16[256,512]{1,0:T(8,128)(2,1)S(1)}, bf16[256,512]{1,0:T(8,128)(2,1)S(1)}, u32[]{:S(2)}, u32[]{:S(2)}) collective-permute-start(bf16[256,512]{1,0:T(8,128)(2,1)S(1)} %slice.63), channel_id=1, source_target_pairs={{0,12},{1,13},{2,14},{3,15},{4,0},{5,1},{6,2},{7,3},{8,4},{9,5},{1... | collective-permute-start | bytes 786440 | tf_op jit(solution)/shard_map/ppermute | solution.py:48
  34.2 8.8 %collective-permute-start.5 = (bf16[256,512]{1,0:T(8,128)(2,1)S(1)}, bf16[256,512]{1,0:T(8,128)(2,1)S(1)}, u32[]{:S(2)}, u32[]{:S(2)}) collective-permute-start(bf16[256,512]{1,0:T(8,128)(2,1)S(1)} %slice.60), channel_id=1, source_target_pairs={{0,1},{1,2},{2,3},{3,0},{4,5},{5,6},{6,7},{7,4},{8,9},{9,10},{10,1... | collective-permute-start | bytes 786440 | tf_op jit(solution)/shard_map/ppermute | solution.py:48
  35.8 12.6 %collective-permute-start.15 = (bf16[512,512]{1,0:T(8,128)(2,1)S(1)}, bf16[512,512]{1,0:T(8,128)(2,1)S(1)}, u32[]{:S(2)}, u32[]{:S(2)}) collective-permute-start(bf16[512,512]{1,0:T(8,128)(2,1)S(1)} %collective-permute-done.10.refs_6_.refs_1_), channel_id=1, source_target_pairs={{0,112},{16,0},{32,16},{48,32},{64,48},{80,64},{96,80},{112,96},{1... | collective-permute-start | bytes 1572872 | tf_op jit(solution)/shard_map/ppermute | solution.py:44
  38.6 13.4 %collective-permute-start.16 = (bf16[512,512]{1,0:T(8,128)(2,1)S(1)}, bf16[512,512]{1,0:T(8,128)(2,1)S(1)}, u32[]{:S(2)}, u32[]{:S(2)}) collective-permute-start(bf16[512,512]{1,0:T(8,128)(2,1)S(1)} %collective-permute-done.11.refs_7_.refs_2_), channel_id=1, source_target_pairs={{0,112},{16,0},{32,16},{48,32},{64,48},{80,64},{96,80},{112,96},{1... | collective-permute-start | bytes 1572872 | tf_op jit(solution)/shard_map/ppermute | solution.py:44
  39.2 9.2 %collective-permute-start.6 = (bf16[256,512]{1,0:T(8,128)(2,1)S(1)}, bf16[256,512]{1,0:T(8,128)(2,1)S(1)}, u32[]{:S(2)}, u32[]{:S(2)}) collective-permute-start(bf16[256,512]{1,0:T(8,128)(2,1)S(1)} %slice.61), channel_id=1, source_target_pairs={{0,3},{1,0},{2,1},{3,2},{4,7},{5,4},{6,5},{7,6},{8,11},{9,8},{10,9... | collective-permute-start | bytes 786440 | tf_op jit(solution)/shard_map/ppermute | solution.py:48
  42.7 12.2 %collective-permute-start.17 = (bf16[256,512]{1,0:T(8,128)(2,1)S(1)}, bf16[256,512]{1,0:T(8,128)(2,1)S(1)}, u32[]{:S(2)}, u32[]{:S(2)}) collective-permute-start(bf16[256,512]{1,0:T(8,128)(2,1)S(1)} %collective-permute-done.12.refs_8_.refs_3_), channel_id=1, source_target_pairs={{0,112},{16,0},{32,16},{48,32},{64,48},{80,64},{96,80},{112,96},{1... | collective-permute-start | bytes 786440 | tf_op jit(solution)/shard_map/ppermute | solution.py:44
  43.0 14.7 %collective-permute-start.18 = (bf16[256,512]{1,0:T(8,128)(2,1)S(1)}, bf16[256,512]{1,0:T(8,128)(2,1)S(1)}, u32[]{:S(2)}, u32[]{:S(2)}) collective-permute-start(bf16[256,512]{1,0:T(8,128)(2,1)S(1)} %collective-permute-done.13.refs_9_.refs_4_), channel_id=1, source_target_pairs={{0,112},{16,0},{32,16},{48,32},{64,48},{80,64},{96,80},{112,96},{1... | collective-permute-start | bytes 786440 | tf_op jit(solution)/shard_map/ppermute | solution.py:44
  81.5 4.7 %collective-permute-start.20 = (f32[16,128]{1,0:T(8,128)S(1)}, f32[16,128]{1,0:T(8,128)S(1)}, u32[]{:S(2)}, u32[]{:S(2)}) collective-permute-start(f32[16,128]{1,0:T(8,128)S(1)} %get-tuple-element.14.r0), channel_id=1, source_target_pairs={{0,2},{1,3},{2,0},{3,1},{4,6},{5,7},{6,4},{7,5},{8,10},{9,11},{10,... | collective-permute-start | bytes 24584 | tf_op jit(solution)/shard_map/ppermute | solution.py:48
  94.0 4.1 %collective-permute-start.23 = (f32[32,128]{1,0:T(8,128)S(1)}, f32[32,128]{1,0:T(8,128)S(1)}, u32[]{:S(2)}, u32[]{:S(2)}) collective-permute-start(f32[32,128]{1,0:T(8,128)S(1)} %get-tuple-element.17), channel_id=1, source_target_pairs={{0,8},{1,9},{2,10},{3,11},{4,12},{5,13},{6,14},{7,15},{8,0},{9,1},... | collective-permute-start | bytes 49160 | tf_op jit(solution)/shard_map/ppermute | solution.py:48
  111.3 4.3 %collective-permute-start.28 = (f32[16,128]{1,0:T(8,128)S(1)}, f32[16,128]{1,0:T(8,128)S(1)}, u32[]{:S(2)}, u32[]{:S(2)}) collective-permute-start(f32[16,128]{1,0:T(8,128)S(1)} %get-tuple-element.19.r0), channel_id=1, source_target_pairs={{0,2},{1,3},{2,0},{3,1},{4,6},{5,7},{6,4},{7,5},{8,10},{9,11},{10,... | collective-permute-start | bytes 24584 | tf_op jit(solution)/shard_map/ppermute | solution.py:48
  121.5 4.1 %collective-permute-start.31 = (f32[32,128]{1,0:T(8,128)S(1)}, f32[32,128]{1,0:T(8,128)S(1)}, u32[]{:S(2)}, u32[]{:S(2)}) collective-permute-start(f32[32,128]{1,0:T(8,128)S(1)} %get-tuple-element.20), channel_id=1, source_target_pairs={{0,8},{1,9},{2,10},{3,11},{4,12},{5,13},{6,14},{7,15},{8,0},{9,1},... | collective-permute-start | bytes 49160 | tf_op jit(solution)/shard_map/ppermute | solution.py:48
  151.2 43.8 %all-to-all-start = ((bf16[16,144,512]{2,1,0:T(8,128)(2,1)}), bf16[16,144,512]{2,1,0:T(8,128)(2,1)S(1)}, u32[]{:S(2)}, u32[]{:S(2)}) async-start(bf16[16,144,512]{2,1,0:T(8,128)(2,1)} %shard_map.80), calls=%async_computation | async-start | bytes 4718592 | tf_op jit(solution)/shard_map/all_to_all | solution.py:547
  (19 other events, 154.0 us)

commit v3 on v2

v3 whole, which is shorter than its diff:
```python
import functools
import math

import jax
import jax.numpy as jnp
from jax import lax
from jax.experimental import pallas as pl
from jax.experimental.pallas import tpu as pltpu
from jax.sharding import PartitionSpec as P

ITERS = 2
EPSILON = 0.2
LOG2E = 1.0 / math.log(2.0)
DEAD = -1e30
EMPTY = -2e30
MARK = 1024.0
SIDE = 4
PART = 128
WIDTH = 512
SRC_CELLS = 16
TGT_CELLS = 8
TILES = WIDTH // PART
LEVELS = TGT_CELLS * TILES
TAIL = 16
PAIRS = 128
STEPS = PAIRS // 2
RING = 20
NOBODY = TGT_CELLS
F32 = jnp.float32
BF16 = jnp.bfloat16
VMEM_LIMIT = 40 * 1024 * 1024


def x_perm(by):
    return [(z * SIDE + x, z * SIDE + (x + by) % SIDE) for z in range(SIDE) for x in range(SIDE)]


def z_perm(by):
    return [(z * SIDE + x, (z + by) % SIDE * SIDE + x) for z in range(SIDE) for x in range(SIDE)]


def to_group(array, by):
    count = lax.axis_size("src")
    return lax.ppermute(array, "src", [(i, (i + by) % count) for i in range(count)])


def to_help(array, perm):
    return lax.ppermute(array, "help", perm)


def lookup(cell_ids, slot_table):
    matches = cell_ids[:, None] == jnp.arange(slot_table.shape[0], dtype=jnp.int32)[None, :]
    return jnp.sum(jnp.where(matches, slot_table[None, :], 0), axis=1)


def spread(points, perm, me):
    parts = [lax.dynamic_slice_in_dim(points, me * PART, PART, 0)]
    for by in range(1, SIDE):
        other = (me + by) % SIDE
        parts.append(to_help(lax.dynamic_slice_in_dim(points, other * PART, PART, 0), perm(by)))
    return jnp.concatenate(parts, axis=0)


def collect(block, perm):
    rows = block.shape[0]
    half = rows // 2
    behind = to_help(block, perm(1))
    ahead = to_help(block, perm(SIDE - 1))
    far_low = to_help(behind[:half], perm(1))
    far_high = to_help(ahead[half:], perm(SIDE - 1))
    return [
        (0, rows, block),
        (rows, rows, behind),
        (3 * rows, rows, ahead),
        (2 * rows, half, far_low),
        (2 * rows + half, half, far_high),
    ]


def ring_parts(array, perm):
    return [array] + [to_help(array, perm(by)) for by in range(1, SIDE)]


def join(parts):
    top = functools.reduce(jnp.maximum, parts)
    total = functools.reduce(jnp.add, [jnp.exp2(part - top) for part in parts])
    return top + jnp.log2(total)


def eye():
    return lax.broadcasted_iota(jnp.int32, (PART, PART), 0) == lax.broadcasted_iota(
        jnp.int32, (PART, PART), 1
    )


def to_lanes(column):
    return jnp.sum(jnp.where(eye(), jnp.broadcast_to(column, (PART, PART)), 0.0), axis=0, keepdims=True)


def to_rows(lane_vector):
    return jnp.transpose(jnp.broadcast_to(lane_vector, (PART, PART)))


def part_of(index):
    return pl.ds(pl.multiple_of(index * PART, PART), PART)


def load_sources(refs, places, order, target, sem):
    copies = []
    for (start, rows), ref in zip(places, refs):
        for cell in range(rows // PART):
            copies.append(
                pltpu.make_async_copy(
                    ref.at[pl.ds(cell * PART, PART)],
                    target.at[part_of(order[start // PART + cell])],
                    sem.at[len(copies)],
                )
            )
    return copies


def load_targets(refs, places, order, target, sem):
    copies = []
    for (start, rows), ref in zip(places, refs):
        side, place = start // WIDTH // SIDE, start // WIDTH % SIDE
        first = (side * SIDE + order[place]) * WIDTH + start % WIDTH
        goal = target.at[pl.ds(pl.multiple_of(first, PART), rows)]
        copies.append(pltpu.make_async_copy(ref, goal, sem.at[len(copies)]))
    return copies


def tile(k):
    return slice(k * PART, (k + 1) * PART)


def cell_rows(t):
    return pl.ds(pl.multiple_of(lax.rem(t, NOBODY) * WIDTH, WIDTH), WIDTH)


def pair(lists, i, half):
    place = 2 * i + half
    return lists[1 + place], lists[1 + PAIRS + place]


def level_rows(level_ref, t):
    return [level_ref[pl.ds(t * TILES + k, 1), :] for k in range(TILES)]


def row_stats(scores, s, tops, totals):
    old = tops[s]
    top = functools.reduce(jnp.maximum, scores, old)
    total = functools.reduce(jnp.add, [jnp.exp2(one - top) for one in scores])
    totals[s] = totals[s] * jnp.exp2(old - top) + total
    tops[s] = top


def clear_stats(tops, totals):
    for one in tops:
        one[...] = jnp.full(one.shape, EMPTY, F32)
    for one in totals:
        one[...] = jnp.ones(one.shape, F32)


def store_row_sums(tops, totals, sums_ref):
    def cell(s, carry):
        top = jnp.max(jnp.maximum(tops[0][s], tops[1][s]), axis=1, keepdims=True)
        total = totals[0][s] * jnp.exp2(tops[0][s] - top) + totals[1][s] * jnp.exp2(tops[1][s] - top)
        total = jnp.sum(total, axis=1, keepdims=True)
        sums_ref[pl.ds(s, 1), :] = to_lanes(top + jnp.log2(total))
        return carry

    lax.fori_loop(0, SRC_CELLS, cell, 0, unroll=4)


def table_copy(kept, ring, sem, step, out=False):
    slot = lax.rem(step, RING)
    ends = (ring.at[slot], kept.at[step])
    return pltpu.make_async_copy(*(ends if out else ends[::-1]), sem.at[slot])


def stream_start(kept, ring, sem, steps):
    for step in range(RING - 1):

        @pl.when(step < steps)
        def _():
            table_copy(kept, ring, sem, step).start()


def stream_step(kept, ring, sem, step, steps):
    table_copy(kept, ring, sem, step).wait()
    ahead = step + RING - 1

    @pl.when(ahead < steps)
    def _():
        table_copy(kept, ring, sem, ahead).start()

    return ring.at[lax.rem(step, RING)]


def first_kernel(places_s, places_t, scale, lists, s_order, t_order, arrived, *refs):
    ns, nt = len(places_s), len(places_t)
    s_refs, t_refs = refs[:ns], refs[ns : ns + nt]
    kept, sums_ref, first_ref, live_ref = refs[ns + nt : ns + nt + 4]
    xs, ys, level_ref, top0, top1, total0, total1, ring, s_sem, t_sem, sem = refs[ns + nt + 4 :]
    tops, totals = (top0, top1), (total0, total1)
    copies = load_targets(t_refs, places_t, t_order, ys, t_sem)
    copies += load_sources(s_refs, places_s, s_order, xs, s_sem)
    for copy in copies:
        copy.start()
    steps = lists[0]
    clear_stats(tops, totals)
    level_ref[LEVELS:, :] = jnp.full((8, PART), DEAD, F32)
    for place in range(TGT_CELLS):
        t = place // SIDE * SIDE + t_order[place % SIDE]
        for k in range(TILES):
            row = place * TILES + k
            level_ref[pl.ds(t * TILES + k, 1), :] = arrived[row : row + 1, :]
    first_ref[...] = level_ref[:LEVELS, :]
    for copy in copies:
        copy.wait()

    def source_cell(s, carry):
        mark = xs[part_of(s), :PART].astype(F32)
        dead = jnp.where(eye() & (mark > 0.5 * MARK), DEAD, 0.0)
        live_ref[pl.ds(s, 1), :] = jnp.sum(dead, axis=0, keepdims=True)
        return carry

    lax.fori_loop(0, SRC_CELLS, source_cell, 0, unroll=4)

    def step(i, carry):
        @pl.when(i >= RING)
        def _():
            table_copy(kept, ring, sem, i - RING, out=True).wait()

        slot = lax.rem(i, RING)
        for half in range(2):
            s, t = pair(lists, i, half)
            inner = lax.dot_general(
                xs[part_of(s), :], ys[cell_rows(t), :], (((1,), (1,)), ((), ())), preferred_element_type=F32
            )
            inner = inner * scale
            ring[slot, half] = inner
            scores = [inner[:, tile(k)] + level for k, level in enumerate(level_rows(level_ref, t))]
            row_stats(scores, s, tops[half], totals[half])
        table_copy(kept, ring, sem, i, out=True).start()
        return carry

    lax.fori_loop(0, steps, step, 0)
    store_row_sums(tops, totals, sums_ref)

    def settle(i, carry):
        table_copy(kept, ring, sem, i, out=True).wait()
        return carry

    lax.fori_loop(jnp.maximum(steps - RING, 0), steps, settle, 0)


def source_levels(parts, live):
    return jnp.where(live < 0.5 * DEAD, DEAD, -join([part[...] for part in parts]))


def spread_rows(level_ref, wide_ref):
    def cell(s, carry):
        wide_ref[s] = to_rows(level_ref[pl.ds(s, 1), :])
        return carry

    lax.fori_loop(0, SRC_CELLS, cell, 0, unroll=4)


def column_kernel(
    lists, r0, r1, r2, r3, live_ref, kept, sums_ref, level_ref, top0, top1, total0, total1, wide_ref, ring, sem
):
    tops, totals = (top0, top1), (total0, total1)
    steps = lists[0]
    stream_start(kept, ring, sem, steps)
    level_ref[...] = source_levels((r0, r1, r2, r3), live_ref[...])
    spread_rows(level_ref, wide_ref)
    clear_stats(tops, totals)

    def step(i, carry):
        table = stream_step(kept, ring, sem, i, steps)
        for half in range(2):
            s, t = pair(lists, i, half)
            level = wide_ref[s]
            old_tops, old_totals = tops[half][t], totals[half][t]
            for k in range(TILES):
                scores = (table[half, :, tile(k)] + level).reshape(PART // 8, 8, PART)
                top = jnp.maximum(old_tops[k], jnp.max(scores, axis=0))
                total = jnp.sum(jnp.exp2(scores - top[None]), axis=0)
                tops[half][t, k] = top
                totals[half][t, k] = old_totals[k] * jnp.exp2(old_tops[k] - top) + total
        return carry

    lax.fori_loop(0, steps, step, 0)
    tops = [one[:TGT_CELLS].reshape(LEVELS, 8, PART) for one in tops]
    totals = [one[:TGT_CELLS].reshape(LEVELS, 8, PART) for one in totals]
    top = jnp.max(jnp.maximum(*tops), axis=1)
    total = sum(part * jnp.exp2(one - top[:, None, :]) for one, part in zip(tops, totals))
    sums_ref[...] = top + jnp.log2(jnp.sum(total, axis=1))


def target_levels(joined, before, after, first_level, level_ref):
    own = -join([joined[: LEVELS // 2, :], before[...]])
    following = -join([joined[LEVELS // 2 :, :], after[...]])
    levels = jnp.concatenate([own, following], axis=0)
    level_ref[:LEVELS, :] = jnp.where(first_level[...] < 0.5 * DEAD, DEAD, levels)
    level_ref[LEVELS:, :] = jnp.full((8, PART), DEAD, F32)


def row_kernel(
    lists, joined, before, after, first_level, kept, sums_ref, level_ref, top0, top1, total0, total1, ring, sem
):
    tops, totals = (top0, top1), (total0, total1)
    steps = lists[0]
    stream_start(kept, ring, sem, steps)
    target_levels(joined, before, after, first_level, level_ref)
    clear_stats(tops, totals)

    def step(i, carry):
        table = stream_step(kept, ring, sem, i, steps)
        for half in range(2):
            s, t = pair(lists, i, half)
            scores = [table[half, :, tile(k)] + level for k, level in enumerate(level_rows(level_ref, t))]
            row_stats(scores, s, tops[half], totals[half])
        return carry

    lax.fori_loop(0, steps, step, 0)
    store_row_sums(tops, totals, sums_ref)


def pieces(value, count):
    found = []
    for _ in range(count):
        piece = value.astype(BF16).astype(F32)
        found.append(piece)
        value = value - piece
    return found


def transport_kernel(
    places_t, lists, t_order, joined, before, after, first_level, src_level, kept, *refs
):
    nt = len(places_t)
    t_refs = refs[:nt]
    out_ref, own_ref, ys, level_ref, wide_ref, map0, map1, mass0, mass1, ring, t_sem, sem = refs[nt:]
    maps, masses = (map0, map1), (mass0, mass1)
    steps = lists[0]
    copies = load_targets(t_refs, places_t, t_order, ys, t_sem)
    for copy in copies:
        copy.start()
    stream_start(kept, ring, sem, steps)
    target_levels(joined, before, after, first_level, level_ref)
    spread_rows(src_level, wide_ref)
    for one in maps + masses:
        one[...] = jnp.zeros(one.shape, F32)
    for k, level in enumerate(level_rows(level_ref, t_order[0])):
        own_ref[k : k + 1, :] = level
    for copy in copies:
        copy.wait()

    def step(i, carry):
        table = stream_step(kept, ring, sem, i, steps)
        for half in range(2):
            s, t = pair(lists, i, half)
            level = wide_ref[s]
            weights = [
                jnp.exp2(table[half, :, tile(k)] + one + level).astype(BF16)
                for k, one in enumerate(level_rows(level_ref, t))
            ]
            maps[half][s] += jnp.dot(
                jnp.concatenate(weights, axis=1), ys[cell_rows(t), :], preferred_element_type=F32
            )
            masses[half][s] += functools.reduce(jnp.add, [one.astype(F32) for one in weights])
        return carry

    lax.fori_loop(0, steps, step, 0)
    rows = lax.broadcasted_iota(jnp.int32, (TAIL, WIDTH), 0)

    def cell(s, carry):
        mass = to_lanes(jnp.sum(mass0[s] + mass1[s], axis=1, keepdims=True))
        out_ref[s, :PART, :] = (map0[s] + map1[s]).astype(BF16)
        parts = pieces(mass, 2) + pieces(src_level[pl.ds(s, 1), :], 3)
        last = jnp.concatenate([parts[4]] * SIDE, axis=1)
        tail = jnp.where(rows == 0, jnp.concatenate(parts[:4], axis=1), jnp.where(rows == 1, last, 0.0))
        out_ref[s, PART:, :] = tail.astype(BF16)
        return carry

    lax.fori_loop(0, SRC_CELLS, cell, 0, unroll=2)


def finish_kernel(counts, got, own_level, half_src, half_tgt, src_ref, tgt_ref, map_ref):
    def tail(sender):
        return got[sender, PART:, :].astype(F32)

    def segment(rows, index):
        return rows[index // SIDE : index // SIDE + 1, index % SIDE * PART : (index % SIDE + 1) * PART]

    lanes = lax.broadcasted_iota(jnp.int32, (1, PART), 1)
    rows = lax.broadcasted_iota(jnp.int32, (PART, 1), 0)
    src_live, tgt_live = counts[0, 0], counts[0, 1]
    for q in range(SIDE):
        tails = [tail(q * SIDE + x) for x in range(SIDE)]
        weight_sum = sum(segment(one, 0) + segment(one, 1) for one in tails)
        live = rows + q * PART < src_live
        inverse = jnp.where(live, 1.0 / to_rows(weight_sum), 0.0)
        for chunk in range(WIDTH // PART):
            columns = slice(chunk * PART, (chunk + 1) * PART)
            numerator = sum(got[q * SIDE + x, :PART, columns].astype(F32) for x in range(SIDE))
            map_ref[q * PART : (q + 1) * PART, columns] = jnp.where(live, numerator * inverse, 0.0)
        level = segment(tails[0], 2) + segment(tails[0], 3) + segment(tails[0], 4)
        value = (level + half_src[q : q + 1, :]) * (EPSILON / LOG2E)
        src_ref[q : q + 1, :] = jnp.where(lanes + q * PART < src_live, value, 0.0)
        value = (own_level[q : q + 1, :] + half_tgt[q : q + 1, :]) * (EPSILON / LOG2E)
        tgt_ref[q : q + 1, :] = jnp.where(lanes + q * PART < tgt_live, value, 0.0)


VM = pl.BlockSpec(memory_space=pltpu.VMEM)
SM = pl.BlockSpec(memory_space=pltpu.SMEM)
ANY = pl.BlockSpec(memory_space=pl.ANY)


def call(kernel, out_shape, in_specs, scratch, *args, out_specs=None):
    outs = jax.tree.map(lambda _: VM, out_shape) if out_specs is None else out_specs
    return pl.pallas_call(
        kernel,
        out_shape=out_shape,
        in_specs=in_specs,
        out_specs=outs,
        scratch_shapes=scratch,
        compiler_params=pltpu.CompilerParams(vmem_limit_bytes=VMEM_LIMIT),
    )(*args)


def shape(*dims, dtype=F32):
    return jax.ShapeDtypeStruct(dims, dtype)


def half_norms(points, scale):
    return (0.5 * scale) * jnp.sum(jnp.square(points.astype(F32)), axis=1)


def shards(tiles, cell_slot, counts, src_points, tgt_points):
    help_index = lax.axis_index("help")
    src_index = lax.axis_index("src")
    z, x = help_index // SIDE, help_index % SIDE
    scale = LOG2E / (math.sqrt(WIDTH) * EPSILON)

    positions = jnp.arange(SIDE * PART, dtype=jnp.int32)[:, None]
    marked_src = jnp.where(positions < counts[0, 0], src_points, jnp.asarray(MARK, BF16))
    marked_tgt = jnp.where(positions < counts[0, 1], tgt_points, jnp.asarray(-MARK, BF16))
    own = collect(marked_tgt, z_perm)
    src_block = spread(marked_src, z_perm, z)
    following = [(SIDE * WIDTH + start, rows, to_group(array, -1)) for start, rows, array in own]
    sources = collect(src_block, x_perm)
    targets_all = own + following
    places_s = tuple((start, rows) for start, rows, _ in sources)
    places_t = tuple((start, rows) for start, rows, _ in targets_all)
    s_arrays = [array for _, _, array in sources]
    t_arrays = [array for _, _, array in targets_all]
    halves = [half_norms(array, scale) for _, _, array in sorted(targets_all, key=lambda one: one[0])]
    halves = jnp.concatenate(halves).reshape(LEVELS, PART)
    arrived = jnp.where(halves > 1e7, DEAD, -halves)

    half_src = half_norms(src_points, scale).reshape(SIDE, PART)
    half_tgt = half_norms(tgt_points, scale).reshape(SIDE, PART)

    src_slot = lookup(tiles[0], cell_slot[0])
    tgt_slot = lookup(tiles[1], cell_slot[1])
    src_cell = src_slot % SRC_CELLS
    tgt_cell = tgt_slot % SRC_CELLS // SIDE + jnp.where(tgt_slot // SRC_CELLS == src_index, 0, SIDE)
    mine = tgt_slot % SIDE == x
    index = jnp.arange(PAIRS, dtype=jnp.int32)
    place = jnp.sum((mine[None, :] & (index[None, :] < index[:, None])).astype(jnp.int32), axis=1)
    hits = mine[None, :] & (place[None, :] == index[:, None])
    pair_src = jnp.sum(jnp.where(hits, src_cell[None, :], 0), axis=1)
    pair_tgt = jnp.sum(jnp.where(hits, tgt_cell[None, :] - NOBODY, 0), axis=1) + NOBODY
    steps = (jnp.sum(mine.astype(jnp.int32)) + 1) // 2
    lists = jnp.concatenate([steps[None], pair_src, pair_tgt])
    local = jnp.arange(SRC_CELLS, dtype=jnp.int32)
    s_order = (z - local % SIDE) % SIDE * SIDE + (x - local // SIDE) % SIDE
    t_order = (z - jnp.arange(SIDE, dtype=jnp.int32)) % SIDE

    sums, small = shape(SRC_CELLS, PART), shape(LEVELS, PART)
    levels = pltpu.VMEM((LEVELS + 8, PART), F32)
    wide = pltpu.VMEM((SRC_CELLS, PART, PART), F32)
    narrow = pltpu.VMEM((TGT_CELLS + 1, TILES, 8, PART), F32)
    ring = [pltpu.VMEM((RING, 2, PART, WIDTH), F32)]
    ring_sem = [pltpu.SemaphoreType.DMA((RING,))]
    t_sem = [pltpu.SemaphoreType.DMA((len(t_arrays),))]
    kept, row_part, first_level, live = call(
        functools.partial(first_kernel, places_s, places_t, scale),
        (shape(STEPS, 2, PART, WIDTH), sums, small, sums),
        [SM] * 3 + [VM] + [ANY] * (len(s_arrays) + len(t_arrays)),
        [
            pltpu.VMEM((SRC_CELLS * PART, WIDTH), BF16),
            pltpu.VMEM((TGT_CELLS * WIDTH, WIDTH), BF16),
            levels,
        ]
        + [wide] * 4
        + ring
        + [pltpu.SemaphoreType.DMA((SRC_CELLS,))]
        + t_sem
        + ring_sem,
        lists,
        s_order,
        t_order,
        arrived,
        *s_arrays,
        *t_arrays,
        out_specs=(ANY, VM, VM, VM),
    )
    for sweep in range(ITERS):
        if sweep:
            row_part = call(
                row_kernel,
                sums,
                [SM] + [VM] * 4 + [ANY],
                [levels] + [wide] * 4 + ring + ring_sem,
                lists,
                joined,
                before,
                after,
                first_level,
                kept,
            )
        col_part, src_level = call(
            column_kernel,
            (small, sums),
            [SM] + [VM] * 5 + [ANY],
            [narrow] * 4 + [wide] + ring + ring_sem,
            lists,
            *ring_parts(row_part, x_perm),
            live,
            kept,
        )
        joined = join(ring_parts(col_part, z_perm))
        before = to_group(joined[LEVELS // 2 :], 1)
        after = to_group(joined[: LEVELS // 2], -1)
    blocks, own_level = call(
        functools.partial(transport_kernel, places_t),
        (shape(SRC_CELLS, PART + TAIL, WIDTH, dtype=BF16), shape(SIDE, PART)),
        [SM] * 2 + [VM] * 5 + [ANY] * (1 + len(t_arrays)),
        [pltpu.VMEM((TGT_CELLS * WIDTH, WIDTH), BF16), levels, wide]
        + [pltpu.VMEM((SRC_CELLS, PART, WIDTH), F32)] * 2
        + [wide] * 2
        + ring
        + t_sem
        + ring_sem,
        lists,
        t_order,
        joined,
        before,
        after,
        first_level,
        src_level,
        kept,
        *t_arrays,
    )
    got = lax.all_to_all(blocks, "help", 0, 0)
    source_out, target_out, transport = call(
        finish_kernel,
        (shape(SIDE, PART), shape(SIDE, PART), shape(SIDE * PART, WIDTH)),
        [SM] + [VM] * 4,
        [],
        counts,
        got,
        own_level,
        half_src,
        half_tgt,
    )
    return (source_out.reshape(-1), target_out.reshape(-1), transport)


def solution(mesh):
    in_specs = (
        P(None, "src"),
        P(),
        P(("src", "help"), None),
        P(("src", "help"), None),
        P(("src", "help"), None),
    )
    out_specs = (P(("src", "help")), P(("src", "help")), P(("src", "help"), None))
    return jax.shard_map(shards, mesh=mesh, in_specs=in_specs, out_specs=out_specs, check_vma=False)
```

time: 197 us -> 177 us (0.90)
  Pallas kernels: 61 us -> 40.6 us
  starting transfers between devices: 57.1 us -> 45.3 us
  waiting for transfers between devices: 70.9 us -> 78.2 us
  other arithmetic: 4.12 us -> 7.05 us
    pallas_call x6, Pallas kernels: 61 us -> 40.6 us  [call(): pl.pallas_call(kernel, out_shape=out_shape, in_specs=in_specs, out_specs=...]
    ppermute x26 -> x23, starting transfers between devices: 36.6 us -> 29.3 us  [to_help(): return lax.ppermute(array, 'help', perm)]
    ppermute x26 -> x23, waiting for transfers between devices: 17.8 us -> 23.2 us  [to_help(): return lax.ppermute(array, 'help', perm)]
    reduce_sum x8 -> x14, other arithmetic: 1.04 us -> 4.1 us  [the longest x11 3.24 us: half_norms(): return 0.5 * scale * jnp.sum(jnp.square(points.astype(F32)), axis=1)]
    ppermute x9, starting transfers between devices: 14.7 us -> 11.8 us  [to_group(): lax.ppermute(array, 'src', [(i, (i + by) % count) for i in range(count)])]
    ppermute x9, waiting for transfers between devices: 15.4 us -> 17.4 us  [to_group(): lax.ppermute(array, 'src', [(i, (i + by) % count) for i in range(count)])]
  transfers between devices with their start and end apart: 36 -> 33, of which waited for: 24 -> 22; matrix products, arithmetic and copies ran while one was open for 1% -> 3% of each run, Pallas kernels for 0% -> 0%
where the time goes in v3:
time: 177 us; the launch traced here: 176 us
  waiting for transfers between devices  78.2 us (44%)
  starting transfers between devices  45.3 us (26%)
  Pallas kernels  40.6 us (23%)
  other arithmetic  7.05 us (4%)
  local copies, waits for them, and re-layouts  2.87 us (2%)
    pallas_call x6, Pallas kernels, call(): pl.pallas_call(kernel, out_shape=out_shape, in_specs=in_specs, out_specs=...  40.6 us
    all_to_all x1, waiting for transfers between devices, shards(): got = lax.all_to_all(blocks, 'help', 0, 0)  37.7 us
    ppermute x23, starting transfers between devices, to_help(): return lax.ppermute(array, 'help', perm)  29.3 us
    ppermute x23, waiting for transfers between devices, to_help(): return lax.ppermute(array, 'help', perm)  23.2 us
    ppermute x9, waiting for transfers between devices, to_group(): lax.ppermute(array, 'src', [(i, (i + by) % count) for i in range(count)])  17.4 us
    ppermute x9, starting transfers between devices, to_group(): lax.ppermute(array, 'src', [(i, (i + by) % count) for i in range(count)])  11.8 us
    all_to_all x1, starting transfers between devices, shards(): got = lax.all_to_all(blocks, 'help', 0, 0)  4.2 us
  transfers between devices with their start and end apart: 33, of which 22 were waited for; matrix products, arithmetic and copies ran while one was open for 3% of the time, Pallas kernels for 0%

profile of v3, /device:TPU:17, one launch (start us, length us, event | category | flops | bytes accessed | tf_op | source)
XLA Modules:
  0.0 175.8 jit_solution(12718127638954243486)
XLA Ops:
  4.3 1.7 collective-permute-start
  6.0 2.2 %collective-permute-start.2 = (bf16[512,512]{1,0:T(8,128)(2,1)S(1)}, bf16[512,512]{1,0:T(8,128)(2,1)S(1)}, u32[]{:S(2)}, u32[]{:S(2)}) collective-permute-start(bf16[512,512]{1,0:T(8,128)(2,1)S(1)} %get-tuple-element.30.refs_5_.refs_0_), channel_id=1, source_target_pairs={{0,12},{1,13},{2,14},{3,15},{4,0},{5,1},{6,2},{7,3},{8,4},{9,5},{1... | collective-permute-start | bytes 1572872 | tf_op jit(solution)/shard_map/ppermute | solution.py:48
  14.8 8.7 %collective-permute-done.10 = bf16[128,512]{1,0:T(8,128)(2,1)S(1)} collective-permute-done((bf16[128,512]{1,0:T(8,128)(2,1)S(1)}, bf16[128,512]{1,0:T(8,128)(2,1)S(1)}, u32[]{:S(2)}, u32[]{:S(2)}) %collective-permute-start.10) | collective-permute-done | bytes 131104 | tf_op jit(solution)/shard_map/ppermute | solution.py:48
  23.4 2.7 %collective-permute-start.4 = (bf16[512,512]{1,0:T(8,128)(2,1)S(1)}, bf16[512,512]{1,0:T(8,128)(2,1)S(1)}, u32[]{:S(2)}, u32[]{:S(2)}) collective-permute-start(bf16[512,512]{1,0:T(8,128)(2,1)S(1)} %get-tuple-element.30.refs_5_.refs_0_), channel_id=1, source_target_pairs={{0,112},{16,0},{32,16},{48,32},{64,48},{80,64},{96,80},{112,96},{1... | collective-permute-start | bytes 1572872 | tf_op jit(solution)/shard_map/ppermute | solution.py:44
  32.2 2.0 %collective-permute-done.4.refs_10_.refs_5_ = bf16[512,512]{1,0:T(8,128)(2,1)S(1)} collective-permute-done((bf16[512,512]{1,0:T(8,128)(2,1)S(1)}, bf16[512,512]{1,0:T(8,128)(2,1)S(1)}, u32[]{:S(2)}, u32[]{:S(2)}) %collective-permute-start.4) | collective-permute-done | bytes 524320 | tf_op jit(solution)/shard_map/ppermute | solution.py:44
  34.4 6.2 %collective-permute-done.12.refs_1_ = bf16[512,512]{1,0:T(8,128)(2,1)S(1)} collective-permute-done((bf16[512,512]{1,0:T(8,128)(2,1)S(1)}, bf16[512,512]{1,0:T(8,128)(2,1)S(1)}, u32[]{:S(2)}, u32[]{:S(2)}) %collective-permute-start.12) | collective-permute-done | bytes 524320 | tf_op jit(solution)/shard_map/ppermute | solution.py:48
  42.0 2.7 %collective-permute-start.15 = (bf16[256,512]{1,0:T(8,128)(2,1)S(1)}, bf16[256,512]{1,0:T(8,128)(2,1)S(1)}, u32[]{:S(2)}, u32[]{:S(2)}) collective-permute-start(bf16[256,512]{1,0:T(8,128)(2,1)S(1)} %slice.59), channel_id=1, source_target_pairs={{0,3},{1,0},{2,1},{3,2},{4,7},{5,4},{6,5},{7,6},{8,11},{9,8},{10,9... | collective-permute-start | bytes 786440 | tf_op jit(solution)/shard_map/ppermute | solution.py:48
  45.8 6.6 %collective-permute-done.6.refs_13_.refs_8_ = bf16[256,512]{1,0:T(8,128)(2,1)S(1)} collective-permute-done((bf16[256,512]{1,0:T(8,128)(2,1)S(1)}, bf16[256,512]{1,0:T(8,128)(2,1)S(1)}, u32[]{:S(2)}, u32[]{:S(2)}) %collective-permute-start.6) | collective-permute-done | bytes 262176 | tf_op jit(solution)/shard_map/ppermute | solution.py:44
  52.5 2.7 %collective-permute-done.7.refs_14_.refs_9_ = bf16[256,512]{1,0:T(8,128)(2,1)S(1)} collective-permute-done((bf16[256,512]{1,0:T(8,128)(2,1)S(1)}, bf16[256,512]{1,0:T(8,128)(2,1)S(1)}, u32[]{:S(2)}, u32[]{:S(2)}) %collective-permute-start.7) | collective-permute-done | bytes 262176 | tf_op jit(solution)/shard_map/ppermute | solution.py:44
  55.6 14.9 %shard_map.76 = (f32[64,2,128,512]{3,2,1,0:T(8,128)}, f32[16,128]{1,0:T(8,128)S(1)}, f32[32,128]{1,0:T(8,128)S(1)}, f32[16,128]{1,0:T(8,128)S(1)}) custom-call(s32[257]{0:T(512)S(1)} %pad_add_fusion.lists, s32[16]{0:T(128)S(1)} %fusion.2.s_order, s32[4]{0:T(128)S(1)} %and_select_fusion.4.t_order, f32[32,128]{1,0:T(8,128)S(1)} %select_bitcast_fusion.arrived, ...), custom_call_target="tpu_custom_call" | custom-call | tf_op jit(solution)/shard_map/pallas_call | solution.py:424
  70.6 3.0 %collective-permute-start.17 = (f32[16,128]{1,0:T(8,128)S(1)}, f32[16,128]{1,0:T(8,128)S(1)}, u32[]{:S(2)}, u32[]{:S(2)}) collective-permute-start(f32[16,128]{1,0:T(8,128)S(1)} %get-tuple-element.15.r0), channel_id=1, source_target_pairs={{0,2},{1,3},{2,0},{3,1},{4,6},{5,7},{6,4},{7,5},{8,10},{9,11},{10,... | collective-permute-start | bytes 24584 | tf_op jit(solution)/shard_map/ppermute | solution.py:48
  76.1 4.8 %shard_map.77 = (f32[32,128]{1,0:T(8,128)S(1)}, f32[16,128]{1,0:T(8,128)}) custom-call(s32[257]{0:T(512)S(1)} %pad_add_fusion.lists, f32[16,128]{1,0:T(8,128)S(1)} %get-tuple-element.15.r0, f32[16,128]{1,0:T(8,128)S(1)} %collective-permute-done.16.r1, f32[16,128]{1,0:T(8,128)S(1)} %collective-permute-done.17.r2, f32[16,128]{1,0:T(8,128)S(1)} %collective-permute-done.18.r3, ...), custom_call_target="tpu_custom_call" | custom-call | tf_op jit(solution)/shard_map/pallas_call | solution.py:424
  86.7 3.1 %collective-permute-start.22 = (f32[16,128]{1,0:T(8,128)S(1)}, f32[16,128]{1,0:T(8,128)S(1)}, u32[]{:S(2)}, u32[]{:S(2)}) collective-permute-start(f32[16,128]{1,0:T(8,128)S(1)} %get-tuple-element.41), channel_id=1, source_target_pairs={{0,16},{16,32},{32,48},{48,64},{64,80},{80,96},{96,112},{112,0},{1... | collective-permute-start | bytes 24584 | tf_op jit(solution)/shard_map/ppermute | solution.py:44
  90.6 2.3 %collective-permute-done.23.after = f32[16,128]{1,0:T(8,128)S(1)} collective-permute-done((f32[16,128]{1,0:T(8,128)S(1)}, f32[16,128]{1,0:T(8,128)S(1)}, u32[]{:S(2)}, u32[]{:S(2)}) %collective-permute-start.23) | collective-permute-done | bytes 8224 | tf_op jit(solution)/shard_map/ppermute | solution.py:44
  92.9 5.2 %shard_map.78.r0 = f32[16,128]{1,0:T(8,128)S(1)} custom-call(s32[257]{0:T(512)S(1)} %pad_add_fusion.lists, f32[32,128]{1,0:T(8,128)S(1)} %multiply_add_fusion.1.joined, f32[16,128]{1,0:T(8,128)S(1)} %collective-permute-done.22.before, f32[16,128]{1,0:T(8,128)S(1)} %collective-permute-done.23.after, f32[32,128]{1,0:T(8,128)S(1)} %get-tuple-element.19.first_level, ...), custom_call_target="tpu_custom_call" | custom-call | tf_op jit(solution)/shard_map/pallas_call | solution.py:424
  98.9 2.2 %collective-permute-start.25 = (f32[16,128]{1,0:T(8,128)S(1)}, f32[16,128]{1,0:T(8,128)S(1)}, u32[]{:S(2)}, u32[]{:S(2)}) collective-permute-start(f32[16,128]{1,0:T(8,128)S(1)} %shard_map.78.r0), channel_id=1, source_target_pairs={{0,2},{1,3},{2,0},{3,1},{4,6},{5,7},{6,4},{7,5},{8,10},{9,11},{10,... | collective-permute-start | bytes 24584 | tf_op jit(solution)/shard_map/ppermute | solution.py:48
  103.6 4.3 %shard_map.79 = (f32[32,128]{1,0:T(8,128)S(1)}, f32[16,128]{1,0:T(8,128)S(1)}) custom-call(s32[257]{0:T(512)S(1)} %pad_add_fusion.lists, f32[16,128]{1,0:T(8,128)S(1)} %shard_map.78.r0, f32[16,128]{1,0:T(8,128)S(1)} %collective-permute-done.24.r1, f32[16,128]{1,0:T(8,128)S(1)} %collective-permute-done.25.r2, f32[16,128]{1,0:T(8,128)S(1)} %collective-permute-done.26.r3, ...), custom_call_target="tpu_custom_call" | custom-call | tf_op jit(solution)/shard_map/pallas_call | solution.py:424
  108.3 2.6 %collective-permute-start.28 = (f32[32,128]{1,0:T(8,128)S(1)}, f32[32,128]{1,0:T(8,128)S(1)}, u32[]{:S(2)}, u32[]{:S(2)}) collective-permute-start(f32[32,128]{1,0:T(8,128)S(1)} %get-tuple-element.20), channel_id=1, source_target_pairs={{0,8},{1,9},{2,10},{3,11},{4,12},{5,13},{6,14},{7,15},{8,0},{9,1},... | collective-permute-start | bytes 49160 | tf_op jit(solution)/shard_map/ppermute | solution.py:48
  113.9 4.0 %collective-permute-start.30 = (f32[16,128]{1,0:T(8,128)S(1)}, f32[16,128]{1,0:T(8,128)S(1)}, u32[]{:S(2)}, u32[]{:S(2)}) collective-permute-start(f32[16,128]{1,0:T(8,128)S(1)} %get-tuple-element.39), channel_id=1, source_target_pairs={{0,16},{16,32},{32,48},{48,64},{64,80},{80,96},{96,112},{112,0},{1... | collective-permute-start | bytes 24584 | tf_op jit(solution)/shard_map/ppermute | solution.py:44
  118.7 2.3 %collective-permute-done.31.after = f32[16,128]{1,0:T(8,128)S(1)} collective-permute-done((f32[16,128]{1,0:T(8,128)S(1)}, f32[16,128]{1,0:T(8,128)S(1)}, u32[]{:S(2)}, u32[]{:S(2)}) %collective-permute-start.31) | collective-permute-done | bytes 8224 | tf_op jit(solution)/shard_map/ppermute | solution.py:44
  121.0 9.4 %shard_map.80 = (bf16[16,144,512]{2,1,0:T(8,128)(2,1)S(1)}, f32[4,128]{1,0:T(4,128)S(1)}) custom-call(s32[257]{0:T(512)S(1)} %pad_add_fusion.lists, s32[4]{0:T(128)S(1)} %and_select_fusion.4.t_order, f32[32,128]{1,0:T(8,128)S(1)} %multiply_add_fusion.joined, f32[16,128]{1,0:T(8,128)S(1)} %collective-permute-done.30.before, ...), custom_call_target="tpu_custom_call" | custom-call | tf_op jit(solution)/shard_map/pallas_call | solution.py:424
  131.8 4.2 %all-to-all-start = ((bf16[16,144,512]{2,1,0:T(8,128)(2,1)}), bf16[16,144,512]{2,1,0:T(8,128)(2,1)S(1)}, u32[]{:S(2)}, u32[]{:S(2)}) async-start(bf16[16,144,512]{2,1,0:T(8,128)(2,1)} %copy-done), calls=%async_computation | async-start | bytes 4718592 | tf_op jit(solution)/shard_map/all_to_all | solution.py:559
  136.2 37.7 %all-to-all-done.got = bf16[16,144,512]{2,1,0:T(8,128)(2,1)S(1)} async-done(((bf16[16,144,512]{2,1,0:T(8,128)(2,1)}), bf16[16,144,512]{2,1,0:T(8,128)(2,1)S(1)}, u32[]{:S(2)}, u32[]{:S(2)}) %all-to-all-start) | async-done | bytes 2359328 | tf_op jit(solution)/shard_map/all_to_all | solution.py:559
  173.9 1.9 %shard_map.81 = (f32[4,128]{1,0:T(4,128)}, f32[4,128]{1,0:T(4,128)}, f32[512,512]{1,0:T(8,128)}) custom-call(s32[1,2]{1,0:T(1,128)S(1)} %copy-done.1, bf16[16,144,512]{2,1,0:T(8,128)(2,1)S(1)} %all-to-all-done.got, f32[4,128]{1,0:T(4,128)S(1)} %get-tuple-element.23.own_level, f32[4,128]{1,0:T(4,128)S(1)} %multiply_bitcast_fusion.1.half_src, ...), custom_call_target="tpu_custom_call" | custom-call | tf_op jit(solution)/shard_map/pallas_call | solution.py:424
  (108 shorter events, 36.7 us)
Async XLA Ops:
  4.3 24.7 %collective-permute-start = (bf16[512,512]{1,0:T(8,128)(2,1)S(1)}, bf16[512,512]{1,0:T(8,128)(2,1)S(1)}, u32[]{:S(2)}, u32[]{:S(2)}) collective-permute-start(bf16[512,512]{1,0:T(8,128)(2,1)S(1)} %get-tuple-element.30.refs_5_.refs_0_), channel_id=1, source_target_pairs={{0,4},{1,5},{2,6},{3,7},{4,8},{5,9},{6,10},{7,11},{8,12},{9,13},{1... | collective-permute-start | bytes 1572872 | tf_op jit(solution)/shard_map/ppermute | solution.py:48
  6.0 24.3 %collective-permute-start.2 = (bf16[512,512]{1,0:T(8,128)(2,1)S(1)}, bf16[512,512]{1,0:T(8,128)(2,1)S(1)}, u32[]{:S(2)}, u32[]{:S(2)}) collective-permute-start(bf16[512,512]{1,0:T(8,128)(2,1)S(1)} %get-tuple-element.30.refs_5_.refs_0_), channel_id=1, source_target_pairs={{0,12},{1,13},{2,14},{3,15},{4,0},{5,1},{6,2},{7,3},{8,4},{9,5},{1... | collective-permute-start | bytes 1572872 | tf_op jit(solution)/shard_map/ppermute | solution.py:48
  10.1 13.3 %collective-permute-start.10 = (bf16[128,512]{1,0:T(8,128)(2,1)S(1)}, bf16[128,512]{1,0:T(8,128)(2,1)S(1)}, u32[]{:S(2)}, u32[]{:S(2)}) collective-permute-start(bf16[128,512]{1,0:T(8,128)(2,1)S(1)} %get-tuple-element.36), channel_id=1, source_target_pairs={{0,8},{1,9},{2,10},{3,11},{4,12},{5,13},{6,14},{7,15},{8,0},{9,1},... | collective-permute-start | bytes 393224 | tf_op jit(solution)/shard_map/ppermute | solution.py:48
  11.4 14.7 %collective-permute-start.11 = (bf16[128,512]{1,0:T(8,128)(2,1)S(1)}, bf16[128,512]{1,0:T(8,128)(2,1)S(1)}, u32[]{:S(2)}, u32[]{:S(2)}) collective-permute-start(bf16[128,512]{1,0:T(8,128)(2,1)S(1)} %get-tuple-element.35), channel_id=1, source_target_pairs={{0,12},{1,13},{2,14},{3,15},{4,0},{5,1},{6,2},{7,3},{8,4},{9,5},{1... | collective-permute-start | bytes 393224 | tf_op jit(solution)/shard_map/ppermute | solution.py:48
  12.0 14.1 %collective-permute-start.9 = (bf16[128,512]{1,0:T(8,128)(2,1)S(1)}, bf16[128,512]{1,0:T(8,128)(2,1)S(1)}, u32[]{:S(2)}, u32[]{:S(2)}) collective-permute-start(bf16[128,512]{1,0:T(8,128)(2,1)S(1)} %get-tuple-element.37), channel_id=1, source_target_pairs={{0,4},{1,5},{2,6},{3,7},{4,8},{5,9},{6,10},{7,11},{8,12},{9,13},{1... | collective-permute-start | bytes 393224 | tf_op jit(solution)/shard_map/ppermute | solution.py:48
  23.4 10.7 %collective-permute-start.4 = (bf16[512,512]{1,0:T(8,128)(2,1)S(1)}, bf16[512,512]{1,0:T(8,128)(2,1)S(1)}, u32[]{:S(2)}, u32[]{:S(2)}) collective-permute-start(bf16[512,512]{1,0:T(8,128)(2,1)S(1)} %get-tuple-element.30.refs_5_.refs_0_), channel_id=1, source_target_pairs={{0,112},{16,0},{32,16},{48,32},{64,48},{80,64},{96,80},{112,96},{1... | collective-permute-start | bytes 1572872 | tf_op jit(solution)/shard_map/ppermute | solution.py:44
  26.2 14.3 %collective-permute-start.12 = (bf16[512,512]{1,0:T(8,128)(2,1)S(1)}, bf16[512,512]{1,0:T(8,128)(2,1)S(1)}, u32[]{:S(2)}, u32[]{:S(2)}) collective-permute-start(bf16[512,512]{1,0:T(8,128)(2,1)S(1)} %pad_maximum_fusion.refs_0_), channel_id=1, source_target_pairs={{0,1},{1,2},{2,3},{3,0},{4,5},{5,6},{6,7},{7,4},{8,9},{9,10},{10,1... | collective-permute-start | bytes 1572872 | tf_op jit(solution)/shard_map/ppermute | solution.py:48
  27.5 14.4 %collective-permute-start.13 = (bf16[512,512]{1,0:T(8,128)(2,1)S(1)}, bf16[512,512]{1,0:T(8,128)(2,1)S(1)}, u32[]{:S(2)}, u32[]{:S(2)}) collective-permute-start(bf16[512,512]{1,0:T(8,128)(2,1)S(1)} %pad_maximum_fusion.refs_0_), channel_id=1, source_target_pairs={{0,3},{1,0},{2,1},{3,2},{4,7},{5,4},{6,5},{7,6},{8,11},{9,8},{10,9... | collective-permute-start | bytes 1572872 | tf_op jit(solution)/shard_map/ppermute | solution.py:48
  29.0 13.0 %collective-permute-start.1 = (bf16[256,512]{1,0:T(8,128)(2,1)S(1)}, bf16[256,512]{1,0:T(8,128)(2,1)S(1)}, u32[]{:S(2)}, u32[]{:S(2)}) collective-permute-start(bf16[256,512]{1,0:T(8,128)(2,1)S(1)} %slice.56), channel_id=1, source_target_pairs={{0,4},{1,5},{2,6},{3,7},{4,8},{5,9},{6,10},{7,11},{8,12},{9,13},{1... | collective-permute-start | bytes 786440 | tf_op jit(solution)/shard_map/ppermute | solution.py:48
  30.3 14.6 %collective-permute-start.3 = (bf16[256,512]{1,0:T(8,128)(2,1)S(1)}, bf16[256,512]{1,0:T(8,128)(2,1)S(1)}, u32[]{:S(2)}, u32[]{:S(2)}) collective-permute-start(bf16[256,512]{1,0:T(8,128)(2,1)S(1)} %slice.57), channel_id=1, source_target_pairs={{0,12},{1,13},{2,14},{3,15},{4,0},{5,1},{6,2},{7,3},{8,4},{9,5},{1... | collective-permute-start | bytes 786440 | tf_op jit(solution)/shard_map/ppermute | solution.py:48
  34.2 11.4 %collective-permute-start.5 = (bf16[512,512]{1,0:T(8,128)(2,1)S(1)}, bf16[512,512]{1,0:T(8,128)(2,1)S(1)}, u32[]{:S(2)}, u32[]{:S(2)}) collective-permute-start(bf16[512,512]{1,0:T(8,128)(2,1)S(1)} %collective-permute-done.refs_6_.refs_1_), channel_id=1, source_target_pairs={{0,112},{16,0},{32,16},{48,32},{64,48},{80,64},{96,80},{112,96},{1... | collective-permute-start | bytes 1572872 | tf_op jit(solution)/shard_map/ppermute | solution.py:44
  40.5 14.8 %collective-permute-start.8 = (bf16[512,512]{1,0:T(8,128)(2,1)S(1)}, bf16[512,512]{1,0:T(8,128)(2,1)S(1)}, u32[]{:S(2)}, u32[]{:S(2)}) collective-permute-start(bf16[512,512]{1,0:T(8,128)(2,1)S(1)} %collective-permute-done.2.refs_7_.refs_2_), channel_id=1, source_target_pairs={{0,112},{16,0},{32,16},{48,32},{64,48},{80,64},{96,80},{112,96},{1... | collective-permute-start | bytes 1572872 | tf_op jit(solution)/shard_map/ppermute | solution.py:44
  41.8 13.7 %collective-permute-start.14 = (bf16[256,512]{1,0:T(8,128)(2,1)S(1)}, bf16[256,512]{1,0:T(8,128)(2,1)S(1)}, u32[]{:S(2)}, u32[]{:S(2)}) collective-permute-start(bf16[256,512]{1,0:T(8,128)(2,1)S(1)} %slice.58), channel_id=1, source_target_pairs={{0,1},{1,2},{2,3},{3,0},{4,5},{5,6},{6,7},{7,4},{8,9},{9,10},{10,1... | collective-permute-start | bytes 786440 | tf_op jit(solution)/shard_map/ppermute | solution.py:48
  42.0 13.6 %collective-permute-start.15 = (bf16[256,512]{1,0:T(8,128)(2,1)S(1)}, bf16[256,512]{1,0:T(8,128)(2,1)S(1)}, u32[]{:S(2)}, u32[]{:S(2)}) collective-permute-start(bf16[256,512]{1,0:T(8,128)(2,1)S(1)} %slice.59), channel_id=1, source_target_pairs={{0,3},{1,0},{2,1},{3,2},{4,7},{5,4},{6,5},{7,6},{8,11},{9,8},{10,9... | collective-permute-start | bytes 786440 | tf_op jit(solution)/shard_map/ppermute | solution.py:48
  45.0 7.4 %collective-permute-start.6 = (bf16[256,512]{1,0:T(8,128)(2,1)S(1)}, bf16[256,512]{1,0:T(8,128)(2,1)S(1)}, u32[]{:S(2)}, u32[]{:S(2)}) collective-permute-start(bf16[256,512]{1,0:T(8,128)(2,1)S(1)} %collective-permute-done.1.refs_8_.refs_3_), channel_id=1, source_target_pairs={{0,112},{16,0},{32,16},{48,32},{64,48},{80,64},{96,80},{112,96},{1... | collective-permute-start | bytes 786440 | tf_op jit(solution)/shard_map/ppermute | solution.py:44
  45.6 9.6 %collective-permute-start.7 = (bf16[256,512]{1,0:T(8,128)(2,1)S(1)}, bf16[256,512]{1,0:T(8,128)(2,1)S(1)}, u32[]{:S(2)}, u32[]{:S(2)}) collective-permute-start(bf16[256,512]{1,0:T(8,128)(2,1)S(1)} %collective-permute-done.3.refs_9_.refs_4_), channel_id=1, source_target_pairs={{0,112},{16,0},{32,16},{48,32},{64,48},{80,64},{96,80},{112,96},{1... | collective-permute-start | bytes 786440 | tf_op jit(solution)/shard_map/ppermute | solution.py:44
  70.5 4.1 %collective-permute-start.16 = (f32[16,128]{1,0:T(8,128)S(1)}, f32[16,128]{1,0:T(8,128)S(1)}, u32[]{:S(2)}, u32[]{:S(2)}) collective-permute-start(f32[16,128]{1,0:T(8,128)S(1)} %get-tuple-element.15.r0), channel_id=1, source_target_pairs={{0,1},{1,2},{2,3},{3,0},{4,5},{5,6},{6,7},{7,4},{8,9},{9,10},{10,1... | collective-permute-start | bytes 24584 | tf_op jit(solution)/shard_map/ppermute | solution.py:48
  70.6 4.3 %collective-permute-start.17 = (f32[16,128]{1,0:T(8,128)S(1)}, f32[16,128]{1,0:T(8,128)S(1)}, u32[]{:S(2)}, u32[]{:S(2)}) collective-permute-start(f32[16,128]{1,0:T(8,128)S(1)} %get-tuple-element.15.r0), channel_id=1, source_target_pairs={{0,2},{1,3},{2,0},{3,1},{4,6},{5,7},{6,4},{7,5},{8,10},{9,11},{10,... | collective-permute-start | bytes 24584 | tf_op jit(solution)/shard_map/ppermute | solution.py:48
  82.2 4.1 %collective-permute-start.20 = (f32[32,128]{1,0:T(8,128)S(1)}, f32[32,128]{1,0:T(8,128)S(1)}, u32[]{:S(2)}, u32[]{:S(2)}) collective-permute-start(f32[32,128]{1,0:T(8,128)S(1)} %get-tuple-element.18), channel_id=1, source_target_pairs={{0,8},{1,9},{2,10},{3,11},{4,12},{5,13},{6,14},{7,15},{8,0},{9,1},... | collective-permute-start | bytes 49160 | tf_op jit(solution)/shard_map/ppermute | solution.py:48
  86.7 3.9 %collective-permute-start.22 = (f32[16,128]{1,0:T(8,128)S(1)}, f32[16,128]{1,0:T(8,128)S(1)}, u32[]{:S(2)}, u32[]{:S(2)}) collective-permute-start(f32[16,128]{1,0:T(8,128)S(1)} %get-tuple-element.41), channel_id=1, source_target_pairs={{0,16},{16,32},{32,48},{48,64},{64,80},{80,96},{96,112},{112,0},{1... | collective-permute-start | bytes 24584 | tf_op jit(solution)/shard_map/ppermute | solution.py:44
  98.9 4.2 %collective-permute-start.25 = (f32[16,128]{1,0:T(8,128)S(1)}, f32[16,128]{1,0:T(8,128)S(1)}, u32[]{:S(2)}, u32[]{:S(2)}) collective-permute-start(f32[16,128]{1,0:T(8,128)S(1)} %shard_map.78.r0), channel_id=1, source_target_pairs={{0,2},{1,3},{2,0},{3,1},{4,6},{5,7},{6,4},{7,5},{8,10},{9,11},{10,... | collective-permute-start | bytes 24584 | tf_op jit(solution)/shard_map/ppermute | solution.py:48
  108.3 4.1 %collective-permute-start.28 = (f32[32,128]{1,0:T(8,128)S(1)}, f32[32,128]{1,0:T(8,128)S(1)}, u32[]{:S(2)}, u32[]{:S(2)}) collective-permute-start(f32[32,128]{1,0:T(8,128)S(1)} %get-tuple-element.20), channel_id=1, source_target_pairs={{0,8},{1,9},{2,10},{3,11},{4,12},{5,13},{6,14},{7,15},{8,0},{9,1},... | collective-permute-start | bytes 49160 | tf_op jit(solution)/shard_map/ppermute | solution.py:48
  113.9 4.8 %collective-permute-start.30 = (f32[16,128]{1,0:T(8,128)S(1)}, f32[16,128]{1,0:T(8,128)S(1)}, u32[]{:S(2)}, u32[]{:S(2)}) collective-permute-start(f32[16,128]{1,0:T(8,128)S(1)} %get-tuple-element.39), channel_id=1, source_target_pairs={{0,16},{16,32},{32,48},{48,64},{64,80},{80,96},{96,112},{112,0},{1... | collective-permute-start | bytes 24584 | tf_op jit(solution)/shard_map/ppermute | solution.py:44
  131.8 42.1 %all-to-all-start = ((bf16[16,144,512]{2,1,0:T(8,128)(2,1)}), bf16[16,144,512]{2,1,0:T(8,128)(2,1)S(1)}, u32[]{:S(2)}, u32[]{:S(2)}) async-start(bf16[16,144,512]{2,1,0:T(8,128)(2,1)} %copy-done), calls=%async_computation | async-start | bytes 4718592 | tf_op jit(solution)/shard_map/all_to_all | solution.py:559
  (14 other events, 100.7 us)

commit v4 on v3

--- a/solution.py
+++ b/solution.py
@@ -53,12 +53,12 @@
     return jnp.sum(jnp.where(matches, slot_table[None, :], 0), axis=1)
 
 
-def spread(points, perm, me):
-    parts = [lax.dynamic_slice_in_dim(points, me * PART, PART, 0)]
-    for by in range(1, SIDE):
-        other = (me + by) % SIDE
-        parts.append(to_help(lax.dynamic_slice_in_dim(points, other * PART, PART, 0), perm(by)))
-    return jnp.concatenate(parts, axis=0)
+def quarters(points, me):
+    return [lax.dynamic_slice_in_dim(points, (me + by) % SIDE * PART, PART, 0) for by in range(SIDE)]
+
+
+def spread(parts, perm):
+    return [part if by == 0 else to_help(part, perm(by)) for by, part in enumerate(parts)]
 
 
 def collect(block, perm):
@@ -121,11 +121,16 @@
 
 def load_targets(refs, places, order, target, sem):
     copies = []
-    for (start, rows), ref in zip(places, refs):
-        side, place = start // WIDTH // SIDE, start // WIDTH % SIDE
-        first = (side * SIDE + order[place]) * WIDTH + start % WIDTH
-        goal = target.at[pl.ds(pl.multiple_of(first, PART), rows)]
-        copies.append(pltpu.make_async_copy(ref, goal, sem.at[len(copies)]))
+    for cells, ref in zip(places, refs):
+        for index, cell in enumerate(cells):
+            side, place = cell // SIDE, cell % SIDE
+            copies.append(
+                pltpu.make_async_copy(
+                    ref.at[pl.ds(index * WIDTH, WIDTH)],
+                    target.at[cell_rows(side * SIDE + order[place])],
+                    sem.at[len(copies)],
+                )
+            )
     return copies
 
 
@@ -448,21 +453,30 @@
     positions = jnp.arange(SIDE * PART, dtype=jnp.int32)[:, None]
     marked_src = jnp.where(positions < counts[0, 0], src_points, jnp.asarray(MARK, BF16))
     marked_tgt = jnp.where(positions < counts[0, 1], tgt_points, jnp.asarray(-MARK, BF16))
-    own = collect(marked_tgt, z_perm)
-    src_block = spread(marked_src, z_perm, z)
-    following = [(SIDE * WIDTH + start, rows, to_group(array, -1)) for start, rows, array in own]
+    next_first = to_group(marked_tgt, -1)
+    parts = spread(quarters(marked_src, z), z_perm)
+    src_block = jnp.concatenate(parts, axis=0)
+    _, later_tgt = lax.optimization_barrier((parts[1], marked_tgt))
+    own = collect(later_tgt, z_perm)
+    _, tiles, cell_slot = lax.optimization_barrier((own[1][2], tiles, cell_slot))
+    around = jnp.concatenate([own[1][2], own[2][2]], axis=0)
+    opposite = jnp.concatenate([own[3][2], own[4][2]], axis=0)
+    own = [((0,), marked_tgt), ((1, 3), around), ((2,), opposite)]
+    following = [((SIDE,), next_first)] + [
+        (tuple(SIDE + cell for cell in cells), to_group(array, -1)) for cells, array in own[1:]
+    ]
     sources = collect(src_block, x_perm)
     targets_all = own + following
     places_s = tuple((start, rows) for start, rows, _ in sources)
-    places_t = tuple((start, rows) for start, rows, _ in targets_all)
+    places_t = tuple(cells for cells, _ in targets_all)
     s_arrays = [array for _, _, array in sources]
-    t_arrays = [array for _, _, array in targets_all]
-    halves = [half_norms(array, scale) for _, _, array in sorted(targets_all, key=lambda one: one[0])]
+    t_arrays = [array for _, array in targets_all]
+    halves = [half_norms(array, scale).reshape(-1, TILES, PART) for array in t_arrays]
+    halves = [
+        part for at in (0, 3) for part in (halves[at], halves[at + 1][:1], halves[at + 2], halves[at + 1][1:])
+    ]
     halves = jnp.concatenate(halves).reshape(LEVELS, PART)
     arrived = jnp.where(halves > 1e7, DEAD, -halves)
-
-    half_src = half_norms(src_points, scale).reshape(SIDE, PART)
-    half_tgt = half_norms(tgt_points, scale).reshape(SIDE, PART)
 
     src_slot = lookup(tiles[0], cell_slot[0])
     tgt_slot = lookup(tiles[1], cell_slot[1])
@@ -486,7 +500,7 @@
     narrow = pltpu.VMEM((TGT_CELLS + 1, TILES, 8, PART), F32)
     ring = [pltpu.VMEM((RING, 2, PART, WIDTH), F32)]
     ring_sem = [pltpu.SemaphoreType.DMA((RING,))]
-    t_sem = [pltpu.SemaphoreType.DMA((len(t_arrays),))]
+    t_sem = [pltpu.SemaphoreType.DMA((TGT_CELLS,))]
     kept, row_part, first_level, live = call(
         functools.partial(first_kernel, places_s, places_t, scale),
         (shape(STEPS, 2, PART, WIDTH), sums, small, sums),
@@ -557,6 +571,9 @@
         *t_arrays,
     )
     got = lax.all_to_all(blocks, "help", 0, 0)
+    _, src_after, tgt_after = lax.optimization_barrier((src_level, src_points, tgt_points))
+    half_src = half_norms(src_after, scale).reshape(SIDE, PART)
+    half_tgt = half_norms(tgt_after, scale).reshape(SIDE, PART)
     source_out, target_out, transport = call(
         finish_kernel,
         (shape(SIDE, PART), shape(SIDE, PART), shape(SIDE * PART, WIDTH)),

time: 177 us -> 173 us (0.977)
  waiting for transfers between devices: 78.2 us -> 68.3 us
  local copies, waits for them, and re-layouts: 2.87 us -> 9.6 us
    ppermute x23, waiting for transfers between devices: 23.2 us -> 17.5 us  [to_help(): return lax.ppermute(array, 'help', perm)]
    ppermute x9 -> x7, waiting for transfers between devices: 17.4 us -> 13.7 us  [to_group(): lax.ppermute(array, 'src', [(i, (i + by) % count) for i in range(count)])]
    ppermute x9 -> x7, starting transfers between devices: 11.8 us -> 9.17 us  [to_group(): lax.ppermute(array, 'src', [(i, (i + by) % count) for i in range(count)])]
    slice x2, local copies, waits for them, and re-layouts: 0.04 us -> 2.39 us  [collect(): far_low = to_help(behind[:half], perm(1))]
    ppermute x23, starting transfers between devices: 29.3 us -> 31.4 us  [to_help(): return lax.ppermute(array, 'help', perm)]
    unnamed x10 -> x21, local copies, waits for them, and re-layouts: 1.42 us -> 3.33 us
  transfers between devices with their start and end apart: 33 -> 31, of which waited for: 22 -> 19; matrix products, arithmetic and copies ran while one was open for 3% -> 7% of each run, Pallas kernels for 0% -> 0%
where the time goes in v4:
time: 173 us
  waiting for transfers between devices  68.3 us (39%)
  starting transfers between devices  45 us (26%)
  Pallas kernels  40.5 us (23%)
  local copies, waits for them, and re-layouts  9.6 us (6%)
  other arithmetic  7.53 us (4%)
  between operations  1.78 us (1%)
    pallas_call x6, Pallas kernels, call(): pl.pallas_call(kernel, out_shape=out_shape, in_specs=in_specs, out_specs=...  40.5 us
    all_to_all x1, waiting for transfers between devices, shards(): got = lax.all_to_all(blocks, 'help', 0, 0)  37.1 us
    ppermute x23, starting transfers between devices, to_help(): return lax.ppermute(array, 'help', perm)  31.4 us
    ppermute x23, waiting for transfers between devices, to_help(): return lax.ppermute(array, 'help', perm)  17.5 us
    ppermute x7, waiting for transfers between devices, to_group(): lax.ppermute(array, 'src', [(i, (i + by) % count) for i in range(count)])  13.7 us
    ppermute x7, starting transfers between devices, to_group(): lax.ppermute(array, 'src', [(i, (i + by) % count) for i in range(count)])  9.17 us
    all_to_all x1, starting transfers between devices, shards(): got = lax.all_to_all(blocks, 'help', 0, 0)  4.52 us
  transfers between devices with their start and end apart: 31, of which 19 were waited for; matrix products, arithmetic and copies ran while one was open for 7% of the time, Pallas kernels for 0%

profile of v4, /device:TPU:17, one launch (start us, length us, event | category | flops | bytes accessed | tf_op | source)
XLA Modules:
  0.0 172.8 jit_solution(3260037493611612571)
XLA Ops:
  4.0 1.7 collective-permute-start
  7.6 3.3 %collective-permute-start.8 = (bf16[128,512]{1,0:T(8,128)(2,1)S(1)}, bf16[128,512]{1,0:T(8,128)(2,1)S(1)}, u32[]{:S(2)}, u32[]{:S(2)}) collective-permute-start(bf16[128,512]{1,0:T(8,128)(2,1)S(1)} %get-tuple-element.45), channel_id=1, source_target_pairs={{0,8},{1,9},{2,10},{3,11},{4,12},{5,13},{6,14},{7,15},{8,0},{9,1},... | collective-permute-start | bytes 393224 | tf_op jit(solution)/shard_map/ppermute | solution.py:48
  12.4 1.9 %collective-permute-start.2 = (bf16[512,512]{1,0:T(8,128)(2,1)S(1)}, bf16[512,512]{1,0:T(8,128)(2,1)S(1)}, u32[]{:S(2)}, u32[]{:S(2)}) collective-permute-start(bf16[512,512]{1,0:T(8,128)(2,1)S(1)} %get-tuple-element.20.refs_5_.refs_0_), channel_id=1, source_target_pairs={{0,12},{1,13},{2,14},{3,15},{4,0},{5,1},{6,2},{7,3},{8,4},{9,5},{1... | collective-permute-start | bytes 1572872 | tf_op jit(solution)/shard_map/ppermute | solution.py:48
  15.0 1.6 collective-permute-done.9
  20.3 6.6 %collective-permute-done.1 = bf16[512,512]{1,0:T(8,128)(2,1)S(1)} collective-permute-done((bf16[512,512]{1,0:T(8,128)(2,1)S(1)}, bf16[512,512]{1,0:T(8,128)(2,1)S(1)}, u32[]{:S(2)}, u32[]{:S(2)}) %collective-permute-start.1) | collective-permute-done | bytes 524320 | tf_op jit(solution)/shard_map/ppermute | solution.py:48
  28.8 2.2 %collective-permute-start.4 = (bf16[256,512]{1,0:T(8,128)(2,1)}, bf16[256,512]{1,0:T(8,128)(2,1)}, u32[]{:S(2)}, u32[]{:S(2)}) collective-permute-start(bf16[256,512]{1,0:T(8,128)(2,1)} %slice.97), channel_id=1, source_target_pairs={{0,12},{1,13},{2,14},{3,15},{4,0},{5,1},{6,2},{7,3},{8,4},{9,5},{1... | collective-permute-start | bytes 786440 | tf_op jit(solution)/shard_map/ppermute | solution.py:48
  32.6 1.7 slice.98
  44.3 7.5 %collective-permute-done.7.refs_10_.refs_5_ = bf16[512,512]{1,0:T(8,128)(2,1)S(1)} collective-permute-done((bf16[512,512]{1,0:T(8,128)(2,1)S(1)}, bf16[512,512]{1,0:T(8,128)(2,1)S(1)}, u32[]{:S(2)}, u32[]{:S(2)}) %collective-permute-start.7) | collective-permute-done | bytes 524320 | tf_op jit(solution)/shard_map/ppermute | solution.py:44
  52.4 14.0 %shard_map.76 = (f32[64,2,128,512]{3,2,1,0:T(8,128)}, f32[16,128]{1,0:T(8,128)S(1)}, f32[32,128]{1,0:T(8,128)S(1)}, f32[16,128]{1,0:T(8,128)S(1)}) custom-call(s32[257]{0:T(512)S(1)} %pad_add_fusion.lists, s32[16]{0:T(128)S(1)} %fusion.2.s_order, s32[4]{0:T(128)S(1)} %and_select_fusion.4.t_order, f32[32,128]{1,0:T(8,128)S(1)} %bitcast.34, ...), custom_call_target="tpu_custom_call" | custom-call | tf_op jit(solution)/shard_map/pallas_call | solution.py:429
  66.5 4.0 %collective-permute-start.15 = (f32[16,128]{1,0:T(8,128)S(1)}, f32[16,128]{1,0:T(8,128)S(1)}, u32[]{:S(2)}, u32[]{:S(2)}) collective-permute-start(f32[16,128]{1,0:T(8,128)S(1)} %get-tuple-element.23.r0), channel_id=1, source_target_pairs={{0,2},{1,3},{2,0},{3,1},{4,6},{5,7},{6,4},{7,5},{8,10},{9,11},{10,... | collective-permute-start | bytes 24584 | tf_op jit(solution)/shard_map/ppermute | solution.py:48
  72.9 5.0 %shard_map.77 = (f32[32,128]{1,0:T(8,128)S(1)}, f32[16,128]{1,0:T(8,128)}) custom-call(s32[257]{0:T(512)S(1)} %pad_add_fusion.lists, f32[16,128]{1,0:T(8,128)S(1)} %get-tuple-element.23.r0, f32[16,128]{1,0:T(8,128)S(1)} %collective-permute-done.14.r1, f32[16,128]{1,0:T(8,128)S(1)} %collective-permute-done.15.r2, f32[16,128]{1,0:T(8,128)S(1)} %collective-permute-done.16.r3, ...), custom_call_target="tpu_custom_call" | custom-call | tf_op jit(solution)/shard_map/pallas_call | solution.py:429
  78.0 1.7 collective-permute-start.18
  82.7 2.7 %collective-permute-start.20 = (f32[16,128]{1,0:T(8,128)S(1)}, f32[16,128]{1,0:T(8,128)S(1)}, u32[]{:S(2)}, u32[]{:S(2)}) collective-permute-start(f32[16,128]{1,0:T(8,128)S(1)} %get-tuple-element.50), channel_id=1, source_target_pairs={{0,16},{16,32},{32,48},{48,64},{64,80},{80,96},{96,112},{112,0},{1... | collective-permute-start | bytes 24584 | tf_op jit(solution)/shard_map/ppermute | solution.py:44
  86.2 2.3 %collective-permute-done.21.after = f32[16,128]{1,0:T(8,128)S(1)} collective-permute-done((f32[16,128]{1,0:T(8,128)S(1)}, f32[16,128]{1,0:T(8,128)S(1)}, u32[]{:S(2)}, u32[]{:S(2)}) %collective-permute-start.21) | collective-permute-done | bytes 8224 | tf_op jit(solution)/shard_map/ppermute | solution.py:44
  88.4 5.4 %shard_map.78.r0 = f32[16,128]{1,0:T(8,128)S(1)} custom-call(s32[257]{0:T(512)S(1)} %pad_add_fusion.lists, f32[32,128]{1,0:T(8,128)S(1)} %multiply_add_fusion.1.joined, f32[16,128]{1,0:T(8,128)S(1)} %collective-permute-done.20.before, f32[16,128]{1,0:T(8,128)S(1)} %collective-permute-done.21.after, f32[32,128]{1,0:T(8,128)S(1)} %get-tuple-element.27.first_level, ...), custom_call_target="tpu_custom_call" | custom-call | tf_op jit(solution)/shard_map/pallas_call | solution.py:429
  95.2 2.1 %collective-permute-start.23 = (f32[16,128]{1,0:T(8,128)S(1)}, f32[16,128]{1,0:T(8,128)S(1)}, u32[]{:S(2)}, u32[]{:S(2)}) collective-permute-start(f32[16,128]{1,0:T(8,128)S(1)} %shard_map.78.r0), channel_id=1, source_target_pairs={{0,2},{1,3},{2,0},{3,1},{4,6},{5,7},{6,4},{7,5},{8,10},{9,11},{10,... | collective-permute-start | bytes 24584 | tf_op jit(solution)/shard_map/ppermute | solution.py:48
  100.0 4.5 %shard_map.79 = (f32[32,128]{1,0:T(8,128)S(1)}, f32[16,128]{1,0:T(8,128)S(1)}) custom-call(s32[257]{0:T(512)S(1)} %pad_add_fusion.lists, f32[16,128]{1,0:T(8,128)S(1)} %shard_map.78.r0, f32[16,128]{1,0:T(8,128)S(1)} %collective-permute-done.22.r1, f32[16,128]{1,0:T(8,128)S(1)} %collective-permute-done.23.r2, f32[16,128]{1,0:T(8,128)S(1)} %collective-permute-done.24.r3, ...), custom_call_target="tpu_custom_call" | custom-call | tf_op jit(solution)/shard_map/pallas_call | solution.py:429
  105.1 2.6 %collective-permute-start.26 = (f32[32,128]{1,0:T(8,128)S(1)}, f32[32,128]{1,0:T(8,128)S(1)}, u32[]{:S(2)}, u32[]{:S(2)}) collective-permute-start(f32[32,128]{1,0:T(8,128)S(1)} %get-tuple-element.28), channel_id=1, source_target_pairs={{0,8},{1,9},{2,10},{3,11},{4,12},{5,13},{6,14},{7,15},{8,0},{9,1},... | collective-permute-start | bytes 49160 | tf_op jit(solution)/shard_map/ppermute | solution.py:48
  110.6 2.9 %collective-permute-start.28 = (f32[16,128]{1,0:T(8,128)S(1)}, f32[16,128]{1,0:T(8,128)S(1)}, u32[]{:S(2)}, u32[]{:S(2)}) collective-permute-start(f32[16,128]{1,0:T(8,128)S(1)} %get-tuple-element.48), channel_id=1, source_target_pairs={{0,16},{16,32},{32,48},{48,64},{64,80},{80,96},{96,112},{112,0},{1... | collective-permute-start | bytes 24584 | tf_op jit(solution)/shard_map/ppermute | solution.py:44
  114.3 2.3 %collective-permute-done.29.after = f32[16,128]{1,0:T(8,128)S(1)} collective-permute-done((f32[16,128]{1,0:T(8,128)S(1)}, f32[16,128]{1,0:T(8,128)S(1)}, u32[]{:S(2)}, u32[]{:S(2)}) %collective-permute-start.29) | collective-permute-done | bytes 8224 | tf_op jit(solution)/shard_map/ppermute | solution.py:44
  116.6 9.8 %shard_map.80 = (bf16[16,144,512]{2,1,0:T(8,128)(2,1)S(1)}, f32[4,128]{1,0:T(4,128)S(1)}) custom-call(s32[257]{0:T(512)S(1)} %pad_add_fusion.lists, s32[4]{0:T(128)S(1)} %and_select_fusion.4.t_order, f32[32,128]{1,0:T(8,128)S(1)} %multiply_add_fusion.joined, f32[16,128]{1,0:T(8,128)S(1)} %collective-permute-done.28.before, ...), custom_call_target="tpu_custom_call" | custom-call | tf_op jit(solution)/shard_map/pallas_call | solution.py:429
  127.8 4.5 %all-to-all-start = ((bf16[16,144,512]{2,1,0:T(8,128)(2,1)}), bf16[16,144,512]{2,1,0:T(8,128)(2,1)S(1)}, u32[]{:S(2)}, u32[]{:S(2)}) async-start(bf16[16,144,512]{2,1,0:T(8,128)(2,1)} %copy-done), calls=%async_computation | async-start | bytes 4718592 | tf_op jit(solution)/shard_map/all_to_all | solution.py:573
  133.8 37.1 %all-to-all-done.got = bf16[16,144,512]{2,1,0:T(8,128)(2,1)S(1)} async-done(((bf16[16,144,512]{2,1,0:T(8,128)(2,1)}), bf16[16,144,512]{2,1,0:T(8,128)(2,1)S(1)}, u32[]{:S(2)}, u32[]{:S(2)}) %all-to-all-start) | async-done | bytes 2359328 | tf_op jit(solution)/shard_map/all_to_all | solution.py:573
  170.9 1.9 %shard_map.81 = (f32[4,128]{1,0:T(4,128)}, f32[4,128]{1,0:T(4,128)}, f32[512,512]{1,0:T(8,128)}) custom-call(s32[1,2]{1,0:T(1,128)S(1)} %copy-done.3, bf16[16,144,512]{2,1,0:T(8,128)(2,1)S(1)} %all-to-all-done.got, f32[4,128]{1,0:T(4,128)S(1)} %get-tuple-element.31.own_level, f32[4,128]{1,0:T(4,128)S(1)} %multiply_bitcast_fusion.1.half_src, ...), custom_call_target="tpu_custom_call" | custom-call | tf_op jit(solution)/shard_map/pallas_call | solution.py:429
  (110 shorter events, 41.7 us)
Async XLA Ops:
  4.0 7.7 %collective-permute-start = (bf16[128,512]{1,0:T(8,128)(2,1)S(1)}, bf16[128,512]{1,0:T(8,128)(2,1)S(1)}, u32[]{:S(2)}, u32[]{:S(2)}) collective-permute-start(bf16[128,512]{1,0:T(8,128)(2,1)S(1)} %get-tuple-element.46), channel_id=1, source_target_pairs={{0,4},{1,5},{2,6},{3,7},{4,8},{5,9},{6,10},{7,11},{8,12},{9,13},{1... | collective-permute-start | bytes 393224 | tf_op jit(solution)/shard_map/ppermute | solution.py:48
  6.7 13.5 %collective-permute-start.5 = (bf16[512,512]{1,0:T(8,128)(2,1)S(1)}, bf16[512,512]{1,0:T(8,128)(2,1)S(1)}, u32[]{:S(2)}, u32[]{:S(2)}) collective-permute-start(bf16[512,512]{1,0:T(8,128)(2,1)S(1)} %get-tuple-element.20.refs_5_.refs_0_), channel_id=1, source_target_pairs={{0,112},{16,0},{32,16},{48,32},{64,48},{80,64},{96,80},{112,96},{1... | collective-permute-start | bytes 1572872 | tf_op jit(solution)/shard_map/ppermute | solution.py:44
  7.6 7.3 %collective-permute-start.8 = (bf16[128,512]{1,0:T(8,128)(2,1)S(1)}, bf16[128,512]{1,0:T(8,128)(2,1)S(1)}, u32[]{:S(2)}, u32[]{:S(2)}) collective-permute-start(bf16[128,512]{1,0:T(8,128)(2,1)S(1)} %get-tuple-element.45), channel_id=1, source_target_pairs={{0,8},{1,9},{2,10},{3,11},{4,12},{5,13},{6,14},{7,15},{8,0},{9,1},... | collective-permute-start | bytes 393224 | tf_op jit(solution)/shard_map/ppermute | solution.py:48
  10.9 5.6 %collective-permute-start.9 = (bf16[128,512]{1,0:T(8,128)(2,1)S(1)}, bf16[128,512]{1,0:T(8,128)(2,1)S(1)}, u32[]{:S(2)}, u32[]{:S(2)}) collective-permute-start(bf16[128,512]{1,0:T(8,128)(2,1)S(1)} %get-tuple-element.44), channel_id=1, source_target_pairs={{0,12},{1,13},{2,14},{3,15},{4,0},{5,1},{6,2},{7,3},{8,4},{9,5},{1... | collective-permute-start | bytes 393224 | tf_op jit(solution)/shard_map/ppermute | solution.py:48
  11.7 15.3 %collective-permute-start.1 = (bf16[512,512]{1,0:T(8,128)(2,1)S(1)}, bf16[512,512]{1,0:T(8,128)(2,1)S(1)}, u32[]{:S(2)}, u32[]{:S(2)}) collective-permute-start(bf16[512,512]{1,0:T(8,128)(2,1)S(1)} %get-tuple-element.20.refs_5_.refs_0_), channel_id=1, source_target_pairs={{0,4},{1,5},{2,6},{3,7},{4,8},{5,9},{6,10},{7,11},{8,12},{9,13},{1... | collective-permute-start | bytes 1572872 | tf_op jit(solution)/shard_map/ppermute | solution.py:48
  12.4 15.7 %collective-permute-start.2 = (bf16[512,512]{1,0:T(8,128)(2,1)S(1)}, bf16[512,512]{1,0:T(8,128)(2,1)S(1)}, u32[]{:S(2)}, u32[]{:S(2)}) collective-permute-start(bf16[512,512]{1,0:T(8,128)(2,1)S(1)} %get-tuple-element.20.refs_5_.refs_0_), channel_id=1, source_target_pairs={{0,12},{1,13},{2,14},{3,15},{4,0},{5,1},{6,2},{7,3},{8,4},{9,5},{1... | collective-permute-start | bytes 1572872 | tf_op jit(solution)/shard_map/ppermute | solution.py:48
  17.4 15.2 %collective-permute-start.10 = (bf16[512,512]{1,0:T(8,128)(2,1)}, bf16[512,512]{1,0:T(8,128)(2,1)}, u32[]{:S(2)}, u32[]{:S(2)}) collective-permute-start(bf16[512,512]{1,0:T(8,128)(2,1)} %pad_maximum_fusion.refs_0_), channel_id=1, source_target_pairs={{0,1},{1,2},{2,3},{3,0},{4,5},{5,6},{6,7},{7,4},{8,9},{9,10},{10,1... | collective-permute-start | bytes 1572872 | tf_op jit(solution)/shard_map/ppermute | solution.py:48
  18.6 17.2 %collective-permute-start.11 = (bf16[512,512]{1,0:T(8,128)(2,1)}, bf16[512,512]{1,0:T(8,128)(2,1)S(1)}, u32[]{:S(2)}, u32[]{:S(2)}) collective-permute-start(bf16[512,512]{1,0:T(8,128)(2,1)} %pad_maximum_fusion.refs_0_), channel_id=1, source_target_pairs={{0,3},{1,0},{2,1},{3,2},{4,7},{5,4},{6,5},{7,6},{8,11},{9,8},{10,9... | collective-permute-start | bytes 1572872 | tf_op jit(solution)/shard_map/ppermute | solution.py:48
  27.6 13.2 %collective-permute-start.3 = (bf16[256,512]{1,0:T(8,128)(2,1)}, bf16[256,512]{1,0:T(8,128)(2,1)}, u32[]{:S(2)}, u32[]{:S(2)}) collective-permute-start(bf16[256,512]{1,0:T(8,128)(2,1)} %slice.96), channel_id=1, source_target_pairs={{0,4},{1,5},{2,6},{3,7},{4,8},{5,9},{6,10},{7,11},{8,12},{9,13},{1... | collective-permute-start | bytes 786440 | tf_op jit(solution)/shard_map/ppermute | solution.py:48
  28.8 13.0 %collective-permute-start.4 = (bf16[256,512]{1,0:T(8,128)(2,1)}, bf16[256,512]{1,0:T(8,128)(2,1)}, u32[]{:S(2)}, u32[]{:S(2)}) collective-permute-start(bf16[256,512]{1,0:T(8,128)(2,1)} %slice.97), channel_id=1, source_target_pairs={{0,12},{1,13},{2,14},{3,15},{4,0},{5,1},{6,2},{7,3},{8,4},{9,5},{1... | collective-permute-start | bytes 786440 | tf_op jit(solution)/shard_map/ppermute | solution.py:48
  31.2 20.8 %collective-permute-start.6 = (bf16[1024,512]{1,0:T(8,128)(2,1)S(1)}, bf16[1024,512]{1,0:T(8,128)(2,1)S(1)}, u32[]{:S(2)}, u32[]{:S(2)}) collective-permute-start(bf16[1024,512]{1,0:T(8,128)(2,1)S(1)} %constant_dynamic-update-slice_fusion.refs_6_.refs_1_), channel_id=1, source_target_pairs={{0,112},{16,0},{32,16},{48,32},{64,48},{80,64},{96,80},{112,96},{1... | collective-permute-start | bytes 3145736 | tf_op jit(solution)/shard_map/ppermute | solution.py:44
  34.3 18.1 %collective-permute-start.12 = (bf16[256,512]{1,0:T(8,128)(2,1)}, bf16[256,512]{1,0:T(8,128)(2,1)S(1)}, u32[]{:S(2)}, u32[]{:S(2)}) collective-permute-start(bf16[256,512]{1,0:T(8,128)(2,1)} %slice.98), channel_id=1, source_target_pairs={{0,1},{1,2},{2,3},{3,0},{4,5},{5,6},{6,7},{7,4},{8,9},{9,10},{10,1... | collective-permute-start | bytes 786440 | tf_op jit(solution)/shard_map/ppermute | solution.py:48
  37.3 15.0 %collective-permute-start.13 = (bf16[256,512]{1,0:T(8,128)(2,1)}, bf16[256,512]{1,0:T(8,128)(2,1)}, u32[]{:S(2)}, u32[]{:S(2)}) collective-permute-start(bf16[256,512]{1,0:T(8,128)(2,1)} %slice.99), channel_id=1, source_target_pairs={{0,3},{1,0},{2,1},{3,2},{4,7},{5,4},{6,5},{7,6},{8,11},{9,8},{10,9... | collective-permute-start | bytes 786440 | tf_op jit(solution)/shard_map/ppermute | solution.py:48
  42.8 9.0 %collective-permute-start.7 = (bf16[512,512]{1,0:T(8,128)(2,1)S(1)}, bf16[512,512]{1,0:T(8,128)(2,1)S(1)}, u32[]{:S(2)}, u32[]{:S(2)}) collective-permute-start(bf16[512,512]{1,0:T(8,128)(2,1)S(1)} %constant_dynamic-update-slice_fusion.2.refs_7_.refs_2_), channel_id=1, source_target_pairs={{0,112},{16,0},{32,16},{48,32},{64,48},{80,64},{96,80},{112,96},{1... | collective-permute-start | bytes 1572872 | tf_op jit(solution)/shard_map/ppermute | solution.py:44
  66.4 4.7 %collective-permute-start.14 = (f32[16,128]{1,0:T(8,128)S(1)}, f32[16,128]{1,0:T(8,128)S(1)}, u32[]{:S(2)}, u32[]{:S(2)}) collective-permute-start(f32[16,128]{1,0:T(8,128)S(1)} %get-tuple-element.23.r0), channel_id=1, source_target_pairs={{0,1},{1,2},{2,3},{3,0},{4,5},{5,6},{6,7},{7,4},{8,9},{9,10},{10,1... | collective-permute-start | bytes 24584 | tf_op jit(solution)/shard_map/ppermute | solution.py:48
  66.5 5.1 %collective-permute-start.15 = (f32[16,128]{1,0:T(8,128)S(1)}, f32[16,128]{1,0:T(8,128)S(1)}, u32[]{:S(2)}, u32[]{:S(2)}) collective-permute-start(f32[16,128]{1,0:T(8,128)S(1)} %get-tuple-element.23.r0), channel_id=1, source_target_pairs={{0,2},{1,3},{2,0},{3,1},{4,6},{5,7},{6,4},{7,5},{8,10},{9,11},{10,... | collective-permute-start | bytes 24584 | tf_op jit(solution)/shard_map/ppermute | solution.py:48
  77.9 4.3 %collective-permute-start.17 = (f32[32,128]{1,0:T(8,128)S(1)}, f32[32,128]{1,0:T(8,128)S(1)}, u32[]{:S(2)}, u32[]{:S(2)}) collective-permute-start(f32[32,128]{1,0:T(8,128)S(1)} %get-tuple-element.26), channel_id=1, source_target_pairs={{0,4},{1,5},{2,6},{3,7},{4,8},{5,9},{6,10},{7,11},{8,12},{9,13},{1... | collective-permute-start | bytes 49160 | tf_op jit(solution)/shard_map/ppermute | solution.py:48
  78.0 4.6 %collective-permute-start.18 = (f32[32,128]{1,0:T(8,128)S(1)}, f32[32,128]{1,0:T(8,128)S(1)}, u32[]{:S(2)}, u32[]{:S(2)}) collective-permute-start(f32[32,128]{1,0:T(8,128)S(1)} %get-tuple-element.26), channel_id=1, source_target_pairs={{0,8},{1,9},{2,10},{3,11},{4,12},{5,13},{6,14},{7,15},{8,0},{9,1},... | collective-permute-start | bytes 49160 | tf_op jit(solution)/shard_map/ppermute | solution.py:48
  93.8 3.8 %collective-permute-start.22 = (f32[16,128]{1,0:T(8,128)S(1)}, f32[16,128]{1,0:T(8,128)S(1)}, u32[]{:S(2)}, u32[]{:S(2)}) collective-permute-start(f32[16,128]{1,0:T(8,128)S(1)} %shard_map.78.r0), channel_id=1, source_target_pairs={{0,1},{1,2},{2,3},{3,0},{4,5},{5,6},{6,7},{7,4},{8,9},{9,10},{10,1... | collective-permute-start | bytes 24584 | tf_op jit(solution)/shard_map/ppermute | solution.py:48
  95.2 4.0 %collective-permute-start.23 = (f32[16,128]{1,0:T(8,128)S(1)}, f32[16,128]{1,0:T(8,128)S(1)}, u32[]{:S(2)}, u32[]{:S(2)}) collective-permute-start(f32[16,128]{1,0:T(8,128)S(1)} %shard_map.78.r0), channel_id=1, source_target_pairs={{0,2},{1,3},{2,0},{3,1},{4,6},{5,7},{6,4},{7,5},{8,10},{9,11},{10,... | collective-permute-start | bytes 24584 | tf_op jit(solution)/shard_map/ppermute | solution.py:48
  104.5 3.9 %collective-permute-start.25 = (f32[32,128]{1,0:T(8,128)S(1)}, f32[32,128]{1,0:T(8,128)S(1)}, u32[]{:S(2)}, u32[]{:S(2)}) collective-permute-start(f32[32,128]{1,0:T(8,128)S(1)} %get-tuple-element.28), channel_id=1, source_target_pairs={{0,4},{1,5},{2,6},{3,7},{4,8},{5,9},{6,10},{7,11},{8,12},{9,13},{1... | collective-permute-start | bytes 49160 | tf_op jit(solution)/shard_map/ppermute | solution.py:48
  105.1 4.1 %collective-permute-start.26 = (f32[32,128]{1,0:T(8,128)S(1)}, f32[32,128]{1,0:T(8,128)S(1)}, u32[]{:S(2)}, u32[]{:S(2)}) collective-permute-start(f32[32,128]{1,0:T(8,128)S(1)} %get-tuple-element.28), channel_id=1, source_target_pairs={{0,8},{1,9},{2,10},{3,11},{4,12},{5,13},{6,14},{7,15},{8,0},{9,1},... | collective-permute-start | bytes 49160 | tf_op jit(solution)/shard_map/ppermute | solution.py:48
  110.6 3.7 %collective-permute-start.28 = (f32[16,128]{1,0:T(8,128)S(1)}, f32[16,128]{1,0:T(8,128)S(1)}, u32[]{:S(2)}, u32[]{:S(2)}) collective-permute-start(f32[16,128]{1,0:T(8,128)S(1)} %get-tuple-element.48), channel_id=1, source_target_pairs={{0,16},{16,32},{32,48},{48,64},{64,80},{80,96},{96,112},{112,0},{1... | collective-permute-start | bytes 24584 | tf_op jit(solution)/shard_map/ppermute | solution.py:44
  127.8 43.1 %all-to-all-start = ((bf16[16,144,512]{2,1,0:T(8,128)(2,1)}), bf16[16,144,512]{2,1,0:T(8,128)(2,1)S(1)}, u32[]{:S(2)}, u32[]{:S(2)}) async-start(bf16[16,144,512]{2,1,0:T(8,128)(2,1)} %copy-done), calls=%async_computation | async-start | bytes 4718592 | tf_op jit(solution)/shard_map/all_to_all | solution.py:573
  (15 other events, 107.8 us)

commit v5 on v4

--- a/solution.py
+++ b/solution.py
@@ -24,11 +24,11 @@
 TAIL = 16
 PAIRS = 128
 STEPS = PAIRS // 2
-RING = 20
+RING = 12
 NOBODY = TGT_CELLS
 F32 = jnp.float32
 BF16 = jnp.bfloat16
-VMEM_LIMIT = 40 * 1024 * 1024
+VMEM_LIMIT = 28 * 1024 * 1024
 
 
 def x_perm(by):
@@ -53,8 +53,17 @@
     return jnp.sum(jnp.where(matches, slot_table[None, :], 0), axis=1)
 
 
-def quarters(points, me):
-    return [lax.dynamic_slice_in_dim(points, (me + by) % SIDE * PART, PART, 0) for by in range(SIDE)]
+def mark_kernel(counts, place, src_ref, tgt_ref, q0, q1, q2, q3, marked_ref):
+    rows = lax.broadcasted_iota(jnp.int32, (PART, WIDTH), 0)
+
+    def marked(ref, q, count, mark):
+        points = ref[part_of(q), :].astype(F32)
+        return jnp.where(rows + q * PART < count, points, mark).astype(BF16)
+
+    for by, out in enumerate((q0, q1, q2, q3)):
+        out[...] = marked(src_ref, lax.rem(place[0] + by, SIDE), counts[0, 0], MARK)
+    for q in range(SIDE):
+        marked_ref[q * PART : (q + 1) * PART, :] = marked(tgt_ref, q, counts[0, 1], -MARK)
 
 
 def spread(parts, perm):
@@ -347,8 +356,7 @@
 ):
     nt = len(places_t)
     t_refs = refs[:nt]
-    out_ref, own_ref, ys, level_ref, wide_ref, map0, map1, mass0, mass1, ring, t_sem, sem = refs[nt:]
-    maps, masses = (map0, map1), (mass0, mass1)
+    out_ref, own_ref, ys, level_ref, wide_ref, map_ref, mass_ref, ring, t_sem, sem = refs[nt:]
     steps = lists[0]
     copies = load_targets(t_refs, places_t, t_order, ys, t_sem)
     for copy in copies:
@@ -356,7 +364,7 @@
     stream_start(kept, ring, sem, steps)
     target_levels(joined, before, after, first_level, level_ref)
     spread_rows(src_level, wide_ref)
-    for one in maps + masses:
+    for one in (map_ref, mass_ref):
         one[...] = jnp.zeros(one.shape, F32)
     for k, level in enumerate(level_rows(level_ref, t_order[0])):
         own_ref[k : k + 1, :] = level
@@ -365,6 +373,7 @@
 
     def step(i, carry):
         table = stream_step(kept, ring, sem, i, steps)
+        parts = []
         for half in range(2):
             s, t = pair(lists, i, half)
             level = wide_ref[s]
@@ -372,18 +381,19 @@
                 jnp.exp2(table[half, :, tile(k)] + one + level).astype(BF16)
                 for k, one in enumerate(level_rows(level_ref, t))
             ]
-            maps[half][s] += jnp.dot(
-                jnp.concatenate(weights, axis=1), ys[cell_rows(t), :], preferred_element_type=F32
-            )
-            masses[half][s] += functools.reduce(jnp.add, [one.astype(F32) for one in weights])
+            part = jnp.dot(jnp.concatenate(weights, axis=1), ys[cell_rows(t), :], preferred_element_type=F32)
+            parts.append((s, part, functools.reduce(jnp.add, [one.astype(F32) for one in weights])))
+        for s, part, mass in parts:
+            map_ref[s] += part
+            mass_ref[s] += mass
         return carry
 
     lax.fori_loop(0, steps, step, 0)
     rows = lax.broadcasted_iota(jnp.int32, (TAIL, WIDTH), 0)
 
     def cell(s, carry):
-        mass = to_lanes(jnp.sum(mass0[s] + mass1[s], axis=1, keepdims=True))
-        out_ref[s, :PART, :] = (map0[s] + map1[s]).astype(BF16)
+        mass = to_lanes(jnp.sum(mass_ref[s], axis=1, keepdims=True))
+        out_ref[s, :PART, :] = map_ref[s].astype(BF16)
         parts = pieces(mass, 2) + pieces(src_level[pl.ds(s, 1), :], 3)
         last = jnp.concatenate([parts[4]] * SIDE, axis=1)
         tail = jnp.where(rows == 0, jnp.concatenate(parts[:4], axis=1), jnp.where(rows == 1, last, 0.0))
@@ -450,11 +460,19 @@
     z, x = help_index // SIDE, help_index % SIDE
     scale = LOG2E / (math.sqrt(WIDTH) * EPSILON)
 
-    positions = jnp.arange(SIDE * PART, dtype=jnp.int32)[:, None]
-    marked_src = jnp.where(positions < counts[0, 0], src_points, jnp.asarray(MARK, BF16))
-    marked_tgt = jnp.where(positions < counts[0, 1], tgt_points, jnp.asarray(-MARK, BF16))
+    quarter = shape(PART, WIDTH, dtype=BF16)
+    *quarters, marked_tgt = call(
+        mark_kernel,
+        (quarter,) * SIDE + (shape(WIDTH, WIDTH, dtype=BF16),),
+        [SM, SM, VM, VM],
+        [],
+        counts,
+        z[None],
+        src_points,
+        tgt_points,
+    )
     next_first = to_group(marked_tgt, -1)
-    parts = spread(quarters(marked_src, z), z_perm)
+    parts = spread(quarters, z_perm)
     src_block = jnp.concatenate(parts, axis=0)
     _, later_tgt = lax.optimization_barrier((parts[1], marked_tgt))
     own = collect(later_tgt, z_perm)
@@ -555,8 +573,7 @@
         (shape(SRC_CELLS, PART + TAIL, WIDTH, dtype=BF16), shape(SIDE, PART)),
         [SM] * 2 + [VM] * 5 + [ANY] * (1 + len(t_arrays)),
         [pltpu.VMEM((TGT_CELLS * WIDTH, WIDTH), BF16), levels, wide]
-        + [pltpu.VMEM((SRC_CELLS, PART, WIDTH), F32)] * 2
-        + [wide] * 2
+        + [pltpu.VMEM((SRC_CELLS, PART, WIDTH), F32), wide]
         + ring
         + t_sem
         + ring_sem,

time: 173 us -> 171 us (0.988); the launches traced: 173 us -> 168 us
  waiting for transfers between devices: 68.3 us -> 63.3 us
  local copies, waits for them, and re-layouts: 9.6 us -> 13.6 us
  other arithmetic: 7.53 us -> 4.1 us
  starting transfers between devices: 45 us -> 43.1 us
  Pallas kernels: 40.5 us -> 42.3 us
    unnamed x21 -> x28, local copies, waits for them, and re-layouts: 3.33 us -> 8.02 us
    all_to_all x1, waiting for transfers between devices: 37.1 us -> 33.4 us  [shards(): got = lax.all_to_all(blocks, 'help', 0, 0)]
    pallas_call x6 -> x7, Pallas kernels: 40.5 us -> 42.3 us  [call(): pl.pallas_call(kernel, out_shape=out_shape, in_specs=in_specs, out_specs=...]
  transfers between devices with their start and end apart: 31 -> 31, of which waited for: 19 -> 17; matrix products, arithmetic and copies ran while one was open for 7% -> 8% of each run, Pallas kernels for 0% -> 0%
where the time goes in v5:
time: 171 us; the launch traced here: 168 us
  waiting for transfers between devices  63.3 us (37%)
  starting transfers between devices  43.1 us (25%)
  Pallas kernels  42.3 us (25%)
  local copies, waits for them, and re-layouts  13.6 us (8%)
  other arithmetic  4.1 us (2%)
    pallas_call x7, Pallas kernels, call(): pl.pallas_call(kernel, out_shape=out_shape, in_specs=in_specs, out_specs=...  42.3 us
    all_to_all x1, waiting for transfers between devices, shards(): got = lax.all_to_all(blocks, 'help', 0, 0)  33.4 us
    ppermute x23, starting transfers between devices, to_help(): return lax.ppermute(array, 'help', perm)  30.8 us
    ppermute x23, waiting for transfers between devices, to_help(): return lax.ppermute(array, 'help', perm)  15.8 us
    ppermute x7, waiting for transfers between devices, to_group(): lax.ppermute(array, 'src', [(i, (i + by) % count) for i in range(count)])  14.1 us
    ppermute x7, starting transfers between devices, to_group(): lax.ppermute(array, 'src', [(i, (i + by) % count) for i in range(count)])  8.49 us
    unnamed x28, local copies, waits for them, and re-layouts  8.02 us
    all_to_all x1, starting transfers between devices, shards(): got = lax.all_to_all(blocks, 'help', 0, 0)  3.86 us
  transfers between devices with their start and end apart: 31, of which 17 were waited for; matrix products, arithmetic and copies ran while one was open for 8% of the time, Pallas kernels for 0%

profile of v5, /device:TPU:17, one launch (start us, length us, event | category | flops | bytes accessed | tf_op | source)
XLA Modules:
  0.0 168.0 jit_solution(1423866362556433520)
XLA Ops:
  4.1 1.7 %collective-permute-start = (bf16[128,512]{1,0:T(8,128)(2,1)S(1)}, bf16[128,512]{1,0:T(8,128)(2,1)S(1)}, u32[]{:S(2)}, u32[]{:S(2)}) collective-permute-start(bf16[128,512]{1,0:T(8,128)(2,1)S(1)} %get-tuple-element.25), channel_id=1, source_target_pairs={{0,4},{1,5},{2,6},{3,7},{4,8},{5,9},{6,10},{7,11},{8,12},{9,13},{1... | collective-permute-start | bytes 393224 | tf_op jit(solution)/shard_map/ppermute | solution.py:48
  6.8 3.3 %collective-permute-start.8 = (bf16[128,512]{1,0:T(8,128)(2,1)S(1)}, bf16[128,512]{1,0:T(8,128)(2,1)S(1)}, u32[]{:S(2)}, u32[]{:S(2)}) collective-permute-start(bf16[128,512]{1,0:T(8,128)(2,1)S(1)} %get-tuple-element.31), channel_id=1, source_target_pairs={{0,8},{1,9},{2,10},{3,11},{4,12},{5,13},{6,14},{7,15},{8,0},{9,1},... | collective-permute-start | bytes 393224 | tf_op jit(solution)/shard_map/ppermute | solution.py:48
  12.4 1.9 %collective-permute-start.2 = (bf16[512,512]{1,0:T(8,128)(2,1)S(1)}, bf16[512,512]{1,0:T(8,128)(2,1)S(1)}, u32[]{:S(2)}, u32[]{:S(2)}) collective-permute-start(bf16[512,512]{1,0:T(8,128)(2,1)S(1)} %get-tuple-element.27.refs_5_.refs_0_), channel_id=1, source_target_pairs={{0,12},{1,13},{2,14},{3,15},{4,0},{5,1},{6,2},{7,3},{8,4},{9,5},{1... | collective-permute-start | bytes 1572872 | tf_op jit(solution)/shard_map/ppermute | solution.py:48
  19.3 7.8 %collective-permute-done.1 = bf16[512,512]{1,0:T(8,128)(2,1)S(1)} collective-permute-done((bf16[512,512]{1,0:T(8,128)(2,1)S(1)}, bf16[512,512]{1,0:T(8,128)(2,1)S(1)}, u32[]{:S(2)}, u32[]{:S(2)}) %collective-permute-start.1) | collective-permute-done | bytes 524320 | tf_op jit(solution)/shard_map/ppermute | solution.py:48
  28.6 2.7 %collective-permute-start.4 = (bf16[256,512]{1,0:T(8,128)(2,1)}, bf16[256,512]{1,0:T(8,128)(2,1)}, u32[]{:S(2)}, u32[]{:S(2)}) collective-permute-start(bf16[256,512]{1,0:T(8,128)(2,1)} %slice.89), channel_id=1, source_target_pairs={{0,12},{1,13},{2,14},{3,15},{4,0},{5,1},{6,2},{7,3},{8,4},{9,5},{1... | collective-permute-start | bytes 786440 | tf_op jit(solution)/shard_map/ppermute | solution.py:48
  32.8 1.7 slice.90
  43.8 8.0 %collective-permute-done.7.refs_10_.refs_5_ = bf16[512,512]{1,0:T(8,128)(2,1)S(1)} collective-permute-done((bf16[512,512]{1,0:T(8,128)(2,1)S(1)}, bf16[512,512]{1,0:T(8,128)(2,1)S(1)}, u32[]{:S(2)}, u32[]{:S(2)}) %collective-permute-start.7) | collective-permute-done | bytes 524320 | tf_op jit(solution)/shard_map/ppermute | solution.py:44
  52.3 14.4 %shard_map.77 = (f32[64,2,128,512]{3,2,1,0:T(8,128)}, f32[16,128]{1,0:T(8,128)S(1)}, f32[32,128]{1,0:T(8,128)S(1)}, f32[16,128]{1,0:T(8,128)S(1)}) custom-call(s32[257]{0:T(512)S(1)} %pad_add_fusion.lists, s32[16]{0:T(128)S(1)} %fusion.2.s_order, s32[4]{0:T(128)S(1)} %and_select_fusion.4.t_order, f32[32,128]{1,0:T(8,128)S(1)} %bitcast.33, ...), custom_call_target="tpu_custom_call" | custom-call | tf_op jit(solution)/shard_map/pallas_call | solution.py:439
  67.0 2.4 %collective-permute-start.15 = (f32[16,128]{1,0:T(8,128)S(1)}, f32[16,128]{1,0:T(8,128)S(1)}, u32[]{:S(2)}, u32[]{:S(2)}) collective-permute-start(f32[16,128]{1,0:T(8,128)S(1)} %get-tuple-element.33.r0), channel_id=1, source_target_pairs={{0,2},{1,3},{2,0},{3,1},{4,6},{5,7},{6,4},{7,5},{8,10},{9,11},{10,... | collective-permute-start | bytes 24584 | tf_op jit(solution)/shard_map/ppermute | solution.py:48
  72.3 5.2 %shard_map.78 = (f32[32,128]{1,0:T(8,128)S(1)}, f32[16,128]{1,0:T(8,128)}) custom-call(s32[257]{0:T(512)S(1)} %pad_add_fusion.lists, f32[16,128]{1,0:T(8,128)S(1)} %get-tuple-element.33.r0, f32[16,128]{1,0:T(8,128)S(1)} %collective-permute-done.14.r1, f32[16,128]{1,0:T(8,128)S(1)} %collective-permute-done.15.r2, f32[16,128]{1,0:T(8,128)S(1)} %collective-permute-done.16.r3, ...), custom_call_target="tpu_custom_call" | custom-call | tf_op jit(solution)/shard_map/pallas_call | solution.py:439
  77.6 1.8 %collective-permute-start.18 = (f32[32,128]{1,0:T(8,128)S(1)}, f32[32,128]{1,0:T(8,128)S(1)}, u32[]{:S(2)}, u32[]{:S(2)}) collective-permute-start(f32[32,128]{1,0:T(8,128)S(1)} %get-tuple-element.36), channel_id=1, source_target_pairs={{0,8},{1,9},{2,10},{3,11},{4,12},{5,13},{6,14},{7,15},{8,0},{9,1},... | collective-permute-start | bytes 49160 | tf_op jit(solution)/shard_map/ppermute | solution.py:48
  82.5 2.1 %collective-permute-start.20 = (f32[16,128]{1,0:T(8,128)S(1)}, f32[16,128]{1,0:T(8,128)S(1)}, u32[]{:S(2)}, u32[]{:S(2)}) collective-permute-start(f32[16,128]{1,0:T(8,128)S(1)} %get-tuple-element.54), channel_id=1, source_target_pairs={{0,16},{16,32},{32,48},{48,64},{64,80},{80,96},{96,112},{112,0},{1... | collective-permute-start | bytes 24584 | tf_op jit(solution)/shard_map/ppermute | solution.py:44
  85.3 2.3 %collective-permute-done.21.after = f32[16,128]{1,0:T(8,128)S(1)} collective-permute-done((f32[16,128]{1,0:T(8,128)S(1)}, f32[16,128]{1,0:T(8,128)S(1)}, u32[]{:S(2)}, u32[]{:S(2)}) %collective-permute-start.21) | collective-permute-done | bytes 8224 | tf_op jit(solution)/shard_map/ppermute | solution.py:44
  87.6 5.7 %shard_map.79.r0 = f32[16,128]{1,0:T(8,128)S(1)} custom-call(s32[257]{0:T(512)S(1)} %pad_add_fusion.lists, f32[32,128]{1,0:T(8,128)S(1)} %multiply_add_fusion.1.joined, f32[16,128]{1,0:T(8,128)S(1)} %collective-permute-done.20.before, f32[16,128]{1,0:T(8,128)S(1)} %collective-permute-done.21.after, f32[32,128]{1,0:T(8,128)S(1)} %get-tuple-element.37.first_level, ...), custom_call_target="tpu_custom_call" | custom-call | tf_op jit(solution)/shard_map/pallas_call | solution.py:439
  94.7 1.7 %collective-permute-start.23 = (f32[16,128]{1,0:T(8,128)S(1)}, f32[16,128]{1,0:T(8,128)S(1)}, u32[]{:S(2)}, u32[]{:S(2)}) collective-permute-start(f32[16,128]{1,0:T(8,128)S(1)} %shard_map.79.r0), channel_id=1, source_target_pairs={{0,2},{1,3},{2,0},{3,1},{4,6},{5,7},{6,4},{7,5},{8,10},{9,11},{10,... | collective-permute-start | bytes 24584 | tf_op jit(solution)/shard_map/ppermute | solution.py:48
  98.9 4.7 %shard_map.80 = (f32[32,128]{1,0:T(8,128)S(1)}, f32[16,128]{1,0:T(8,128)S(1)}) custom-call(s32[257]{0:T(512)S(1)} %pad_add_fusion.lists, f32[16,128]{1,0:T(8,128)S(1)} %shard_map.79.r0, f32[16,128]{1,0:T(8,128)S(1)} %collective-permute-done.22.r1, f32[16,128]{1,0:T(8,128)S(1)} %collective-permute-done.23.r2, f32[16,128]{1,0:T(8,128)S(1)} %collective-permute-done.24.r3, ...), custom_call_target="tpu_custom_call" | custom-call | tf_op jit(solution)/shard_map/pallas_call | solution.py:439
  103.7 1.6 collective-permute-start.25
  105.3 1.8 %collective-permute-start.26 = (f32[32,128]{1,0:T(8,128)S(1)}, f32[32,128]{1,0:T(8,128)S(1)}, u32[]{:S(2)}, u32[]{:S(2)}) collective-permute-start(f32[32,128]{1,0:T(8,128)S(1)} %get-tuple-element.38), channel_id=1, source_target_pairs={{0,8},{1,9},{2,10},{3,11},{4,12},{5,13},{6,14},{7,15},{8,0},{9,1},... | collective-permute-start | bytes 49160 | tf_op jit(solution)/shard_map/ppermute | solution.py:48
  110.0 3.4 %collective-permute-start.28 = (f32[16,128]{1,0:T(8,128)S(1)}, f32[16,128]{1,0:T(8,128)S(1)}, u32[]{:S(2)}, u32[]{:S(2)}) collective-permute-start(f32[16,128]{1,0:T(8,128)S(1)} %get-tuple-element.52), channel_id=1, source_target_pairs={{0,16},{16,32},{32,48},{48,64},{64,80},{80,96},{96,112},{112,0},{1... | collective-permute-start | bytes 24584 | tf_op jit(solution)/shard_map/ppermute | solution.py:44
  114.1 2.3 %collective-permute-done.29.after = f32[16,128]{1,0:T(8,128)S(1)} collective-permute-done((f32[16,128]{1,0:T(8,128)S(1)}, f32[16,128]{1,0:T(8,128)S(1)}, u32[]{:S(2)}, u32[]{:S(2)}) %collective-permute-start.29) | collective-permute-done | bytes 8224 | tf_op jit(solution)/shard_map/ppermute | solution.py:44
  116.4 9.7 %shard_map.81 = (bf16[16,144,512]{2,1,0:T(8,128)(2,1)S(1)}, f32[4,128]{1,0:T(4,128)S(1)}) custom-call(s32[257]{0:T(512)S(1)} %pad_add_fusion.lists, s32[4]{0:T(128)S(1)} %and_select_fusion.4.t_order, f32[32,128]{1,0:T(8,128)S(1)} %multiply_add_fusion.joined, f32[16,128]{1,0:T(8,128)S(1)} %collective-permute-done.28.before, ...), custom_call_target="tpu_custom_call" | custom-call | tf_op jit(solution)/shard_map/pallas_call | solution.py:439
  127.5 3.9 %all-to-all-start = ((bf16[16,144,512]{2,1,0:T(8,128)(2,1)}), bf16[16,144,512]{2,1,0:T(8,128)(2,1)S(1)}, u32[]{:S(2)}, u32[]{:S(2)}) async-start(bf16[16,144,512]{2,1,0:T(8,128)(2,1)} %copy-done), calls=%async_computation | async-start | bytes 4718592 | tf_op jit(solution)/shard_map/all_to_all | solution.py:590
  132.8 33.4 %all-to-all-done.got = bf16[16,144,512]{2,1,0:T(8,128)(2,1)S(1)} async-done(((bf16[16,144,512]{2,1,0:T(8,128)(2,1)}), bf16[16,144,512]{2,1,0:T(8,128)(2,1)S(1)}, u32[]{:S(2)}, u32[]{:S(2)}) %all-to-all-start) | async-done | bytes 2359328 | tf_op jit(solution)/shard_map/all_to_all | solution.py:590
  166.2 1.9 %shard_map.82 = (f32[4,128]{1,0:T(4,128)}, f32[4,128]{1,0:T(4,128)}, f32[512,512]{1,0:T(8,128)}) custom-call(s32[1,2]{1,0:T(1,128)S(1)} %copy-done.7, bf16[16,144,512]{2,1,0:T(8,128)(2,1)S(1)} %all-to-all-done.got, f32[4,128]{1,0:T(4,128)S(1)} %get-tuple-element.41.own_level, f32[4,128]{1,0:T(4,128)S(1)} %multiply_bitcast_fusion.1.half_src, ...), custom_call_target="tpu_custom_call" | custom-call | tf_op jit(solution)/shard_map/pallas_call | solution.py:439
  (113 shorter events, 41.1 us)
Async XLA Ops:
  4.1 7.5 %collective-permute-start = (bf16[128,512]{1,0:T(8,128)(2,1)S(1)}, bf16[128,512]{1,0:T(8,128)(2,1)S(1)}, u32[]{:S(2)}, u32[]{:S(2)}) collective-permute-start(bf16[128,512]{1,0:T(8,128)(2,1)S(1)} %get-tuple-element.25), channel_id=1, source_target_pairs={{0,4},{1,5},{2,6},{3,7},{4,8},{5,9},{6,10},{7,11},{8,12},{9,13},{1... | collective-permute-start | bytes 393224 | tf_op jit(solution)/shard_map/ppermute | solution.py:48
  5.8 13.3 %collective-permute-start.5 = (bf16[512,512]{1,0:T(8,128)(2,1)S(1)}, bf16[512,512]{1,0:T(8,128)(2,1)S(1)}, u32[]{:S(2)}, u32[]{:S(2)}) collective-permute-start(bf16[512,512]{1,0:T(8,128)(2,1)S(1)} %get-tuple-element.27.refs_5_.refs_0_), channel_id=1, source_target_pairs={{0,112},{16,0},{32,16},{48,32},{64,48},{80,64},{96,80},{112,96},{1... | collective-permute-start | bytes 1572872 | tf_op jit(solution)/shard_map/ppermute | solution.py:44
  6.8 8.2 %collective-permute-start.8 = (bf16[128,512]{1,0:T(8,128)(2,1)S(1)}, bf16[128,512]{1,0:T(8,128)(2,1)S(1)}, u32[]{:S(2)}, u32[]{:S(2)}) collective-permute-start(bf16[128,512]{1,0:T(8,128)(2,1)S(1)} %get-tuple-element.31), channel_id=1, source_target_pairs={{0,8},{1,9},{2,10},{3,11},{4,12},{5,13},{6,14},{7,15},{8,0},{9,1},... | collective-permute-start | bytes 393224 | tf_op jit(solution)/shard_map/ppermute | solution.py:48
  10.1 5.6 %collective-permute-start.9 = (bf16[128,512]{1,0:T(8,128)(2,1)S(1)}, bf16[128,512]{1,0:T(8,128)(2,1)S(1)}, u32[]{:S(2)}, u32[]{:S(2)}) collective-permute-start(bf16[128,512]{1,0:T(8,128)(2,1)S(1)} %get-tuple-element.32), channel_id=1, source_target_pairs={{0,12},{1,13},{2,14},{3,15},{4,0},{5,1},{6,2},{7,3},{8,4},{9,5},{1... | collective-permute-start | bytes 393224 | tf_op jit(solution)/shard_map/ppermute | solution.py:48
  11.7 15.4 %collective-permute-start.1 = (bf16[512,512]{1,0:T(8,128)(2,1)S(1)}, bf16[512,512]{1,0:T(8,128)(2,1)S(1)}, u32[]{:S(2)}, u32[]{:S(2)}) collective-permute-start(bf16[512,512]{1,0:T(8,128)(2,1)S(1)} %get-tuple-element.27.refs_5_.refs_0_), channel_id=1, source_target_pairs={{0,4},{1,5},{2,6},{3,7},{4,8},{5,9},{6,10},{7,11},{8,12},{9,13},{1... | collective-permute-start | bytes 1572872 | tf_op jit(solution)/shard_map/ppermute | solution.py:48
  12.4 15.4 %collective-permute-start.2 = (bf16[512,512]{1,0:T(8,128)(2,1)S(1)}, bf16[512,512]{1,0:T(8,128)(2,1)S(1)}, u32[]{:S(2)}, u32[]{:S(2)}) collective-permute-start(bf16[512,512]{1,0:T(8,128)(2,1)S(1)} %get-tuple-element.27.refs_5_.refs_0_), channel_id=1, source_target_pairs={{0,12},{1,13},{2,14},{3,15},{4,0},{5,1},{6,2},{7,3},{8,4},{9,5},{1... | collective-permute-start | bytes 1572872 | tf_op jit(solution)/shard_map/ppermute | solution.py:48
  16.4 16.4 %collective-permute-start.10 = (bf16[512,512]{1,0:T(8,128)(2,1)}, bf16[512,512]{1,0:T(8,128)(2,1)}, u32[]{:S(2)}, u32[]{:S(2)}) collective-permute-start(bf16[512,512]{1,0:T(8,128)(2,1)} %constant_dynamic-update-slice_fusion.12.refs_0_), channel_id=1, source_target_pairs={{0,1},{1,2},{2,3},{3,0},{4,5},{5,6},{6,7},{7,4},{8,9},{9,10},{10,1... | collective-permute-start | bytes 1572872 | tf_op jit(solution)/shard_map/ppermute | solution.py:48
  17.6 18.4 %collective-permute-start.11 = (bf16[512,512]{1,0:T(8,128)(2,1)}, bf16[512,512]{1,0:T(8,128)(2,1)S(1)}, u32[]{:S(2)}, u32[]{:S(2)}) collective-permute-start(bf16[512,512]{1,0:T(8,128)(2,1)} %constant_dynamic-update-slice_fusion.12.refs_0_), channel_id=1, source_target_pairs={{0,3},{1,0},{2,1},{3,2},{4,7},{5,4},{6,5},{7,6},{8,11},{9,8},{10,9... | collective-permute-start | bytes 1572872 | tf_op jit(solution)/shard_map/ppermute | solution.py:48
  27.8 13.2 %collective-permute-start.3 = (bf16[256,512]{1,0:T(8,128)(2,1)}, bf16[256,512]{1,0:T(8,128)(2,1)}, u32[]{:S(2)}, u32[]{:S(2)}) collective-permute-start(bf16[256,512]{1,0:T(8,128)(2,1)} %slice.88), channel_id=1, source_target_pairs={{0,4},{1,5},{2,6},{3,7},{4,8},{5,9},{6,10},{7,11},{8,12},{9,13},{1... | collective-permute-start | bytes 786440 | tf_op jit(solution)/shard_map/ppermute | solution.py:48
  28.6 13.5 %collective-permute-start.4 = (bf16[256,512]{1,0:T(8,128)(2,1)}, bf16[256,512]{1,0:T(8,128)(2,1)}, u32[]{:S(2)}, u32[]{:S(2)}) collective-permute-start(bf16[256,512]{1,0:T(8,128)(2,1)} %slice.89), channel_id=1, source_target_pairs={{0,12},{1,13},{2,14},{3,15},{4,0},{5,1},{6,2},{7,3},{8,4},{9,5},{1... | collective-permute-start | bytes 786440 | tf_op jit(solution)/shard_map/ppermute | solution.py:48
  31.3 20.7 %collective-permute-start.6 = (bf16[1024,512]{1,0:T(8,128)(2,1)S(1)}, bf16[1024,512]{1,0:T(8,128)(2,1)S(1)}, u32[]{:S(2)}, u32[]{:S(2)}) collective-permute-start(bf16[1024,512]{1,0:T(8,128)(2,1)S(1)} %constant_dynamic-update-slice_fusion.refs_6_.refs_1_), channel_id=1, source_target_pairs={{0,112},{16,0},{32,16},{48,32},{64,48},{80,64},{96,80},{112,96},{1... | collective-permute-start | bytes 3145736 | tf_op jit(solution)/shard_map/ppermute | solution.py:44
  34.5 17.8 %collective-permute-start.12 = (bf16[256,512]{1,0:T(8,128)(2,1)}, bf16[256,512]{1,0:T(8,128)(2,1)S(1)}, u32[]{:S(2)}, u32[]{:S(2)}) collective-permute-start(bf16[256,512]{1,0:T(8,128)(2,1)} %slice.90), channel_id=1, source_target_pairs={{0,1},{1,2},{2,3},{3,0},{4,5},{5,6},{6,7},{7,4},{8,9},{9,10},{10,1... | collective-permute-start | bytes 786440 | tf_op jit(solution)/shard_map/ppermute | solution.py:48
  37.5 14.8 %collective-permute-start.13 = (bf16[256,512]{1,0:T(8,128)(2,1)}, bf16[256,512]{1,0:T(8,128)(2,1)}, u32[]{:S(2)}, u32[]{:S(2)}) collective-permute-start(bf16[256,512]{1,0:T(8,128)(2,1)} %slice.91), channel_id=1, source_target_pairs={{0,3},{1,0},{2,1},{3,2},{4,7},{5,4},{6,5},{7,6},{8,11},{9,8},{10,9... | collective-permute-start | bytes 786440 | tf_op jit(solution)/shard_map/ppermute | solution.py:48
  43.0 8.8 %collective-permute-start.7 = (bf16[512,512]{1,0:T(8,128)(2,1)S(1)}, bf16[512,512]{1,0:T(8,128)(2,1)S(1)}, u32[]{:S(2)}, u32[]{:S(2)}) collective-permute-start(bf16[512,512]{1,0:T(8,128)(2,1)S(1)} %constant_dynamic-update-slice_fusion.2.refs_7_.refs_2_), channel_id=1, source_target_pairs={{0,112},{16,0},{32,16},{48,32},{64,48},{80,64},{96,80},{112,96},{1... | collective-permute-start | bytes 1572872 | tf_op jit(solution)/shard_map/ppermute | solution.py:44
  66.8 3.8 %collective-permute-start.14 = (f32[16,128]{1,0:T(8,128)S(1)}, f32[16,128]{1,0:T(8,128)S(1)}, u32[]{:S(2)}, u32[]{:S(2)}) collective-permute-start(f32[16,128]{1,0:T(8,128)S(1)} %get-tuple-element.33.r0), channel_id=1, source_target_pairs={{0,1},{1,2},{2,3},{3,0},{4,5},{5,6},{6,7},{7,4},{8,9},{9,10},{10,1... | collective-permute-start | bytes 24584 | tf_op jit(solution)/shard_map/ppermute | solution.py:48
  67.0 4.0 %collective-permute-start.15 = (f32[16,128]{1,0:T(8,128)S(1)}, f32[16,128]{1,0:T(8,128)S(1)}, u32[]{:S(2)}, u32[]{:S(2)}) collective-permute-start(f32[16,128]{1,0:T(8,128)S(1)} %get-tuple-element.33.r0), channel_id=1, source_target_pairs={{0,2},{1,3},{2,0},{3,1},{4,6},{5,7},{6,4},{7,5},{8,10},{9,11},{10,... | collective-permute-start | bytes 24584 | tf_op jit(solution)/shard_map/ppermute | solution.py:48
  77.5 3.9 %collective-permute-start.17 = (f32[32,128]{1,0:T(8,128)S(1)}, f32[32,128]{1,0:T(8,128)S(1)}, u32[]{:S(2)}, u32[]{:S(2)}) collective-permute-start(f32[32,128]{1,0:T(8,128)S(1)} %get-tuple-element.36), channel_id=1, source_target_pairs={{0,4},{1,5},{2,6},{3,7},{4,8},{5,9},{6,10},{7,11},{8,12},{9,13},{1... | collective-permute-start | bytes 49160 | tf_op jit(solution)/shard_map/ppermute | solution.py:48
  77.6 4.2 %collective-permute-start.18 = (f32[32,128]{1,0:T(8,128)S(1)}, f32[32,128]{1,0:T(8,128)S(1)}, u32[]{:S(2)}, u32[]{:S(2)}) collective-permute-start(f32[32,128]{1,0:T(8,128)S(1)} %get-tuple-element.36), channel_id=1, source_target_pairs={{0,8},{1,9},{2,10},{3,11},{4,12},{5,13},{6,14},{7,15},{8,0},{9,1},... | collective-permute-start | bytes 49160 | tf_op jit(solution)/shard_map/ppermute | solution.py:48
  93.3 3.9 %collective-permute-start.22 = (f32[16,128]{1,0:T(8,128)S(1)}, f32[16,128]{1,0:T(8,128)S(1)}, u32[]{:S(2)}, u32[]{:S(2)}) collective-permute-start(f32[16,128]{1,0:T(8,128)S(1)} %shard_map.79.r0), channel_id=1, source_target_pairs={{0,1},{1,2},{2,3},{3,0},{4,5},{5,6},{6,7},{7,4},{8,9},{9,10},{10,1... | collective-permute-start | bytes 24584 | tf_op jit(solution)/shard_map/ppermute | solution.py:48
  94.7 4.1 %collective-permute-start.23 = (f32[16,128]{1,0:T(8,128)S(1)}, f32[16,128]{1,0:T(8,128)S(1)}, u32[]{:S(2)}, u32[]{:S(2)}) collective-permute-start(f32[16,128]{1,0:T(8,128)S(1)} %shard_map.79.r0), channel_id=1, source_target_pairs={{0,2},{1,3},{2,0},{3,1},{4,6},{5,7},{6,4},{7,5},{8,10},{9,11},{10,... | collective-permute-start | bytes 24584 | tf_op jit(solution)/shard_map/ppermute | solution.py:48
  103.7 4.1 %collective-permute-start.25 = (f32[32,128]{1,0:T(8,128)S(1)}, f32[32,128]{1,0:T(8,128)S(1)}, u32[]{:S(2)}, u32[]{:S(2)}) collective-permute-start(f32[32,128]{1,0:T(8,128)S(1)} %get-tuple-element.38), channel_id=1, source_target_pairs={{0,4},{1,5},{2,6},{3,7},{4,8},{5,9},{6,10},{7,11},{8,12},{9,13},{1... | collective-permute-start | bytes 49160 | tf_op jit(solution)/shard_map/ppermute | solution.py:48
  105.3 4.1 %collective-permute-start.26 = (f32[32,128]{1,0:T(8,128)S(1)}, f32[32,128]{1,0:T(8,128)S(1)}, u32[]{:S(2)}, u32[]{:S(2)}) collective-permute-start(f32[32,128]{1,0:T(8,128)S(1)} %get-tuple-element.38), channel_id=1, source_target_pairs={{0,8},{1,9},{2,10},{3,11},{4,12},{5,13},{6,14},{7,15},{8,0},{9,1},... | collective-permute-start | bytes 49160 | tf_op jit(solution)/shard_map/ppermute | solution.py:48
  110.0 4.2 %collective-permute-start.28 = (f32[16,128]{1,0:T(8,128)S(1)}, f32[16,128]{1,0:T(8,128)S(1)}, u32[]{:S(2)}, u32[]{:S(2)}) collective-permute-start(f32[16,128]{1,0:T(8,128)S(1)} %get-tuple-element.52), channel_id=1, source_target_pairs={{0,16},{16,32},{32,48},{48,64},{64,80},{80,96},{96,112},{112,0},{1... | collective-permute-start | bytes 24584 | tf_op jit(solution)/shard_map/ppermute | solution.py:44
  127.5 38.7 %all-to-all-start = ((bf16[16,144,512]{2,1,0:T(8,128)(2,1)}), bf16[16,144,512]{2,1,0:T(8,128)(2,1)S(1)}, u32[]{:S(2)}, u32[]{:S(2)}) async-start(bf16[16,144,512]{2,1,0:T(8,128)(2,1)} %copy-done), calls=%async_computation | async-start | bytes 4718592 | tf_op jit(solution)/shard_map/all_to_all | solution.py:590
  (17 other events, 99.9 us)

commit v6 on v5

--- a/solution.py
+++ b/solution.py
@@ -183,7 +183,7 @@
         sums_ref[pl.ds(s, 1), :] = to_lanes(top + jnp.log2(total))
         return carry
 
-    lax.fori_loop(0, SRC_CELLS, cell, 0, unroll=4)
+    lax.fori_loop(0, SRC_CELLS, cell, 0, unroll=8)
 
 
 def table_copy(kept, ring, sem, step, out=False):
@@ -239,7 +239,7 @@
         live_ref[pl.ds(s, 1), :] = jnp.sum(dead, axis=0, keepdims=True)
         return carry
 
-    lax.fori_loop(0, SRC_CELLS, source_cell, 0, unroll=4)
+    lax.fori_loop(0, SRC_CELLS, source_cell, 0, unroll=8)
 
     def step(i, carry):
         @pl.when(i >= RING)
@@ -278,7 +278,7 @@
         wide_ref[s] = to_rows(level_ref[pl.ds(s, 1), :])
         return carry
 
-    lax.fori_loop(0, SRC_CELLS, cell, 0, unroll=4)
+    lax.fori_loop(0, SRC_CELLS, cell, 0, unroll=8)
 
 
 def column_kernel(

time: 171 us -> 172 us (level); the launches traced: 168 us -> 171 us
  waiting for transfers between devices: 63.3 us -> 66.1 us
    all_to_all x1, waiting for transfers between devices: 33.4 us -> 36.5 us  [shards(): got = lax.all_to_all(blocks, 'help', 0, 0)]
  transfers between devices with their start and end apart: 31 -> 31, of which waited for: 17 -> 17; matrix products, arithmetic and copies ran while one was open for 8% -> 7% of each run, Pallas kernels for 0% -> 0%
where the time goes in v6:
time: 172 us; the launch traced here: 171 us
  waiting for transfers between devices  66.1 us (38%)
  starting transfers between devices  44.5 us (26%)
  Pallas kernels  41.2 us (24%)
  local copies, waits for them, and re-layouts  13.6 us (8%)
  other arithmetic  4.1 us (2%)
    pallas_call x7, Pallas kernels, call(): pl.pallas_call(kernel, out_shape=out_shape, in_specs=in_specs, out_specs=...  41.2 us
    all_to_all x1, waiting for transfers between devices, shards(): got = lax.all_to_all(blocks, 'help', 0, 0)  36.5 us
    ppermute x23, starting transfers between devices, to_help(): return lax.ppermute(array, 'help', perm)  31 us
    ppermute x23, waiting for transfers between devices, to_help(): return lax.ppermute(array, 'help', perm)  15.5 us
    ppermute x7, waiting for transfers between devices, to_group(): lax.ppermute(array, 'src', [(i, (i + by) % count) for i in range(count)])  14.1 us
    ppermute x7, starting transfers between devices, to_group(): lax.ppermute(array, 'src', [(i, (i + by) % count) for i in range(count)])  9.61 us
    unnamed x28, local copies, waits for them, and re-layouts  8.02 us
    all_to_all x1, starting transfers between devices, shards(): got = lax.all_to_all(blocks, 'help', 0, 0)  3.86 us
  transfers between devices with their start and end apart: 31, of which 17 were waited for; matrix products, arithmetic and copies ran while one was open for 7% of the time, Pallas kernels for 0%

profile of v6, /device:TPU:17, one launch (start us, length us, event | category | flops | bytes accessed | tf_op | source)
XLA Modules:
  0.0 171.2 jit_solution(12952840506888124618)
XLA Ops:
  4.1 1.7 collective-permute-start
  6.8 3.3 %collective-permute-start.8 = (bf16[128,512]{1,0:T(8,128)(2,1)S(1)}, bf16[128,512]{1,0:T(8,128)(2,1)S(1)}, u32[]{:S(2)}, u32[]{:S(2)}) collective-permute-start(bf16[128,512]{1,0:T(8,128)(2,1)S(1)} %get-tuple-element.31), channel_id=1, source_target_pairs={{0,8},{1,9},{2,10},{3,11},{4,12},{5,13},{6,14},{7,15},{8,0},{9,1},... | collective-permute-start | bytes 393224 | tf_op jit(solution)/shard_map/ppermute | solution.py:48
  12.4 1.9 %collective-permute-start.2 = (bf16[512,512]{1,0:T(8,128)(2,1)S(1)}, bf16[512,512]{1,0:T(8,128)(2,1)S(1)}, u32[]{:S(2)}, u32[]{:S(2)}) collective-permute-start(bf16[512,512]{1,0:T(8,128)(2,1)S(1)} %get-tuple-element.27.refs_5_.refs_0_), channel_id=1, source_target_pairs={{0,12},{1,13},{2,14},{3,15},{4,0},{5,1},{6,2},{7,3},{8,4},{9,5},{1... | collective-permute-start | bytes 1572872 | tf_op jit(solution)/shard_map/ppermute | solution.py:48
  19.3 7.8 %collective-permute-done.1 = bf16[512,512]{1,0:T(8,128)(2,1)S(1)} collective-permute-done((bf16[512,512]{1,0:T(8,128)(2,1)S(1)}, bf16[512,512]{1,0:T(8,128)(2,1)S(1)}, u32[]{:S(2)}, u32[]{:S(2)}) %collective-permute-start.1) | collective-permute-done | bytes 524320 | tf_op jit(solution)/shard_map/ppermute | solution.py:48
  28.6 2.7 %collective-permute-start.4 = (bf16[256,512]{1,0:T(8,128)(2,1)}, bf16[256,512]{1,0:T(8,128)(2,1)}, u32[]{:S(2)}, u32[]{:S(2)}) collective-permute-start(bf16[256,512]{1,0:T(8,128)(2,1)} %slice.89), channel_id=1, source_target_pairs={{0,12},{1,13},{2,14},{3,15},{4,0},{5,1},{6,2},{7,3},{8,4},{9,5},{1... | collective-permute-start | bytes 786440 | tf_op jit(solution)/shard_map/ppermute | solution.py:48
  32.8 1.7 slice.90
  43.8 8.0 %collective-permute-done.7.refs_10_.refs_5_ = bf16[512,512]{1,0:T(8,128)(2,1)S(1)} collective-permute-done((bf16[512,512]{1,0:T(8,128)(2,1)S(1)}, bf16[512,512]{1,0:T(8,128)(2,1)S(1)}, u32[]{:S(2)}, u32[]{:S(2)}) %collective-permute-start.7) | collective-permute-done | bytes 524320 | tf_op jit(solution)/shard_map/ppermute | solution.py:44
  52.3 14.0 %shard_map.77 = (f32[64,2,128,512]{3,2,1,0:T(8,128)}, f32[16,128]{1,0:T(8,128)S(1)}, f32[32,128]{1,0:T(8,128)S(1)}, f32[16,128]{1,0:T(8,128)S(1)}) custom-call(s32[257]{0:T(512)S(1)} %pad_add_fusion.lists, s32[16]{0:T(128)S(1)} %fusion.2.s_order, s32[4]{0:T(128)S(1)} %and_select_fusion.4.t_order, f32[32,128]{1,0:T(8,128)S(1)} %bitcast.33, ...), custom_call_target="tpu_custom_call" | custom-call | tf_op jit(solution)/shard_map/pallas_call | solution.py:439
  67.1 2.5 %collective-permute-start.15 = (f32[16,128]{1,0:T(8,128)S(1)}, f32[16,128]{1,0:T(8,128)S(1)}, u32[]{:S(2)}, u32[]{:S(2)}) collective-permute-start(f32[16,128]{1,0:T(8,128)S(1)} %get-tuple-element.33.r0), channel_id=1, source_target_pairs={{0,2},{1,3},{2,0},{3,1},{4,6},{5,7},{6,4},{7,5},{8,10},{9,11},{10,... | collective-permute-start | bytes 24584 | tf_op jit(solution)/shard_map/ppermute | solution.py:48
  72.0 5.1 %shard_map.78 = (f32[32,128]{1,0:T(8,128)S(1)}, f32[16,128]{1,0:T(8,128)}) custom-call(s32[257]{0:T(512)S(1)} %pad_add_fusion.lists, f32[16,128]{1,0:T(8,128)S(1)} %get-tuple-element.33.r0, f32[16,128]{1,0:T(8,128)S(1)} %collective-permute-done.14.r1, f32[16,128]{1,0:T(8,128)S(1)} %collective-permute-done.15.r2, f32[16,128]{1,0:T(8,128)S(1)} %collective-permute-done.16.r3, ...), custom_call_target="tpu_custom_call" | custom-call | tf_op jit(solution)/shard_map/pallas_call | solution.py:439
  81.8 3.4 %collective-permute-start.20 = (f32[16,128]{1,0:T(8,128)S(1)}, f32[16,128]{1,0:T(8,128)S(1)}, u32[]{:S(2)}, u32[]{:S(2)}) collective-permute-start(f32[16,128]{1,0:T(8,128)S(1)} %get-tuple-element.54), channel_id=1, source_target_pairs={{0,16},{16,32},{32,48},{48,64},{64,80},{80,96},{96,112},{112,0},{1... | collective-permute-start | bytes 24584 | tf_op jit(solution)/shard_map/ppermute | solution.py:44
  86.0 2.3 %collective-permute-done.21.after = f32[16,128]{1,0:T(8,128)S(1)} collective-permute-done((f32[16,128]{1,0:T(8,128)S(1)}, f32[16,128]{1,0:T(8,128)S(1)}, u32[]{:S(2)}, u32[]{:S(2)}) %collective-permute-start.21) | collective-permute-done | bytes 8224 | tf_op jit(solution)/shard_map/ppermute | solution.py:44
  88.3 5.6 %shard_map.79.r0 = f32[16,128]{1,0:T(8,128)S(1)} custom-call(s32[257]{0:T(512)S(1)} %pad_add_fusion.lists, f32[32,128]{1,0:T(8,128)S(1)} %multiply_add_fusion.1.joined, f32[16,128]{1,0:T(8,128)S(1)} %collective-permute-done.20.before, f32[16,128]{1,0:T(8,128)S(1)} %collective-permute-done.21.after, f32[32,128]{1,0:T(8,128)S(1)} %get-tuple-element.37.first_level, ...), custom_call_target="tpu_custom_call" | custom-call | tf_op jit(solution)/shard_map/pallas_call | solution.py:439
  94.1 2.9 %collective-permute-start.23 = (f32[16,128]{1,0:T(8,128)S(1)}, f32[16,128]{1,0:T(8,128)S(1)}, u32[]{:S(2)}, u32[]{:S(2)}) collective-permute-start(f32[16,128]{1,0:T(8,128)S(1)} %shard_map.79.r0), channel_id=1, source_target_pairs={{0,2},{1,3},{2,0},{3,1},{4,6},{5,7},{6,4},{7,5},{8,10},{9,11},{10,... | collective-permute-start | bytes 24584 | tf_op jit(solution)/shard_map/ppermute | solution.py:48
  99.5 4.6 %shard_map.80 = (f32[32,128]{1,0:T(8,128)S(1)}, f32[16,128]{1,0:T(8,128)S(1)}) custom-call(s32[257]{0:T(512)S(1)} %pad_add_fusion.lists, f32[16,128]{1,0:T(8,128)S(1)} %shard_map.79.r0, f32[16,128]{1,0:T(8,128)S(1)} %collective-permute-done.22.r1, f32[16,128]{1,0:T(8,128)S(1)} %collective-permute-done.23.r2, f32[16,128]{1,0:T(8,128)S(1)} %collective-permute-done.24.r3, ...), custom_call_target="tpu_custom_call" | custom-call | tf_op jit(solution)/shard_map/pallas_call | solution.py:439
  104.1 1.7 collective-permute-start.25
  105.8 1.8 %collective-permute-start.26 = (f32[32,128]{1,0:T(8,128)S(1)}, f32[32,128]{1,0:T(8,128)S(1)}, u32[]{:S(2)}, u32[]{:S(2)}) collective-permute-start(f32[32,128]{1,0:T(8,128)S(1)} %get-tuple-element.38), channel_id=1, source_target_pairs={{0,8},{1,9},{2,10},{3,11},{4,12},{5,13},{6,14},{7,15},{8,0},{9,1},... | collective-permute-start | bytes 49160 | tf_op jit(solution)/shard_map/ppermute | solution.py:48
  108.3 1.6 collective-permute-done.26
  110.5 3.2 %collective-permute-start.28 = (f32[16,128]{1,0:T(8,128)S(1)}, f32[16,128]{1,0:T(8,128)S(1)}, u32[]{:S(2)}, u32[]{:S(2)}) collective-permute-start(f32[16,128]{1,0:T(8,128)S(1)} %get-tuple-element.52), channel_id=1, source_target_pairs={{0,16},{16,32},{32,48},{48,64},{64,80},{80,96},{96,112},{112,0},{1... | collective-permute-start | bytes 24584 | tf_op jit(solution)/shard_map/ppermute | solution.py:44
  114.5 2.3 %collective-permute-done.29.after = f32[16,128]{1,0:T(8,128)S(1)} collective-permute-done((f32[16,128]{1,0:T(8,128)S(1)}, f32[16,128]{1,0:T(8,128)S(1)}, u32[]{:S(2)}, u32[]{:S(2)}) %collective-permute-start.29) | collective-permute-done | bytes 8224 | tf_op jit(solution)/shard_map/ppermute | solution.py:44
  116.8 9.3 %shard_map.81 = (bf16[16,144,512]{2,1,0:T(8,128)(2,1)S(1)}, f32[4,128]{1,0:T(4,128)S(1)}) custom-call(s32[257]{0:T(512)S(1)} %pad_add_fusion.lists, s32[4]{0:T(128)S(1)} %and_select_fusion.4.t_order, f32[32,128]{1,0:T(8,128)S(1)} %multiply_add_fusion.joined, f32[16,128]{1,0:T(8,128)S(1)} %collective-permute-done.28.before, ...), custom_call_target="tpu_custom_call" | custom-call | tf_op jit(solution)/shard_map/pallas_call | solution.py:439
  127.5 3.9 %all-to-all-start = ((bf16[16,144,512]{2,1,0:T(8,128)(2,1)}), bf16[16,144,512]{2,1,0:T(8,128)(2,1)S(1)}, u32[]{:S(2)}, u32[]{:S(2)}) async-start(bf16[16,144,512]{2,1,0:T(8,128)(2,1)} %copy-done), calls=%async_computation | async-start | bytes 4718592 | tf_op jit(solution)/shard_map/all_to_all | solution.py:590
  132.8 36.5 %all-to-all-done.got = bf16[16,144,512]{2,1,0:T(8,128)(2,1)S(1)} async-done(((bf16[16,144,512]{2,1,0:T(8,128)(2,1)}), bf16[16,144,512]{2,1,0:T(8,128)(2,1)S(1)}, u32[]{:S(2)}, u32[]{:S(2)}) %all-to-all-start) | async-done | bytes 2359328 | tf_op jit(solution)/shard_map/all_to_all | solution.py:590
  169.3 1.9 %shard_map.82 = (f32[4,128]{1,0:T(4,128)}, f32[4,128]{1,0:T(4,128)}, f32[512,512]{1,0:T(8,128)}) custom-call(s32[1,2]{1,0:T(1,128)S(1)} %copy-done.7, bf16[16,144,512]{2,1,0:T(8,128)(2,1)S(1)} %all-to-all-done.got, f32[4,128]{1,0:T(4,128)S(1)} %get-tuple-element.41.own_level, f32[4,128]{1,0:T(4,128)S(1)} %multiply_bitcast_fusion.1.half_src, ...), custom_call_target="tpu_custom_call" | custom-call | tf_op jit(solution)/shard_map/pallas_call | solution.py:439
  (113 shorter events, 40.1 us)
Async XLA Ops:
  4.1 7.5 %collective-permute-start = (bf16[128,512]{1,0:T(8,128)(2,1)S(1)}, bf16[128,512]{1,0:T(8,128)(2,1)S(1)}, u32[]{:S(2)}, u32[]{:S(2)}) collective-permute-start(bf16[128,512]{1,0:T(8,128)(2,1)S(1)} %get-tuple-element.25), channel_id=1, source_target_pairs={{0,4},{1,5},{2,6},{3,7},{4,8},{5,9},{6,10},{7,11},{8,12},{9,13},{1... | collective-permute-start | bytes 393224 | tf_op jit(solution)/shard_map/ppermute | solution.py:48
  5.8 13.3 %collective-permute-start.5 = (bf16[512,512]{1,0:T(8,128)(2,1)S(1)}, bf16[512,512]{1,0:T(8,128)(2,1)S(1)}, u32[]{:S(2)}, u32[]{:S(2)}) collective-permute-start(bf16[512,512]{1,0:T(8,128)(2,1)S(1)} %get-tuple-element.27.refs_5_.refs_0_), channel_id=1, source_target_pairs={{0,112},{16,0},{32,16},{48,32},{64,48},{80,64},{96,80},{112,96},{1... | collective-permute-start | bytes 1572872 | tf_op jit(solution)/shard_map/ppermute | solution.py:44
  6.8 8.2 %collective-permute-start.8 = (bf16[128,512]{1,0:T(8,128)(2,1)S(1)}, bf16[128,512]{1,0:T(8,128)(2,1)S(1)}, u32[]{:S(2)}, u32[]{:S(2)}) collective-permute-start(bf16[128,512]{1,0:T(8,128)(2,1)S(1)} %get-tuple-element.31), channel_id=1, source_target_pairs={{0,8},{1,9},{2,10},{3,11},{4,12},{5,13},{6,14},{7,15},{8,0},{9,1},... | collective-permute-start | bytes 393224 | tf_op jit(solution)/shard_map/ppermute | solution.py:48
  10.1 5.6 %collective-permute-start.9 = (bf16[128,512]{1,0:T(8,128)(2,1)S(1)}, bf16[128,512]{1,0:T(8,128)(2,1)S(1)}, u32[]{:S(2)}, u32[]{:S(2)}) collective-permute-start(bf16[128,512]{1,0:T(8,128)(2,1)S(1)} %get-tuple-element.32), channel_id=1, source_target_pairs={{0,12},{1,13},{2,14},{3,15},{4,0},{5,1},{6,2},{7,3},{8,4},{9,5},{1... | collective-permute-start | bytes 393224 | tf_op jit(solution)/shard_map/ppermute | solution.py:48
  11.7 15.4 %collective-permute-start.1 = (bf16[512,512]{1,0:T(8,128)(2,1)S(1)}, bf16[512,512]{1,0:T(8,128)(2,1)S(1)}, u32[]{:S(2)}, u32[]{:S(2)}) collective-permute-start(bf16[512,512]{1,0:T(8,128)(2,1)S(1)} %get-tuple-element.27.refs_5_.refs_0_), channel_id=1, source_target_pairs={{0,4},{1,5},{2,6},{3,7},{4,8},{5,9},{6,10},{7,11},{8,12},{9,13},{1... | collective-permute-start | bytes 1572872 | tf_op jit(solution)/shard_map/ppermute | solution.py:48
  12.4 15.4 %collective-permute-start.2 = (bf16[512,512]{1,0:T(8,128)(2,1)S(1)}, bf16[512,512]{1,0:T(8,128)(2,1)S(1)}, u32[]{:S(2)}, u32[]{:S(2)}) collective-permute-start(bf16[512,512]{1,0:T(8,128)(2,1)S(1)} %get-tuple-element.27.refs_5_.refs_0_), channel_id=1, source_target_pairs={{0,12},{1,13},{2,14},{3,15},{4,0},{5,1},{6,2},{7,3},{8,4},{9,5},{1... | collective-permute-start | bytes 1572872 | tf_op jit(solution)/shard_map/ppermute | solution.py:48
  16.4 16.4 %collective-permute-start.10 = (bf16[512,512]{1,0:T(8,128)(2,1)}, bf16[512,512]{1,0:T(8,128)(2,1)}, u32[]{:S(2)}, u32[]{:S(2)}) collective-permute-start(bf16[512,512]{1,0:T(8,128)(2,1)} %constant_dynamic-update-slice_fusion.12.refs_0_), channel_id=1, source_target_pairs={{0,1},{1,2},{2,3},{3,0},{4,5},{5,6},{6,7},{7,4},{8,9},{9,10},{10,1... | collective-permute-start | bytes 1572872 | tf_op jit(solution)/shard_map/ppermute | solution.py:48
  17.6 18.4 %collective-permute-start.11 = (bf16[512,512]{1,0:T(8,128)(2,1)}, bf16[512,512]{1,0:T(8,128)(2,1)S(1)}, u32[]{:S(2)}, u32[]{:S(2)}) collective-permute-start(bf16[512,512]{1,0:T(8,128)(2,1)} %constant_dynamic-update-slice_fusion.12.refs_0_), channel_id=1, source_target_pairs={{0,3},{1,0},{2,1},{3,2},{4,7},{5,4},{6,5},{7,6},{8,11},{9,8},{10,9... | collective-permute-start | bytes 1572872 | tf_op jit(solution)/shard_map/ppermute | solution.py:48
  27.8 13.2 %collective-permute-start.3 = (bf16[256,512]{1,0:T(8,128)(2,1)}, bf16[256,512]{1,0:T(8,128)(2,1)}, u32[]{:S(2)}, u32[]{:S(2)}) collective-permute-start(bf16[256,512]{1,0:T(8,128)(2,1)} %slice.88), channel_id=1, source_target_pairs={{0,4},{1,5},{2,6},{3,7},{4,8},{5,9},{6,10},{7,11},{8,12},{9,13},{1... | collective-permute-start | bytes 786440 | tf_op jit(solution)/shard_map/ppermute | solution.py:48
  28.6 13.5 %collective-permute-start.4 = (bf16[256,512]{1,0:T(8,128)(2,1)}, bf16[256,512]{1,0:T(8,128)(2,1)}, u32[]{:S(2)}, u32[]{:S(2)}) collective-permute-start(bf16[256,512]{1,0:T(8,128)(2,1)} %slice.89), channel_id=1, source_target_pairs={{0,12},{1,13},{2,14},{3,15},{4,0},{5,1},{6,2},{7,3},{8,4},{9,5},{1... | collective-permute-start | bytes 786440 | tf_op jit(solution)/shard_map/ppermute | solution.py:48
  31.3 20.7 %collective-permute-start.6 = (bf16[1024,512]{1,0:T(8,128)(2,1)S(1)}, bf16[1024,512]{1,0:T(8,128)(2,1)S(1)}, u32[]{:S(2)}, u32[]{:S(2)}) collective-permute-start(bf16[1024,512]{1,0:T(8,128)(2,1)S(1)} %constant_dynamic-update-slice_fusion.refs_6_.refs_1_), channel_id=1, source_target_pairs={{0,112},{16,0},{32,16},{48,32},{64,48},{80,64},{96,80},{112,96},{1... | collective-permute-start | bytes 3145736 | tf_op jit(solution)/shard_map/ppermute | solution.py:44
  34.5 17.8 %collective-permute-start.12 = (bf16[256,512]{1,0:T(8,128)(2,1)}, bf16[256,512]{1,0:T(8,128)(2,1)S(1)}, u32[]{:S(2)}, u32[]{:S(2)}) collective-permute-start(bf16[256,512]{1,0:T(8,128)(2,1)} %slice.90), channel_id=1, source_target_pairs={{0,1},{1,2},{2,3},{3,0},{4,5},{5,6},{6,7},{7,4},{8,9},{9,10},{10,1... | collective-permute-start | bytes 786440 | tf_op jit(solution)/shard_map/ppermute | solution.py:48
  37.5 14.8 %collective-permute-start.13 = (bf16[256,512]{1,0:T(8,128)(2,1)}, bf16[256,512]{1,0:T(8,128)(2,1)}, u32[]{:S(2)}, u32[]{:S(2)}) collective-permute-start(bf16[256,512]{1,0:T(8,128)(2,1)} %slice.91), channel_id=1, source_target_pairs={{0,3},{1,0},{2,1},{3,2},{4,7},{5,4},{6,5},{7,6},{8,11},{9,8},{10,9... | collective-permute-start | bytes 786440 | tf_op jit(solution)/shard_map/ppermute | solution.py:48
  43.0 8.8 %collective-permute-start.7 = (bf16[512,512]{1,0:T(8,128)(2,1)S(1)}, bf16[512,512]{1,0:T(8,128)(2,1)S(1)}, u32[]{:S(2)}, u32[]{:S(2)}) collective-permute-start(bf16[512,512]{1,0:T(8,128)(2,1)S(1)} %constant_dynamic-update-slice_fusion.2.refs_7_.refs_2_), channel_id=1, source_target_pairs={{0,112},{16,0},{32,16},{48,32},{64,48},{80,64},{96,80},{112,96},{1... | collective-permute-start | bytes 1572872 | tf_op jit(solution)/shard_map/ppermute | solution.py:44
  66.3 4.4 %collective-permute-start.14 = (f32[16,128]{1,0:T(8,128)S(1)}, f32[16,128]{1,0:T(8,128)S(1)}, u32[]{:S(2)}, u32[]{:S(2)}) collective-permute-start(f32[16,128]{1,0:T(8,128)S(1)} %get-tuple-element.33.r0), channel_id=1, source_target_pairs={{0,1},{1,2},{2,3},{3,0},{4,5},{5,6},{6,7},{7,4},{8,9},{9,10},{10,1... | collective-permute-start | bytes 24584 | tf_op jit(solution)/shard_map/ppermute | solution.py:48
  67.1 4.0 %collective-permute-start.15 = (f32[16,128]{1,0:T(8,128)S(1)}, f32[16,128]{1,0:T(8,128)S(1)}, u32[]{:S(2)}, u32[]{:S(2)}) collective-permute-start(f32[16,128]{1,0:T(8,128)S(1)} %get-tuple-element.33.r0), channel_id=1, source_target_pairs={{0,2},{1,3},{2,0},{3,1},{4,6},{5,7},{6,4},{7,5},{8,10},{9,11},{10,... | collective-permute-start | bytes 24584 | tf_op jit(solution)/shard_map/ppermute | solution.py:48
  77.2 4.3 %collective-permute-start.18 = (f32[32,128]{1,0:T(8,128)S(1)}, f32[32,128]{1,0:T(8,128)S(1)}, u32[]{:S(2)}, u32[]{:S(2)}) collective-permute-start(f32[32,128]{1,0:T(8,128)S(1)} %get-tuple-element.36), channel_id=1, source_target_pairs={{0,8},{1,9},{2,10},{3,11},{4,12},{5,13},{6,14},{7,15},{8,0},{9,1},... | collective-permute-start | bytes 49160 | tf_op jit(solution)/shard_map/ppermute | solution.py:48
  81.8 4.2 %collective-permute-start.20 = (f32[16,128]{1,0:T(8,128)S(1)}, f32[16,128]{1,0:T(8,128)S(1)}, u32[]{:S(2)}, u32[]{:S(2)}) collective-permute-start(f32[16,128]{1,0:T(8,128)S(1)} %get-tuple-element.54), channel_id=1, source_target_pairs={{0,16},{16,32},{32,48},{48,64},{64,80},{80,96},{96,112},{112,0},{1... | collective-permute-start | bytes 24584 | tf_op jit(solution)/shard_map/ppermute | solution.py:44
  93.9 4.1 %collective-permute-start.22 = (f32[16,128]{1,0:T(8,128)S(1)}, f32[16,128]{1,0:T(8,128)S(1)}, u32[]{:S(2)}, u32[]{:S(2)}) collective-permute-start(f32[16,128]{1,0:T(8,128)S(1)} %shard_map.79.r0), channel_id=1, source_target_pairs={{0,1},{1,2},{2,3},{3,0},{4,5},{5,6},{6,7},{7,4},{8,9},{9,10},{10,1... | collective-permute-start | bytes 24584 | tf_op jit(solution)/shard_map/ppermute | solution.py:48
  94.1 4.2 %collective-permute-start.23 = (f32[16,128]{1,0:T(8,128)S(1)}, f32[16,128]{1,0:T(8,128)S(1)}, u32[]{:S(2)}, u32[]{:S(2)}) collective-permute-start(f32[16,128]{1,0:T(8,128)S(1)} %shard_map.79.r0), channel_id=1, source_target_pairs={{0,2},{1,3},{2,0},{3,1},{4,6},{5,7},{6,4},{7,5},{8,10},{9,11},{10,... | collective-permute-start | bytes 24584 | tf_op jit(solution)/shard_map/ppermute | solution.py:48
  104.1 4.2 %collective-permute-start.25 = (f32[32,128]{1,0:T(8,128)S(1)}, f32[32,128]{1,0:T(8,128)S(1)}, u32[]{:S(2)}, u32[]{:S(2)}) collective-permute-start(f32[32,128]{1,0:T(8,128)S(1)} %get-tuple-element.38), channel_id=1, source_target_pairs={{0,4},{1,5},{2,6},{3,7},{4,8},{5,9},{6,10},{7,11},{8,12},{9,13},{1... | collective-permute-start | bytes 49160 | tf_op jit(solution)/shard_map/ppermute | solution.py:48
  105.8 4.1 %collective-permute-start.26 = (f32[32,128]{1,0:T(8,128)S(1)}, f32[32,128]{1,0:T(8,128)S(1)}, u32[]{:S(2)}, u32[]{:S(2)}) collective-permute-start(f32[32,128]{1,0:T(8,128)S(1)} %get-tuple-element.38), channel_id=1, source_target_pairs={{0,8},{1,9},{2,10},{3,11},{4,12},{5,13},{6,14},{7,15},{8,0},{9,1},... | collective-permute-start | bytes 49160 | tf_op jit(solution)/shard_map/ppermute | solution.py:48
  110.5 4.0 %collective-permute-start.28 = (f32[16,128]{1,0:T(8,128)S(1)}, f32[16,128]{1,0:T(8,128)S(1)}, u32[]{:S(2)}, u32[]{:S(2)}) collective-permute-start(f32[16,128]{1,0:T(8,128)S(1)} %get-tuple-element.52), channel_id=1, source_target_pairs={{0,16},{16,32},{32,48},{48,64},{64,80},{80,96},{96,112},{112,0},{1... | collective-permute-start | bytes 24584 | tf_op jit(solution)/shard_map/ppermute | solution.py:44
  127.5 41.8 %all-to-all-start = ((bf16[16,144,512]{2,1,0:T(8,128)(2,1)}), bf16[16,144,512]{2,1,0:T(8,128)(2,1)S(1)}, u32[]{:S(2)}, u32[]{:S(2)}) async-start(bf16[16,144,512]{2,1,0:T(8,128)(2,1)} %copy-done), calls=%async_computation | async-start | bytes 4718592 | tf_op jit(solution)/shard_map/all_to_all | solution.py:590
  (17 other events, 103.7 us)
